TPU v7x, 32 devices: a whole 2x2x4 slice. The times are simulated.
32 devices in a mesh: groups: 2 (over x), src: 16 (over z, y, core).
Axes of the slice: x: 2, y: 2, z: 4, core: 2. Of those that a mesh axis runs over, the one named last changes fastest.
Arguments:
- source_field: float32 [32, 131072], P('groups', 'src'), parts along dimension 0, may hold values from -6 to 6
- neighbours: int32 [6, 131072], P(None, 'src'), may hold values from 0 to 8447, as said below
- slope_weights: float32 [2, 6, 131072], P(None, None, 'src'), may hold values from -2 to 2
- pair_block: int32 [16, 256], replicated, may hold values from 0 to 1023, as said below
- pair_dest: int32 [16, 256], P('src'), may hold values from 0 to 63
- remap_weights: bfloat16 [4096, 384, 128], P('src'), may hold values from -0.15625 to 0.15625
Outputs:
- remapped: float32 [32, 128, 1024], P('groups', 'src'), parts along dimension 0
- meridional: float32 [32, 128, 1024], P('groups', 'src'), parts along dimension 0
There are 2 independent parts, one for each index of `groups`. A program takes and returns all parts, laid end to end along the dimension named above; an argument that names none is the same for every part. Nothing has to cross between parts.
Inputs may be any that keep to these rules, and one draw needn't show every extreme that they name: `neighbours`: entry (k, c) is a position in cell c's partition of 8192 cells extended by the last 128 cells of the previous partition before and the first 128 of the next after, the partitions closing into a loop; it lies within 128 of cell c's own position. `pair_block`: an entry names source block (partition * 64 + block of that partition). In every row at most 16 entries name blocks of one partition, and they name at most 8 distinct blocks.
All inputs are finite; a program needn't handle non-finite values.
Results may differ from a plain program's by a relative error of at most 0.0029.
Values may be sent and summed in bfloat16 or wider, within the bound.
No kernel may reach another device: no remote copies, remote signals or barrier semaphores. Data moves between devices by JAX's collectives and lax.ppermute only.
A program may use at most 128 MiB of HBM per device.

v0:
```python
import jax
import jax.numpy as jnp
from jax import lax
from jax.sharding import PartitionSpec as P

K = 6
BLK = 128
HALO = 128
NB = 64
LAT_DEV = 8
LONB = 8
DB = 64


def extended_2(block, sides, width, periodic):
    for axis, dim in sides:
        count = lax.axis_size(axis)
        forward = [(i, i + 1) for i in range(count - 1)]
        if periodic:
            forward.append((count - 1, 0))
        backward = [(target, source) for source, target in forward]
        low = lax.ppermute(
            lax.slice_in_dim(block, block.shape[dim] - width, None, axis=dim), axis, forward
        )
        high = lax.ppermute(lax.slice_in_dim(block, 0, width, axis=dim), axis, backward)
        block = jnp.concatenate([low, block, high], axis=dim)
    return block


def pair_slots(sources):
    count = sources.shape[1]
    order_ids = jnp.arange(count, dtype=jnp.int32)
    same_source = sources[:, :, None] == sources[:, None, :]
    earlier = (order_ids[:, None] < order_ids[None, :])[None]
    return jnp.sum((same_source & earlier).astype(jnp.int32), axis=1)


def outgoing(moments, sources, blocks, slot_of, own_index, capacity):
    own_pairs = sources == own_index
    slot_ids = jnp.arange(capacity, dtype=jnp.int32)
    matched = own_pairs[:, :, None] & (slot_of[:, :, None] == slot_ids[None, None, :])
    block_index = jnp.max(jnp.where(matched, blocks[:, :, None], 0), axis=1)
    chosen = jnp.take(moments, block_index.reshape(-1), axis=0)
    return chosen.reshape(sources.shape[0], capacity, moments.shape[1], moments.shape[2])


def local(source_field, neighbours, slope_weights, pair_block, pair_dest, remap_weights):
    levels, cell_count = source_field.shape
    own_index = lax.axis_index("src")
    partitions = lax.axis_size("src")
    pair_total = pair_block.shape[1]
    pair_bound = max(2, (pair_total + partitions - 1) // partitions)
    extended = extended_2(source_field, (("src", 1),), HALO, True)
    slope_east = jnp.zeros(source_field.shape, jnp.float32)
    slope_north = jnp.zeros(source_field.shape, jnp.float32)
    for offset in range(K):
        difference = jnp.take(extended, neighbours[offset], axis=1) - source_field
        slope_east = slope_east + slope_weights[0, offset][None, :] * difference
        slope_north = slope_north + slope_weights[1, offset][None, :] * difference
    stacked = jnp.stack([source_field, slope_east, slope_north])
    stacked = stacked.reshape(3, levels, NB, BLK).transpose(2, 1, 0, 3)
    moments = stacked.reshape(NB, levels, 3 * BLK).astype(jnp.bfloat16)
    sources = pair_block // NB
    blocks = pair_block % NB
    slot_of = pair_slots(sources)
    sending = outgoing(moments, sources, blocks, slot_of, own_index, pair_bound)
    received = lax.all_to_all(sending, "src", split_axis=0, concat_axis=0, tiled=True)
    own_sources = lax.dynamic_index_in_dim(sources, own_index, 0, keepdims=False)
    own_slots = lax.dynamic_index_in_dim(slot_of, own_index, 0, keepdims=False)
    position = own_sources * pair_bound + own_slots
    flat_received = received.reshape(-1, levels, 3 * BLK)
    gathered = jnp.take(flat_received, position, axis=0)
    contrib = jnp.einsum(
        "pli,pio->plo", gathered, remap_weights, preferred_element_type=jnp.float32
    )
    dest_row = pair_dest[0]
    pair_count = dest_row.shape[0]
    one_hot = (dest_row[None, :] == jnp.arange(DB, dtype=jnp.int32)[:, None]).astype(jnp.float32)
    tile_sum = jnp.dot(
        one_hot, contrib.reshape(pair_count, levels * BLK), precision=lax.Precision.HIGHEST
    )
    remapped = (
        tile_sum.reshape(LAT_DEV, LONB, levels, BLK)
        .transpose(2, 0, 1, 3)
        .reshape(levels, LAT_DEV, LONB * BLK)
    )
    padded = extended_2(remapped, (("src", 1),), 1, False)
    meridional = 0.5 * (padded[:, 2:] - padded[:, :-2])
    return (remapped, meridional)


def solution(mesh):
    return jax.shard_map(
        local,
        mesh=mesh,
        in_specs=(
            P("groups", "src"),
            P(None, "src"),
            P(None, None, "src"),
            P(),
            P("src", None),
            P("src", None, None),
        ),
        out_specs=(P("groups", "src", None), P("groups", "src", None)),
        check_vma=False,
    )
```

profile of v0, /device:TPU:18, one launch (start us, length us, event | category | flops | bytes accessed | tf_op | source)
XLA Modules:
  0.0 336.6 jit_solution(15595268057688654377)
XLA Ops:
  1.4 2.6 collective-permute-start.1
  4.0 2.2 fusion.25
  15.5 2.7 copy.84
  18.2 30.2 %gather_fusion.2 = f32[8192,16]{1,0:T(8,128)} fusion(f32[16,8448]{0,1:T(8,128)} %copy.84, s32[8192]{0:T(1024)S(1)} %fusion.13), kind=kCustom, calls=%fused_computation.clone | custom fusion | bytes 1081344 | tf_op jit(solution)/shard_map/jit(_take)/gather | solution.py:57
  48.4 2.8 copy.85
  51.2 30.2 %gather_fusion.3 = f32[8192,16]{1,0:T(8,128)} fusion(f32[16,8448]{0,1:T(8,128)} %copy.84, s32[8192]{0:T(1024)S(1)} %fusion.14), kind=kCustom, calls=%fused_computation.1.clone | custom fusion | bytes 1081344 | tf_op jit(solution)/shard_map/jit(_take)/gather | solution.py:57
  81.4 2.8 copy.87
  84.2 30.2 %gather_fusion.4 = f32[8192,16]{1,0:T(8,128)} fusion(f32[16,8448]{0,1:T(8,128)} %copy.84, s32[8192]{0:T(1024)S(1)} %fusion.15), kind=kCustom, calls=%fused_computation.2.clone | custom fusion | bytes 1081344 | tf_op jit(solution)/shard_map/jit(_take)/gather | solution.py:57
  114.3 2.8 copy.89
  117.1 30.2 %gather_fusion.5 = f32[8192,16]{1,0:T(8,128)} fusion(f32[16,8448]{0,1:T(8,128)} %copy.84, s32[8192]{0:T(1024)S(1)} %fusion.16), kind=kCustom, calls=%fused_computation.3.clone | custom fusion | bytes 1081344 | tf_op jit(solution)/shard_map/jit(_take)/gather | solution.py:57
  147.3 2.8 copy.91
  150.1 30.2 %gather_fusion.6 = f32[8192,16]{1,0:T(8,128)} fusion(f32[16,8448]{0,1:T(8,128)} %copy.84, s32[8192]{0:T(1024)S(1)} %fusion.17), kind=kCustom, calls=%fused_computation.4.clone | custom fusion | bytes 1081344 | tf_op jit(solution)/shard_map/jit(_take)/gather | solution.py:57
  180.3 2.8 copy.93
  183.1 30.2 %gather_fusion.7 = f32[8192,16]{1,0:T(8,128)} fusion(f32[16,8448]{0,1:T(8,128)} %copy.84, s32[8192]{0:T(1024)S(1)} %copy-done.4), kind=kCustom, calls=%fused_computation.5.clone | custom fusion | bytes 1081344 | tf_op jit(solution)/shard_map/jit(_take)/gather | solution.py:57
  213.3 3.6 %copy.95 = f32[8192,16]{0,1:T(8,128)} copy(f32[8192,16]{1,0:T(8,128)} %gather_fusion.7) | data formatting | bytes 1048576 | tf_op jit(solution)/shard_map/jit(_take)/gather | solution.py:57
  223.2 2.8 gather_fusion
  226.0 3.4 broadcast_select_fusion
  229.4 5.7 %all-to-all-start = ((bf16[16,16,16,384]{3,2,1,0:T(8,128)(2,1)}), bf16[16,16,16,384]{3,2,1,0:T(8,128)(2,1)S(1)}, u32[]{:S(2)}, u32[]{:S(2)}) async-start(bf16[16,16,16,384]{3,2,1,0:T(8,128)(2,1)} %broadcast_select_fusion), calls=%async_computation | async-start | bytes 6291456 | tf_op jit(solution)/shard_map/all_to_all | solution.py:67
  235.8 69.4 %all-to-all-done = bf16[16,16,16,384]{3,2,1,0:T(8,128)(2,1)S(1)} async-done(((bf16[16,16,16,384]{3,2,1,0:T(8,128)(2,1)}), bf16[16,16,16,384]{3,2,1,0:T(8,128)(2,1)S(1)}, u32[]{:S(2)}, u32[]{:S(2)}) %all-to-all-start) | async-done | bytes 3145760 | tf_op jit(solution)/shard_map/all_to_all | solution.py:67
  306.8 3.2 gather_fusion.1
  310.0 10.3 %fusion = f32[256,16,128]{2,1,0:T(8,128)S(1)} fusion(bf16[256,384,128]{2,1,0:T(8,128)(2,1)} %param.13, bf16[256,16,384]{2,1,0:T(8,128)(2,1)S(1)} %gather_fusion.1, pred[256]{0:T(512)(128)(4,1)S(1)} %compare_and_fusion.7), kind=kOutput, calls=%fused_computation.9 | convolution fusion | flops 404226048 | bytes 30408960 | tf_op jit(solution)/shard_map/pli,pio->plo/dot_general | solution.py:73
  320.3 2.2 copy.111
  326.2 2.9 collective-permute-start.2
  331.1 4.5 %collective-permute-done.3 = f32[16,1,1024]{2,1,0:T(1,128)S(1)} collective-permute-done((f32[16,1,1024]{2,1,0:T(1,128)S(1)}, f32[16,1,1024]{2,1,0:T(1,128)S(1)}, u32[]{:S(2)}, u32[]{:S(2)}) %collective-permute-start.3) | collective-permute-done | bytes 65568 | tf_op jit(solution)/shard_map/ppermute | solution.py:22
  (74 shorter events, 25.0 us)
Async XLA Ops:
  1.3 13.1 %collective-permute-start = (f32[16,128]{1,0:T(8,128)S(1)}, f32[16,128]{1,0:T(8,128)S(1)}, u32[]{:S(2)}, u32[]{:S(2)}) collective-permute-start(f32[16,128]{1,0:T(8,128)S(1)} %get-tuple-element.21), channel_id=1, source_target_pairs={{0,1},{1,2},{2,3},{3,4},{4,5},{5,6},{6,7},{7,8},{8,9},{9,10},{10,1... | collective-permute-start | bytes 24584 | tf_op jit(solution)/shard_map/ppermute | solution.py:22
  1.4 13.1 %collective-permute-start.1 = (f32[16,128]{1,0:T(8,128)S(1)}, f32[16,128]{1,0:T(8,128)S(1)}, u32[]{:S(2)}, u32[]{:S(2)}) collective-permute-start(f32[16,128]{1,0:T(8,128)S(1)} %get-tuple-element.22), channel_id=1, source_target_pairs={{1,0},{2,1},{3,2},{4,3},{5,4},{6,5},{7,6},{8,7},{9,8},{10,9},{11,1... | collective-permute-start | bytes 24584 | tf_op jit(solution)/shard_map/ppermute | solution.py:25
  11.2 7.0 %copy-start.11 = (s32[16,256]{1,0:T(8,128)}, s32[16,256]{1,0:T(8,128)S(1)}, u32[]{:S(2)}) copy-start(s32[16,256]{1,0:T(8,128)S(1)} %convert_reduce_fusion) | copy-start | bytes 49156
  180.3 2.8 copy-start.4
  213.3 3.6 %copy-start.1 = (f32[16,8192]{1,0:T(8,128)S(1)}, f32[16,8192]{1,0:T(8,128)}, u32[]{:S(2)}) copy-start(f32[16,8192]{1,0:T(8,128)} %param.8) | copy-start | bytes 1572868
  216.8 2.7 copy-start.2
  216.9 2.7 copy-start.5
  216.9 2.7 copy-start.6
  216.9 2.7 copy-start.7
  216.9 2.7 copy-start.8
  216.9 2.7 copy-start.9
  216.9 2.7 copy-start.10
  223.2 2.8 copy-start.12
  229.4 75.8 %all-to-all-start = ((bf16[16,16,16,384]{3,2,1,0:T(8,128)(2,1)}), bf16[16,16,16,384]{3,2,1,0:T(8,128)(2,1)S(1)}, u32[]{:S(2)}, u32[]{:S(2)}) async-start(bf16[16,16,16,384]{3,2,1,0:T(8,128)(2,1)} %broadcast_select_fusion), calls=%async_computation | async-start | bytes 6291456 | tf_op jit(solution)/shard_map/all_to_all | solution.py:67
  305.2 1.6 copy-start
  322.5 1.9 copy-start.13
  326.1 10.5 %copy-start.3 = (f32[16,8,1024]{2,1,0:T(8,128)}, f32[16,8,1024]{2,1,0:T(8,128)S(1)}, u32[]{:S(2)}) copy-start(f32[16,8,1024]{2,1,0:T(8,128)S(1)} %copy.104) | copy-start | bytes 1572868
  326.2 4.8 %collective-permute-start.2 = (f32[16,1,1024]{2,1,0:T(1,128)S(1)}, f32[16,1,1024]{2,1,0:T(1,128)S(1)}, u32[]{:S(2)}, u32[]{:S(2)}) collective-permute-start(f32[16,1,1024]{2,1,0:T(1,128)S(1)} %get-tuple-element.17), channel_id=1, source_target_pairs={{1,0},{2,1},{3,2},{4,3},{5,4},{6,5},{7,6},{8,7},{9,8},{10,9},{11,1... | collective-permute-start | bytes 196616 | tf_op jit(solution)/shard_map/ppermute | solution.py:25
  329.1 6.5 %collective-permute-start.3 = (f32[16,1,1024]{2,1,0:T(1,128)S(1)}, f32[16,1,1024]{2,1,0:T(1,128)S(1)}, u32[]{:S(2)}, u32[]{:S(2)}) collective-permute-start(f32[16,1,1024]{2,1,0:T(1,128)S(1)} %get-tuple-element.18), channel_id=1, source_target_pairs={{0,1},{1,2},{2,3},{3,4},{4,5},{5,6},{6,7},{7,8},{8,9},{9,10},{10,1... | collective-permute-start | bytes 196616 | tf_op jit(solution)/shard_map/ppermute | solution.py:22
where the time goes:
time: 338 us; the launch traced here: 337 us
  local copies, waits for them, and re-layouts  220 us (65%)
  waiting for transfers between devices  73.9 us (22%)
  other arithmetic  16.7 us (5%)
  starting transfers between devices  13.2 us (4%)
  matrix products  11.5 us (3%)
    gather x12, local copies, waits for them, and re-layouts, local(): difference = jnp.take(extended, neighbours[offset], axis=1) - source_field  199 us
    all_to_all x1, waiting for transfers between devices, local(): lax.all_to_all(sending, 'src', split_axis=0, concat_axis=0, tiled=True)  69.4 us
    dot_general x1, matrix products, local(): jnp.einsum('pli,pio->plo', gathered, remap_weights, preferred_element_typ...  10.3 us
  transfers between devices with their start and end apart: 5, of which 2 were waited for; matrix products, arithmetic and copies ran while one was open for 3% of the time, Pallas kernels for 0%

commit v1 on v0

v1 whole, which is shorter than its diff:
```python
import functools

import jax
import jax.numpy as jnp
from jax import lax
from jax.experimental import pallas as pl
from jax.experimental.pallas import tpu as pltpu
from jax.sharding import PartitionSpec as P

K = 6
BLK = 128
HALO = 128
NB = 64
LAT_DEV = 8
LONB = 8
DB = 64
ROWS = 9
CODE = 32767.0
FIELD_BOUND = 6.0
WEIGHT_BOUND = 2.0
VMEM = pl.BlockSpec(memory_space=pltpu.VMEM)
SMEM = pl.BlockSpec(memory_space=pltpu.SMEM)
ANY = pl.BlockSpec(memory_space=pl.ANY)


def encode(values, bound):
    scaled = jnp.abs(values) * (1.0 / bound)
    root = jnp.exp2(jnp.log2(jnp.maximum(scaled, 1e-30)) * 0.2)
    code = jnp.minimum(jnp.floor(root * CODE + 0.5), CODE)
    code = jnp.where(scaled > 1e-24, code, 0.0)
    return jnp.where(values < 0, -code, code).astype(jnp.int32)


def pack(high, low):
    return high * 65536 + (low + 32768)


def unpack(word):
    return word >> 16, (word & 65535) - 32768


def decode(code, bound):
    real = code.astype(jnp.float32)
    square = real * real
    return square * square * (real * (bound / CODE**5))


def pack_field_kernel(field_ref, out_ref):
    half = field_ref.shape[0] // 2
    high = encode(field_ref[:half], FIELD_BOUND)
    low = encode(field_ref[half:], FIELD_BOUND)
    out_ref[...] = pack(high, low)


def pack_field(field):
    levels, cells = field.shape
    step = 2048
    return pl.pallas_call(
        pack_field_kernel,
        grid=(cells // step,),
        in_specs=[pl.BlockSpec((levels, step), lambda i: (0, i))],
        out_specs=pl.BlockSpec((levels // 2, step), lambda i: (0, i)),
        out_shape=jax.ShapeDtypeStruct((levels // 2, cells), jnp.int32),
    )(field)


def pack_geometry_kernel(neighbours_ref, weights_ref, out_ref):
    step = out_ref.shape[1]
    column = lax.broadcasted_iota(jnp.int32, (1, step), 1) + pl.program_id(0) * step
    start = (column >> 7) << 7
    relative = neighbours_ref[...] - start
    for k in range(K):
        east = encode(weights_ref[k, 0:1, :], WEIGHT_BOUND)
        north = encode(weights_ref[k, 1:2, :], WEIGHT_BOUND)
        out_ref[k : k + 1, :] = pack(east, north)
    for k in range(K // 2):
        out_ref[K + k : K + k + 1, :] = pack(relative[k : k + 1], relative[k + 3 : k + 4])


def pack_geometry(neighbours, slope_weights):
    cells = neighbours.shape[1]
    step = 2048
    return pl.pallas_call(
        pack_geometry_kernel,
        grid=(cells // step,),
        in_specs=[
            pl.BlockSpec((K, step), lambda i: (0, i)),
            pl.BlockSpec((K, 2, step), lambda i: (0, 0, i)),
        ],
        out_specs=pl.BlockSpec((16, step), lambda i: (0, i)),
        out_shape=jax.ShapeDtypeStruct((16, cells), jnp.int32),
    )(neighbours, jnp.transpose(slope_weights, (1, 0, 2)))


def choose_geometry_kernel(block_ref, packed_ref, out_ref):
    tiles, slots = block_ref.shape

    def tile(t, carry):
        for s in range(slots):
            lanes = pl.ds(pl.multiple_of(block_ref[t, s] * BLK, BLK), BLK)
            out_ref[t, s * ROWS : (s + 1) * ROWS, :] = packed_ref[:ROWS, lanes]
        return carry

    lax.fori_loop(0, tiles, tile, 0)


def choose_geometry(blocks, packed):
    tiles, slots = blocks.shape
    return pl.pallas_call(
        choose_geometry_kernel,
        in_specs=[SMEM, VMEM],
        out_specs=VMEM,
        out_shape=jax.ShapeDtypeStruct((tiles, slots * ROWS, BLK), jnp.int32),
    )(blocks, packed)


def ranks(present):
    ids = jnp.arange(NB, dtype=jnp.int32)
    before = (ids[:, None] < ids[None, :])[None]
    return jnp.sum((present[:, :, None] & before).astype(jnp.int32), axis=1)


def blocks_of_slots(present, rank, slots):
    ids = jnp.arange(NB, dtype=jnp.int32)
    wanted = jnp.arange(slots, dtype=jnp.int32)
    match = present[:, :, None] & (rank[:, :, None] == wanted[None, None, :])
    return jnp.sum(jnp.where(match, ids[None, :, None], 0), axis=1)


def slopes_and_moments(window, words):
    low_block, mid_block, high_block = window
    east_code, north_code = unpack(words[0:K])
    east_weight = decode(east_code, WEIGHT_BOUND)
    north_weight = decode(north_code, WEIGHT_BOUND)
    first, second = unpack(words[K : K + 3])
    own = [decode(code, FIELD_BOUND) for code in unpack(mid_block)]
    east = [jnp.zeros_like(own[0]) for _ in own]
    north = [jnp.zeros_like(own[0]) for _ in own]
    shape = mid_block.shape
    for k in range(K):
        row = first[k : k + 1] if k < 3 else second[k - 3 : k - 2]
        place = jnp.broadcast_to(row, shape)
        lane = place & (BLK - 1)
        picked = [
            jnp.take_along_axis(part, lane, axis=1, mode="promise_in_bounds")
            for part in (low_block, mid_block, high_block)
        ]
        word = jnp.where(place < BLK, picked[0], jnp.where(place < 2 * BLK, picked[1], picked[2]))
        for side, code in enumerate(unpack(word)):
            difference = decode(code, FIELD_BOUND) - own[side]
            east[side] = east[side] + east_weight[k : k + 1] * difference
            north[side] = north[side] + north_weight[k : k + 1] * difference
    return [jnp.concatenate(part, axis=0).astype(jnp.bfloat16) for part in (own, east, north)]


def remap_kernel(parts, chunk, slots, *refs):
    me_ref, block_ref, slot_ref, dest_ref, geometry_ref, weights_ref = refs[:6]
    shards = refs[6 : 6 + len(parts)]
    out_ref, edge_ref = refs[6 + len(parts) : 8 + len(parts)]
    field, moments, weights, total, field_sem, weight_sem = refs[8 + len(parts) :]
    partitions = block_ref.shape[0]
    cells = NB * BLK
    blocks = partitions * NB
    pairs = slot_ref.shape[0]
    chunks = pairs // chunk
    me = me_ref[0]

    copies = []
    for (code, start, size), shard in zip(parts, shards):
        if code is None:
            target = field
        else:
            lanes = pl.ds(pl.multiple_of((me ^ code) * cells + start, BLK), size)
            target = field.at[:, lanes]
        copies.append(pltpu.make_async_copy(shard, target, field_sem))
    for copy in copies:
        copy.start()

    def weight_copy(c):
        piece = pl.ds(c * chunk, chunk)
        return pltpu.make_async_copy(weights_ref.at[piece], weights.at[piece], weight_sem.at[c])

    for c in range(chunks):
        weight_copy(c).start()
    total[...] = jnp.zeros_like(total)
    for copy in copies:
        copy.wait()

    def source(q, carry):
        for s in range(slots):
            block = q * NB + block_ref[q, s]
            window = []
            for shift in (-1, 0, 1):
                near = lax.rem(block + (shift + blocks), blocks)
                window.append(field[:, pl.ds(pl.multiple_of(near * BLK, BLK), BLK)])
            words = geometry_ref[q, s * ROWS : (s + 1) * ROWS, :]
            for m, part in enumerate(slopes_and_moments(window, words)):
                moments[q * slots + s, :, m * BLK : (m + 1) * BLK] = part
        return carry

    lax.fori_loop(0, partitions, source, 0)

    def piece(c, carry):
        weight_copy(c).wait()
        for i in range(chunk):
            p = c * chunk + i
            product = jnp.dot(moments[slot_ref[p]], weights[p], preferred_element_type=jnp.float32)
            dest = dest_ref[p]
            rows = pl.ds(dest >> 3, 16, stride=LAT_DEV)
            total[dest & 7, rows, :] = total[dest & 7, rows, :] + product
        return carry

    lax.fori_loop(0, chunks, piece, 0)
    levels = out_ref.shape[0]
    for o in range(LONB):
        lanes = slice(o * BLK, (o + 1) * BLK)
        out_ref[:, :, lanes] = total[o].reshape(levels, LAT_DEV, BLK)
        edge_ref[0, :, lanes] = total[o, pl.ds(0, levels, stride=LAT_DEV), :]
        edge_ref[1, :, lanes] = total[o, pl.ds(LAT_DEV - 1, levels, stride=LAT_DEV), :]


def remap(me, blocks, slot, dest, geometry, weights, parts, shards, levels):
    partitions, slots = blocks.shape
    pairs = slot.shape[0]
    chunk = 16
    return pl.pallas_call(
        functools.partial(remap_kernel, parts, chunk, slots),
        in_specs=[SMEM] * 4 + [VMEM, ANY] + [ANY] * len(shards),
        out_specs=(VMEM, VMEM),
        out_shape=(
            jax.ShapeDtypeStruct((levels, LAT_DEV, LONB * BLK), jnp.float32),
            jax.ShapeDtypeStruct((2, levels, LONB * BLK), jnp.float32),
        ),
        scratch_shapes=[
            pltpu.VMEM((levels // 2, partitions * NB * BLK), jnp.int32),
            pltpu.VMEM((partitions * slots, levels, 3 * BLK), jnp.bfloat16),
            pltpu.VMEM(weights.shape, jnp.bfloat16),
            pltpu.VMEM((LONB, levels * LAT_DEV, BLK), jnp.float32),
            pltpu.SemaphoreType.DMA,
            pltpu.SemaphoreType.DMA((pairs // chunk,)),
        ],
        compiler_params=pltpu.CompilerParams(vmem_limit_bytes=56 * 1024 * 1024),
    )(me, blocks, slot, dest, geometry, weights, *shards)


def share_field(packed, count):
    if count != 16:
        whole = lax.all_gather(packed, "src", axis=1, tiled=True)
        return [(None, 0, whole.shape[1])], [whole]

    def swap(array, code):
        return lax.ppermute(array, "src", [(i, i ^ code) for i in range(count)])

    cells = packed.shape[1]
    half = cells // 2
    far = swap(packed, 8)
    z = swap(packed, 4)
    y = swap(packed, 2)
    diagonal = swap(z, 2)
    far_z = swap(far, 4)
    far_y = swap(far, 2)
    far_low = swap(far_z[:, :half], 2)
    far_high = swap(far_y[:, half:], 4)
    held = [
        (0, 0, packed),
        (2, 0, y),
        (4, 0, z),
        (6, 0, diagonal),
        (8, 0, far),
        (12, 0, far_z),
        (10, 0, far_y),
        (14, 0, far_low),
        (14, half, far_high),
    ]
    held = held + [(code ^ 1, start, swap(array, 1)) for code, start, array in held]
    parts = [(code, start, array.shape[1]) for code, start, array in held]
    return parts, [array for _, _, array in held]


def local(source_field, neighbours, slope_weights, pair_block, pair_dest, remap_weights):
    levels, cell_count = source_field.shape
    own_index = lax.axis_index("src")
    partitions = lax.axis_size("src")
    pair_total = pair_block.shape[1]
    slots = max(1, pair_total // partitions // 2)
    ids = jnp.arange(NB, dtype=jnp.int32)

    packed = pack_field(source_field)
    parts, shards = share_field(packed, partitions)

    own_names = own_index * NB + ids
    asked = jnp.any(pair_block[:, :, None] == own_names[None, None, :], axis=1)
    outgoing_blocks = blocks_of_slots(asked, ranks(asked), slots)
    geometry = choose_geometry(outgoing_blocks, pack_geometry(neighbours, slope_weights))
    geometry = lax.all_to_all(geometry, "src", split_axis=0, concat_axis=0, tiled=True)

    row = lax.dynamic_index_in_dim(pair_block, own_index, 0, keepdims=False)
    names = jnp.arange(partitions * NB, dtype=jnp.int32)
    same = row[:, None] == names[None, :]
    needed = jnp.any(same, axis=0).reshape(partitions, NB)
    rank = ranks(needed)
    blocks = blocks_of_slots(needed, rank, slots)
    slot_of_name = (jnp.arange(partitions, dtype=jnp.int32)[:, None] * slots + rank).reshape(-1)
    slot = jnp.sum(jnp.where(same, slot_of_name[None, :], 0), axis=1)

    remapped, edges = remap(
        own_index.reshape(1), blocks, slot, pair_dest[0], geometry, remap_weights, parts, shards, levels
    )
    up = [(i, i + 1) for i in range(partitions - 1)]
    down = [(i + 1, i) for i in range(partitions - 1)]
    below = lax.ppermute(edges[1], "src", up)
    above = lax.ppermute(edges[0], "src", down)
    padded = jnp.concatenate([below[:, None], remapped, above[:, None]], axis=1)
    meridional = 0.5 * (padded[:, 2:] - padded[:, :-2])
    return remapped, meridional


def solution(mesh):
    return jax.shard_map(
        local,
        mesh=mesh,
        in_specs=(
            P("groups", "src"),
            P(None, "src"),
            P(None, None, "src"),
            P(),
            P("src", None),
            P("src", None, None),
        ),
        out_specs=(P("groups", "src", None), P("groups", "src", None)),
        check_vma=False,
    )
```

time: 338 us -> 91.4 us (0.27)
  local copies, waits for them, and re-layouts: 220 us -> 4.69 us
  waiting for transfers between devices: 73.9 us -> 25.7 us
  Pallas kernels: 0 us -> 32.9 us
  matrix products: 11.5 us -> 0 us
  other arithmetic: 16.7 us -> 6.75 us
  starting transfers between devices: 13.2 us -> 19.7 us
    gather x14 -> x0, local copies, waits for them, and re-layouts: 205 us -> none  [the longest x12 199 us: local(): difference = jnp.take(extended, neighbours[offset], axis=1) - source_field]
    all_to_all x1, waiting for transfers between devices: 69.4 us -> 0.01 us  [local(): lax.all_to_all(geometry, 'src', split_axis=0, concat_axis=0, tiled=True)]
    pallas_call x0 -> x4, Pallas kernels: none -> 32.9 us  [the longest x1 24 us: remap(): pl.pallas_call(functools.partial(remap_kernel, parts, chunk, slots), in_s...]
    ppermute x4 -> x19, waiting for transfers between devices: 4.55 us -> 25.7 us  [the longest x17 21.2 us: swap(): return lax.ppermute(array, 'src', [(i, i ^ code) for i in range(count)])]
    dot_general x2 -> x0, matrix products: 11.5 us -> none  [the longest x1 10.3 us: local(): jnp.einsum('pli,pio->plo', gathered, remap_weights, preferred_element_typ...]
    ppermute x4 -> x19, starting transfers between devices: 7.47 us -> 13.3 us  [the longest x17 8.35 us: swap(): return lax.ppermute(array, 'src', [(i, i ^ code) for i in range(count)])]
    select_n x4 -> x0, other arithmetic: 4.81 us -> none  [the longest x2 3.37 us: outgoing(): chosen = jnp.take(moments, block_index.reshape(-1), axis=0)]
  transfers between devices with their start and end apart: 5 -> 20, of which waited for: 2 -> 8; matrix products, arithmetic and copies ran while one was open for 3% -> 8% of each run, Pallas kernels for 0% -> 6%
where the time goes in v1:
time: 91.4 us; the launch traced here: 90.6 us
  Pallas kernels  32.9 us (36%)
  waiting for transfers between devices  25.7 us (28%)
  starting transfers between devices  19.7 us (22%)
  other arithmetic  6.75 us (7%)
  local copies, waits for them, and re-layouts  4.69 us (5%)
    pallas_call x1, Pallas kernels, remap(): pl.pallas_call(functools.partial(remap_kernel, parts, chunk, slots), in_s...  24 us
    ppermute x17, waiting for transfers between devices, swap(): return lax.ppermute(array, 'src', [(i, i ^ code) for i in range(count)])  21.2 us
    ppermute x17, starting transfers between devices, swap(): return lax.ppermute(array, 'src', [(i, i ^ code) for i in range(count)])  8.35 us
    all_to_all x1, starting transfers between devices, local(): lax.all_to_all(geometry, 'src', split_axis=0, concat_axis=0, tiled=True)  6.41 us
    ppermute x1, waiting for transfers between devices, local(): below = lax.ppermute(edges[1], 'src', up)  4.47 us
    pallas_call x1, Pallas kernels, pack_geometry(): pl.pallas_call(pack_geometry_kernel, grid=(cells // step,), in_specs=[pl....  3.38 us
    pallas_call x1, Pallas kernels, pack_field(): pl.pallas_call(pack_field_kernel, grid=(cells // step,), in_specs=[pl.Blo...  3.27 us
    ppermute x1, starting transfers between devices, local(): above = lax.ppermute(edges[0], 'src', down)  3.01 us
  transfers between devices with their start and end apart: 20, of which 8 were waited for; matrix products, arithmetic and copies ran while one was open for 8% of the time, Pallas kernels for 6%

profile of v1, /device:TPU:18, one launch (start us, length us, event | category | flops | bytes accessed | tf_op | source)
XLA Modules:
  0.0 90.6 jit_solution(672420748925032488)
XLA Ops:
  0.6 3.3 %shard_map.79.refs_6_ = s32[8,8192]{1,0:T(8,128)} custom-call(f32[16,8192]{1,0:T(8,128)} %field_ref.1), custom_call_target="tpu_custom_call" | custom-call | tf_op jit(solution)/shard_map/pallas_call | solution.py:58
  4.3 0.7 constant_dynamic-slice_fusion
  5.3 1.1 %compare_reduce_fusion = pred[16,64]{1,0:T(8,128)(4,1)S(1)} fusion(s32[16,256]{1,0:T(8,128)} %param.9, s32[64]{0:T(128)S(1)} %iota_add_fusion), kind=kLoop, calls=%fused_computation.3 | loop fusion | flops 523264 | bytes 17664 | tf_op jit(solution)/shard_map/reduce_or | solution.py:292
  6.8 3.4 %shard_map.77.packed_ref = s32[16,8192]{1,0:T(8,128)} custom-call(s32[6,8192]{1,0:T(8,128)} %neighbours_ref.1, f32[6,2,8192]{2,1,0:T(2,128)} %bitcast.10), custom_call_target="tpu_custom_call" | custom-call | tf_op jit(solution)/shard_map/pallas_call | solution.py:83
  10.2 0.9 %select_reduce_fusion.1.block_ref = s32[16,8]{1,0:T(8,128)} fusion(s32[16,64]{1,0:T(8,128)S(1)} %get-tuple-element.6, pred[16,64]{1,0:T(8,128)(4,1)S(1)} %compare_reduce_fusion), kind=kLoop, calls=%fused_computation.12 | loop fusion | flops 32640 | bytes 5632 | tf_op jit(solution)/shard_map/reduce_sum | solution.py:127
  11.1 2.2 %shard_map.78 = s32[16,72,128]{2,1,0:T(8,128)} custom-call(s32[16,8]{1,0:T(8,128)} %select_reduce_fusion.1.block_ref, s32[16,8192]{1,0:T(8,128)} %shard_map.77.packed_ref), custom_call_target="tpu_custom_call" | custom-call | tf_op jit(solution)/shard_map/pallas_call | solution.py:109
  13.3 6.4 %all-to-all-start = ((s32[16,72,128]{2,1,0:T(8,128)}), s32[16,72,128]{2,1,0:T(8,128)S(1)}, u32[]{:S(2)}, u32[]{:S(2)}) async-start(s32[16,72,128]{2,1,0:T(8,128)} %shard_map.78), calls=%async_computation | async-start | bytes 1179648 | tf_op jit(solution)/shard_map/all_to_all | solution.py:295
  19.7 1.5 %collective-permute-start.1 = (s32[8,8192]{1,0:T(8,128)}, s32[8,8192]{1,0:T(8,128)S(1)}, u32[]{:S(2)}, u32[]{:S(2)}) collective-permute-start(s32[8,8192]{1,0:T(8,128)} %shard_map.79.refs_6_), channel_id=1, source_target_pairs={{0,4},{1,5},{2,6},{3,7},{4,0},{5,1},{6,2},{7,3},{8,12},{9,13},{10,... | collective-permute-start | bytes 786440 | tf_op jit(solution)/shard_map/ppermute | solution.py:252
  21.2 1.5 %collective-permute-start = (s32[8,8192]{1,0:T(8,128)}, s32[8,8192]{1,0:T(8,128)S(1)}, u32[]{:S(2)}, u32[]{:S(2)}) collective-permute-start(s32[8,8192]{1,0:T(8,128)} %shard_map.79.refs_6_), channel_id=1, source_target_pairs={{0,2},{1,3},{2,0},{3,1},{4,6},{5,7},{6,4},{7,5},{8,10},{9,11},{10,... | collective-permute-start | bytes 786440 | tf_op jit(solution)/shard_map/ppermute | solution.py:252
  23.8 14.3 %collective-permute-done.1.refs_8_ = s32[8,8192]{1,0:T(8,128)S(1)} collective-permute-done((s32[8,8192]{1,0:T(8,128)}, s32[8,8192]{1,0:T(8,128)S(1)}, u32[]{:S(2)}, u32[]{:S(2)}) %collective-permute-start.1) | collective-permute-done | bytes 262176 | tf_op jit(solution)/shard_map/ppermute | solution.py:252
  38.6 1.3 %collective-permute-done.5.refs_12_ = s32[8,8192]{1,0:T(8,128)S(1)} collective-permute-done((s32[8,8192]{1,0:T(8,128)S(1)}, s32[8,8192]{1,0:T(8,128)S(1)}, u32[]{:S(2)}, u32[]{:S(2)}) %collective-permute-start.5) | collective-permute-done | bytes 262176 | tf_op jit(solution)/shard_map/ppermute | solution.py:252
  40.6 2.6 %collective-permute-done.4.refs_11_ = s32[8,8192]{1,0:T(8,128)S(1)} collective-permute-done((s32[8,8192]{1,0:T(8,128)S(1)}, s32[8,8192]{1,0:T(8,128)S(1)}, u32[]{:S(2)}, u32[]{:S(2)}) %collective-permute-start.4) | collective-permute-done | bytes 262176 | tf_op jit(solution)/shard_map/ppermute | solution.py:252
  43.2 0.7 slice.27
  45.1 1.5 %collective-permute-start.6 = (s32[8,4096]{1,0:T(8,128)}, s32[8,4096]{1,0:T(8,128)}, u32[]{:S(2)}, u32[]{:S(2)}) collective-permute-start(s32[8,4096]{1,0:T(8,128)} %slice.26), channel_id=1, source_target_pairs={{0,2},{1,3},{2,0},{3,1},{4,6},{5,7},{6,4},{7,5},{8,10},{9,11},{10,... | collective-permute-start | bytes 393224 | tf_op jit(solution)/shard_map/ppermute | solution.py:252
  46.6 1.3 %collective-permute-done.2.refs_9_ = s32[8,8192]{1,0:T(8,128)S(1)} collective-permute-done((s32[8,8192]{1,0:T(8,128)S(1)}, s32[8,8192]{1,0:T(8,128)S(1)}, u32[]{:S(2)}, u32[]{:S(2)}) %collective-permute-start.2) | collective-permute-done | bytes 262176 | tf_op jit(solution)/shard_map/ppermute | solution.py:252
  48.5 0.9 %select_reduce_fusion.2.refs_1_ = s32[16,8]{1,0:T(8,128)} fusion(s32[16,64]{1,0:T(8,128)S(1)} %get-tuple-element.7, pred[16,64]{1,0:T(8,128)(4,1)S(1)} %and.45), kind=kLoop, calls=%fused_computation.14 | loop fusion | flops 32640 | bytes 5632 | tf_op jit(solution)/shard_map/reduce_sum | solution.py:127
  49.4 1.4 %collective-permute-done.7.refs_14_ = s32[8,4096]{1,0:T(8,128)} collective-permute-done((s32[8,4096]{1,0:T(8,128)}, s32[8,4096]{1,0:T(8,128)}, u32[]{:S(2)}, u32[]{:S(2)}) %collective-permute-start.7) | collective-permute-done | bytes 131104 | tf_op jit(solution)/shard_map/ppermute | solution.py:252
  51.3 0.8 select_reduce_fusion.refs_2_
  53.8 24.0 %shard_map.80 = (f32[16,8,1024]{2,1,0:T(8,128)}, f32[2,16,1024]{2,1,0:T(8,128)}) custom-call(s32[1]{0:T(128)} %bitcast.refs_0_, s32[16,8]{1,0:T(8,128)} %select_reduce_fusion.2.refs_1_, s32[256]{0:T(256)} %select_reduce_fusion.refs_2_, s32[256]{0:T(256)} %bitcast.15, s32[16,72,128]{2,1,0:T(8,128)} %copy-done, bf16[256,384,128]{2,1,0:T(8,128)(2,1)} %refs_5_.1, ...), custom_call_target="tpu_custom_call" | custom-call | tf_op jit(solution)/shard_map/pallas_call | solution.py:226
  77.9 0.9 slice_bitcast_fusion.1
  78.8 3.0 %collective-permute-start.17 = (f32[16,1024]{1,0:T(8,128)S(1)}, f32[16,1024]{1,0:T(8,128)S(1)}, u32[]{:S(2)}, u32[]{:S(2)}) collective-permute-start(f32[16,1024]{1,0:T(8,128)S(1)} %get-tuple-element.8), channel_id=1, source_target_pairs={{1,0},{2,1},{3,2},{4,3},{5,4},{6,5},{7,6},{8,7},{9,8},{10,9},{11,1... | collective-permute-start | bytes 196616 | tf_op jit(solution)/shard_map/ppermute | solution.py:312
  81.8 1.9 %collective-permute-start.18 = (f32[16,1024]{1,0:T(8,128)S(1)}, f32[16,1024]{1,0:T(8,128)S(1)}, u32[]{:S(2)}, u32[]{:S(2)}) collective-permute-start(f32[16,1024]{1,0:T(8,128)S(1)} %get-tuple-element.9), channel_id=1, source_target_pairs={{0,1},{1,2},{2,3},{3,4},{4,5},{5,6},{6,7},{7,8},{8,9},{9,10},{10,1... | collective-permute-start | bytes 196616 | tf_op jit(solution)/shard_map/ppermute | solution.py:311
  83.8 4.5 %collective-permute-done.18 = f32[16,1024]{1,0:T(8,128)S(1)} collective-permute-done((f32[16,1024]{1,0:T(8,128)S(1)}, f32[16,1024]{1,0:T(8,128)S(1)}, u32[]{:S(2)}, u32[]{:S(2)}) %collective-permute-start.18) | collective-permute-done | bytes 65568 | tf_op jit(solution)/shard_map/ppermute | solution.py:311
  88.4 2.2 %fusion.2 = f32[16,8,1024]{2,1,0:T(8,128)} fusion(f32[16,8,1024]{2,1,0:T(8,128)} %get-tuple-element.2, f32[16,1,1024]{2,1,0:T(1,128)S(1)} %copy.11, f32[16,1,1024]{2,1,0:T(1,128)S(1)} %copy.10), kind=kLoop, calls=%fused_computation.6 | loop fusion | flops 524288 | bytes 1179648 | tf_op jit(solution)/shard_map/mul | solution.py:314
  (65 shorter events, 7.4 us)
Async XLA Ops:
  3.9 18.7 %collective-permute-start.3 = (s32[8,8192]{1,0:T(8,128)}, s32[8,8192]{1,0:T(8,128)S(1)}, u32[]{:S(2)}, u32[]{:S(2)}) collective-permute-start(s32[8,8192]{1,0:T(8,128)} %shard_map.79.refs_6_), channel_id=1, source_target_pairs={{0,8},{1,9},{2,10},{3,11},{4,12},{5,13},{6,14},{7,15},{8,0},{9,1},... | collective-permute-start | bytes 786440 | tf_op jit(solution)/shard_map/ppermute | solution.py:252
  13.3 39.7 %all-to-all-start = ((s32[16,72,128]{2,1,0:T(8,128)}), s32[16,72,128]{2,1,0:T(8,128)S(1)}, u32[]{:S(2)}, u32[]{:S(2)}) async-start(s32[16,72,128]{2,1,0:T(8,128)} %shard_map.78), calls=%async_computation | async-start | bytes 1179648 | tf_op jit(solution)/shard_map/all_to_all | solution.py:295
  19.7 18.4 %collective-permute-start.1 = (s32[8,8192]{1,0:T(8,128)}, s32[8,8192]{1,0:T(8,128)S(1)}, u32[]{:S(2)}, u32[]{:S(2)}) collective-permute-start(s32[8,8192]{1,0:T(8,128)} %shard_map.79.refs_6_), channel_id=1, source_target_pairs={{0,4},{1,5},{2,6},{3,7},{4,0},{5,1},{6,2},{7,3},{8,12},{9,13},{10,... | collective-permute-start | bytes 786440 | tf_op jit(solution)/shard_map/ppermute | solution.py:252
  21.2 16.9 %collective-permute-start = (s32[8,8192]{1,0:T(8,128)}, s32[8,8192]{1,0:T(8,128)S(1)}, u32[]{:S(2)}, u32[]{:S(2)}) collective-permute-start(s32[8,8192]{1,0:T(8,128)} %shard_map.79.refs_6_), channel_id=1, source_target_pairs={{0,2},{1,3},{2,0},{3,1},{4,6},{5,7},{6,4},{7,5},{8,10},{9,11},{10,... | collective-permute-start | bytes 786440 | tf_op jit(solution)/shard_map/ppermute | solution.py:252
  22.6 30.4 %copy-start.3 = (s32[8,8192]{1,0:T(8,128)}, s32[8,8192]{1,0:T(8,128)S(1)}, u32[]{:S(2)}) copy-start(s32[8,8192]{1,0:T(8,128)S(1)} %collective-permute-done.3.refs_10_) | copy-start | bytes 786436
  22.6 17.3 %collective-permute-start.5 = (s32[8,8192]{1,0:T(8,128)S(1)}, s32[8,8192]{1,0:T(8,128)S(1)}, u32[]{:S(2)}, u32[]{:S(2)}) collective-permute-start(s32[8,8192]{1,0:T(8,128)S(1)} %collective-permute-done.3.refs_10_), channel_id=1, source_target_pairs={{0,2},{1,3},{2,0},{3,1},{4,6},{5,7},{6,4},{7,5},{8,10},{9,11},{10,... | collective-permute-start | bytes 786440 | tf_op jit(solution)/shard_map/ppermute | solution.py:252
  23.2 20.0 %collective-permute-start.4 = (s32[8,8192]{1,0:T(8,128)S(1)}, s32[8,8192]{1,0:T(8,128)S(1)}, u32[]{:S(2)}, u32[]{:S(2)}) collective-permute-start(s32[8,8192]{1,0:T(8,128)S(1)} %collective-permute-done.3.refs_10_), channel_id=1, source_target_pairs={{0,4},{1,5},{2,6},{3,7},{4,0},{5,1},{6,2},{7,3},{8,12},{9,13},{10,... | collective-permute-start | bytes 786440 | tf_op jit(solution)/shard_map/ppermute | solution.py:252
  23.8 20.9 %collective-permute-start.8 = (s32[8,8192]{1,0:T(8,128)}, s32[8,8192]{1,0:T(8,128)S(1)}, u32[]{:S(2)}, u32[]{:S(2)}) collective-permute-start(s32[8,8192]{1,0:T(8,128)} %shard_map.79.refs_6_), channel_id=1, source_target_pairs={{0,1},{1,0},{2,3},{3,2},{4,5},{5,4},{6,7},{7,6},{8,9},{9,8},{10,11... | collective-permute-start | bytes 786440 | tf_op jit(solution)/shard_map/ppermute | solution.py:252
  38.1 15.0 %copy-start.4 = (s32[8,8192]{1,0:T(8,128)}, s32[8,8192]{1,0:T(8,128)S(1)}, u32[]{:S(2)}) copy-start(s32[8,8192]{1,0:T(8,128)S(1)} %collective-permute-done.1.refs_8_) | copy-start | bytes 786436
  38.1 7.0 %collective-permute-start.12 = (s32[8,8192]{1,0:T(8,128)S(1)}, s32[8,8192]{1,0:T(8,128)S(1)}, u32[]{:S(2)}, u32[]{:S(2)}) collective-permute-start(s32[8,8192]{1,0:T(8,128)S(1)} %collective-permute-done.3.refs_10_), channel_id=1, source_target_pairs={{0,1},{1,0},{2,3},{3,2},{4,5},{5,4},{6,7},{7,6},{8,9},{9,8},{10,11... | collective-permute-start | bytes 786440 | tf_op jit(solution)/shard_map/ppermute | solution.py:252
  38.1 15.0 %copy-start.5 = (s32[8,8192]{1,0:T(8,128)}, s32[8,8192]{1,0:T(8,128)S(1)}, u32[]{:S(2)}) copy-start(s32[8,8192]{1,0:T(8,128)S(1)} %collective-permute-done.refs_7_) | copy-start | bytes 786436
  38.1 8.4 %collective-permute-start.10 = (s32[8,8192]{1,0:T(8,128)S(1)}, s32[8,8192]{1,0:T(8,128)S(1)}, u32[]{:S(2)}, u32[]{:S(2)}) collective-permute-start(s32[8,8192]{1,0:T(8,128)S(1)} %collective-permute-done.1.refs_8_), channel_id=1, source_target_pairs={{0,1},{1,0},{2,3},{3,2},{4,5},{5,4},{6,7},{7,6},{8,9},{9,8},{10,11... | collective-permute-start | bytes 786440 | tf_op jit(solution)/shard_map/ppermute | solution.py:252
  39.9 13.1 %copy-start.1 = (s32[8,8192]{1,0:T(8,128)}, s32[8,8192]{1,0:T(8,128)S(1)}, u32[]{:S(2)}) copy-start(s32[8,8192]{1,0:T(8,128)S(1)} %collective-permute-done.5.refs_12_) | copy-start | bytes 786436
  39.9 7.9 %collective-permute-start.2 = (s32[8,8192]{1,0:T(8,128)S(1)}, s32[8,8192]{1,0:T(8,128)S(1)}, u32[]{:S(2)}, u32[]{:S(2)}) collective-permute-start(s32[8,8192]{1,0:T(8,128)S(1)} %collective-permute-done.1.refs_8_), channel_id=1, source_target_pairs={{0,2},{1,3},{2,0},{3,1},{4,6},{5,7},{6,4},{7,5},{8,10},{9,11},{10,... | collective-permute-start | bytes 786440 | tf_op jit(solution)/shard_map/ppermute | solution.py:252
  43.2 4.6 %collective-permute-start.9 = (s32[8,8192]{1,0:T(8,128)S(1)}, s32[8,8192]{1,0:T(8,128)S(1)}, u32[]{:S(2)}, u32[]{:S(2)}) collective-permute-start(s32[8,8192]{1,0:T(8,128)S(1)} %collective-permute-done.refs_7_), channel_id=1, source_target_pairs={{0,1},{1,0},{2,3},{3,2},{4,5},{5,4},{6,7},{7,6},{8,9},{9,8},{10,11... | collective-permute-start | bytes 786440 | tf_op jit(solution)/shard_map/ppermute | solution.py:252
  44.6 6.2 %collective-permute-start.7 = (s32[8,4096]{1,0:T(8,128)}, s32[8,4096]{1,0:T(8,128)}, u32[]{:S(2)}, u32[]{:S(2)}) collective-permute-start(s32[8,4096]{1,0:T(8,128)} %slice.27), channel_id=1, source_target_pairs={{0,4},{1,5},{2,6},{3,7},{4,0},{5,1},{6,2},{7,3},{8,12},{9,13},{10,... | collective-permute-start | bytes 393224 | tf_op jit(solution)/shard_map/ppermute | solution.py:252
  45.1 5.9 %collective-permute-start.6 = (s32[8,4096]{1,0:T(8,128)}, s32[8,4096]{1,0:T(8,128)}, u32[]{:S(2)}, u32[]{:S(2)}) collective-permute-start(s32[8,4096]{1,0:T(8,128)} %slice.26), channel_id=1, source_target_pairs={{0,2},{1,3},{2,0},{3,1},{4,6},{5,7},{6,4},{7,5},{8,10},{9,11},{10,... | collective-permute-start | bytes 393224 | tf_op jit(solution)/shard_map/ppermute | solution.py:252
  46.5 5.6 %collective-permute-start.14 = (s32[8,8192]{1,0:T(8,128)S(1)}, s32[8,8192]{1,0:T(8,128)S(1)}, u32[]{:S(2)}, u32[]{:S(2)}) collective-permute-start(s32[8,8192]{1,0:T(8,128)S(1)} %collective-permute-done.5.refs_12_), channel_id=1, source_target_pairs={{0,1},{1,0},{2,3},{3,2},{4,5},{5,4},{6,7},{7,6},{8,9},{9,8},{10,11... | collective-permute-start | bytes 786440 | tf_op jit(solution)/shard_map/ppermute | solution.py:252
  47.8 4.3 %collective-permute-start.13 = (s32[8,8192]{1,0:T(8,128)S(1)}, s32[8,8192]{1,0:T(8,128)}, u32[]{:S(2)}, u32[]{:S(2)}) collective-permute-start(s32[8,8192]{1,0:T(8,128)S(1)} %collective-permute-done.4.refs_11_), channel_id=1, source_target_pairs={{0,1},{1,0},{2,3},{3,2},{4,5},{5,4},{6,7},{7,6},{8,9},{9,8},{10,11... | collective-permute-start | bytes 786440 | tf_op jit(solution)/shard_map/ppermute | solution.py:252
  47.8 4.3 %collective-permute-start.11 = (s32[8,8192]{1,0:T(8,128)S(1)}, s32[8,8192]{1,0:T(8,128)}, u32[]{:S(2)}, u32[]{:S(2)}) collective-permute-start(s32[8,8192]{1,0:T(8,128)S(1)} %collective-permute-done.2.refs_9_), channel_id=1, source_target_pairs={{0,1},{1,0},{2,3},{3,2},{4,5},{5,4},{6,7},{7,6},{8,9},{9,8},{10,11... | collective-permute-start | bytes 786440 | tf_op jit(solution)/shard_map/ppermute | solution.py:252
  50.8 1.6 %collective-permute-start.16 = (s32[8,4096]{1,0:T(8,128)}, s32[8,4096]{1,0:T(8,128)S(1)}, u32[]{:S(2)}, u32[]{:S(2)}) collective-permute-start(s32[8,4096]{1,0:T(8,128)} %collective-permute-done.7.refs_14_), channel_id=1, source_target_pairs={{0,1},{1,0},{2,3},{3,2},{4,5},{5,4},{6,7},{7,6},{8,9},{9,8},{10,11... | collective-permute-start | bytes 393224 | tf_op jit(solution)/shard_map/ppermute | solution.py:252
  51.0 2.1 %collective-permute-start.15 = (s32[8,4096]{1,0:T(8,128)}, s32[8,4096]{1,0:T(8,128)}, u32[]{:S(2)}, u32[]{:S(2)}) collective-permute-start(s32[8,4096]{1,0:T(8,128)} %collective-permute-done.6.refs_13_), channel_id=1, source_target_pairs={{0,1},{1,0},{2,3},{3,2},{4,5},{5,4},{6,7},{7,6},{8,9},{9,8},{10,11... | collective-permute-start | bytes 393224 | tf_op jit(solution)/shard_map/ppermute | solution.py:252
  78.8 5.0 %collective-permute-start.17 = (f32[16,1024]{1,0:T(8,128)S(1)}, f32[16,1024]{1,0:T(8,128)S(1)}, u32[]{:S(2)}, u32[]{:S(2)}) collective-permute-start(f32[16,1024]{1,0:T(8,128)S(1)} %get-tuple-element.8), channel_id=1, source_target_pairs={{1,0},{2,1},{3,2},{4,3},{5,4},{6,5},{7,6},{8,7},{9,8},{10,9},{11,1... | collective-permute-start | bytes 196616 | tf_op jit(solution)/shard_map/ppermute | solution.py:312
  81.8 6.5 %collective-permute-start.18 = (f32[16,1024]{1,0:T(8,128)S(1)}, f32[16,1024]{1,0:T(8,128)S(1)}, u32[]{:S(2)}, u32[]{:S(2)}) collective-permute-start(f32[16,1024]{1,0:T(8,128)S(1)} %get-tuple-element.9), channel_id=1, source_target_pairs={{0,1},{1,2},{2,3},{3,4},{4,5},{5,6},{6,7},{7,8},{8,9},{9,10},{10,1... | collective-permute-start | bytes 196616 | tf_op jit(solution)/shard_map/ppermute | solution.py:311
  (9 other events, 45.9 us)

commit v2 on v1

--- a/solution.py
+++ b/solution.py
@@ -45,73 +45,50 @@
     return square * square * (real * (bound / CODE**5))
 
 
-def pack_field_kernel(field_ref, out_ref):
+def prepare_kernel(block_ref, field_ref, neighbours_ref, weights_ref, field_out, geometry_out, packed):
+    tiles, slots = block_ref.shape
     half = field_ref.shape[0] // 2
-    high = encode(field_ref[:half], FIELD_BOUND)
-    low = encode(field_ref[half:], FIELD_BOUND)
-    out_ref[...] = pack(high, low)
-
-
-def pack_field(field):
-    levels, cells = field.shape
-    step = 2048
-    return pl.pallas_call(
-        pack_field_kernel,
-        grid=(cells // step,),
-        in_specs=[pl.BlockSpec((levels, step), lambda i: (0, i))],
-        out_specs=pl.BlockSpec((levels // 2, step), lambda i: (0, i)),
-        out_shape=jax.ShapeDtypeStruct((levels // 2, cells), jnp.int32),
-    )(field)
-
-
-def pack_geometry_kernel(neighbours_ref, weights_ref, out_ref):
-    step = out_ref.shape[1]
-    column = lax.broadcasted_iota(jnp.int32, (1, step), 1) + pl.program_id(0) * step
-    start = (column >> 7) << 7
-    relative = neighbours_ref[...] - start
-    for k in range(K):
-        east = encode(weights_ref[k, 0:1, :], WEIGHT_BOUND)
-        north = encode(weights_ref[k, 1:2, :], WEIGHT_BOUND)
-        out_ref[k : k + 1, :] = pack(east, north)
-    for k in range(K // 2):
-        out_ref[K + k : K + k + 1, :] = pack(relative[k : k + 1], relative[k + 3 : k + 4])
-
-
-def pack_geometry(neighbours, slope_weights):
-    cells = neighbours.shape[1]
-    step = 2048
-    return pl.pallas_call(
-        pack_geometry_kernel,
-        grid=(cells // step,),
-        in_specs=[
-            pl.BlockSpec((K, step), lambda i: (0, i)),
-            pl.BlockSpec((K, 2, step), lambda i: (0, 0, i)),
-        ],
-        out_specs=pl.BlockSpec((16, step), lambda i: (0, i)),
-        out_shape=jax.ShapeDtypeStruct((16, cells), jnp.int32),
-    )(neighbours, jnp.transpose(slope_weights, (1, 0, 2)))
-
-
-def choose_geometry_kernel(block_ref, packed_ref, out_ref):
-    tiles, slots = block_ref.shape
+    cells = neighbours_ref.shape[1]
+    step = 1024
+
+    def piece(i, carry):
+        lanes = pl.ds(pl.multiple_of(i * step, step), step)
+        high = encode(field_ref[:half, lanes], FIELD_BOUND)
+        low = encode(field_ref[half:, lanes], FIELD_BOUND)
+        field_out[:, lanes] = pack(high, low)
+        column = lax.broadcasted_iota(jnp.int32, (1, step), 1) + i * step
+        start = (column >> 7) << 7
+        relative = neighbours_ref[:, lanes] - start
+        east = encode(weights_ref[:, 0, lanes], WEIGHT_BOUND)
+        north = encode(weights_ref[:, 1, lanes], WEIGHT_BOUND)
+        packed[:K, lanes] = pack(east, north)
+        packed[K:ROWS, lanes] = pack(relative[: K // 2], relative[K // 2 :])
+        return carry
+
+    lax.fori_loop(0, cells // step, piece, 0)
 
     def tile(t, carry):
         for s in range(slots):
             lanes = pl.ds(pl.multiple_of(block_ref[t, s] * BLK, BLK), BLK)
-            out_ref[t, s * ROWS : (s + 1) * ROWS, :] = packed_ref[:ROWS, lanes]
+            geometry_out[t, s * ROWS : (s + 1) * ROWS, :] = packed[:ROWS, lanes]
         return carry
 
     lax.fori_loop(0, tiles, tile, 0)
 
 
-def choose_geometry(blocks, packed):
+def prepare(blocks, field, neighbours, slope_weights):
     tiles, slots = blocks.shape
+    levels, cells = field.shape
     return pl.pallas_call(
-        choose_geometry_kernel,
-        in_specs=[SMEM, VMEM],
-        out_specs=VMEM,
-        out_shape=jax.ShapeDtypeStruct((tiles, slots * ROWS, BLK), jnp.int32),
-    )(blocks, packed)
+        prepare_kernel,
+        in_specs=[SMEM, VMEM, VMEM, VMEM],
+        out_specs=(VMEM, VMEM),
+        out_shape=(
+            jax.ShapeDtypeStruct((levels // 2, cells), jnp.int32),
+            jax.ShapeDtypeStruct((tiles, slots * ROWS, BLK), jnp.int32),
+        ),
+        scratch_shapes=[pltpu.VMEM((16, cells), jnp.int32)],
+    )(blocks, field, neighbours, jnp.transpose(slope_weights, (1, 0, 2)))
 
 
 def ranks(present):
@@ -153,17 +130,21 @@
     return [jnp.concatenate(part, axis=0).astype(jnp.bfloat16) for part in (own, east, north)]
 
 
-def remap_kernel(parts, chunk, slots, *refs):
-    me_ref, block_ref, slot_ref, dest_ref, geometry_ref, weights_ref = refs[:6]
-    shards = refs[6 : 6 + len(parts)]
-    out_ref, edge_ref = refs[6 + len(parts) : 8 + len(parts)]
-    field, moments, weights, total, field_sem, weight_sem = refs[8 + len(parts) :]
+def remap_kernel(parts, chunk, slots, shares, *refs):
+    me_ref, block_ref, slot_ref, dest_ref = refs[:4]
+    geometry_refs = refs[4 : 4 + shares]
+    refs = refs[4 + shares :]
+    weights_ref, refs = refs[0], refs[1:]
+    shards = refs[: len(parts)]
+    out_ref, top_ref, bottom_ref = refs[len(parts) : 3 + len(parts)]
+    field, moments, weights, total, field_sem, weight_sem = refs[3 + len(parts) :]
     partitions = block_ref.shape[0]
     cells = NB * BLK
     blocks = partitions * NB
     pairs = slot_ref.shape[0]
     chunks = pairs // chunk
     me = me_ref[0]
+    share = slots // shares
 
     copies = []
     for (code, start, size), shard in zip(parts, shards):
@@ -181,21 +162,24 @@
         return pltpu.make_async_copy(weights_ref.at[piece], weights.at[piece], weight_sem.at[c])
 
     for c in range(chunks):
-        weight_copy(c).start()
+        weight_copy(c).start(priority=1)
     total[...] = jnp.zeros_like(total)
     for copy in copies:
         copy.wait()
 
     def source(q, carry):
-        for s in range(slots):
+        for j in range(slots):
+            part = j // share
+            s = (part ^ me_ref[1]) * share + j % share
             block = q * NB + block_ref[q, s]
             window = []
             for shift in (-1, 0, 1):
                 near = lax.rem(block + (shift + blocks), blocks)
                 window.append(field[:, pl.ds(pl.multiple_of(near * BLK, BLK), BLK)])
-            words = geometry_ref[q, s * ROWS : (s + 1) * ROWS, :]
-            for m, part in enumerate(slopes_and_moments(window, words)):
-                moments[q * slots + s, :, m * BLK : (m + 1) * BLK] = part
+            row = j % share * ROWS
+            words = geometry_refs[part][q, row : row + ROWS, :]
+            for m, moment in enumerate(slopes_and_moments(window, words)):
+                moments[q * slots + s, :, m * BLK : (m + 1) * BLK] = moment
         return carry
 
     lax.fori_loop(0, partitions, source, 0)
@@ -215,8 +199,8 @@
     for o in range(LONB):
         lanes = slice(o * BLK, (o + 1) * BLK)
         out_ref[:, :, lanes] = total[o].reshape(levels, LAT_DEV, BLK)
-        edge_ref[0, :, lanes] = total[o, pl.ds(0, levels, stride=LAT_DEV), :]
-        edge_ref[1, :, lanes] = total[o, pl.ds(LAT_DEV - 1, levels, stride=LAT_DEV), :]
+        top_ref[:, lanes] = total[o, pl.ds(0, levels, stride=LAT_DEV), :]
+        bottom_ref[:, lanes] = total[o, pl.ds(LAT_DEV - 1, levels, stride=LAT_DEV), :]
 
 
 def remap(me, blocks, slot, dest, geometry, weights, parts, shards, levels):
@@ -224,12 +208,13 @@
     pairs = slot.shape[0]
     chunk = 16
     return pl.pallas_call(
-        functools.partial(remap_kernel, parts, chunk, slots),
-        in_specs=[SMEM] * 4 + [VMEM, ANY] + [ANY] * len(shards),
-        out_specs=(VMEM, VMEM),
+        functools.partial(remap_kernel, parts, chunk, slots, len(geometry)),
+        in_specs=[SMEM] * 4 + [VMEM] * len(geometry) + [ANY] + [ANY] * len(shards),
+        out_specs=(VMEM, VMEM, VMEM),
         out_shape=(
             jax.ShapeDtypeStruct((levels, LAT_DEV, LONB * BLK), jnp.float32),
-            jax.ShapeDtypeStruct((2, levels, LONB * BLK), jnp.float32),
+            jax.ShapeDtypeStruct((levels, LONB * BLK), jnp.float32),
+            jax.ShapeDtypeStruct((levels, LONB * BLK), jnp.float32),
         ),
         scratch_shapes=[
             pltpu.VMEM((levels // 2, partitions * NB * BLK), jnp.int32),
@@ -240,27 +225,26 @@
             pltpu.SemaphoreType.DMA((pairs // chunk,)),
         ],
         compiler_params=pltpu.CompilerParams(vmem_limit_bytes=56 * 1024 * 1024),
-    )(me, blocks, slot, dest, geometry, weights, *shards)
-
-
-def share_field(packed, count):
+    )(me, blocks, slot, dest, *geometry, weights, *shards)
+
+
+def share_field(packed, count, beside):
     if count != 16:
         whole = lax.all_gather(packed, "src", axis=1, tiled=True)
-        return [(None, 0, whole.shape[1])], [whole]
+        return [(None, 0, whole.shape[1])], [whole], beside
 
     def swap(array, code):
         return lax.ppermute(array, "src", [(i, i ^ code) for i in range(count)])
 
-    cells = packed.shape[1]
-    half = cells // 2
     far = swap(packed, 8)
     z = swap(packed, 4)
     y = swap(packed, 2)
-    diagonal = swap(z, 2)
+    far, z, y = lax.optimization_barrier((far, z, y))
     far_z = swap(far, 4)
     far_y = swap(far, 2)
-    far_low = swap(far_z[:, :half], 2)
-    far_high = swap(far_y[:, half:], 4)
+    diagonal = swap(z, 2)
+    far_z, far_y, beside = lax.optimization_barrier((far_z, far_y, beside))
+    far_diagonal = swap(far_z, 2)
     held = [
         (0, 0, packed),
         (2, 0, y),
@@ -269,12 +253,11 @@
         (8, 0, far),
         (12, 0, far_z),
         (10, 0, far_y),
-        (14, 0, far_low),
-        (14, half, far_high),
+        (14, 0, far_diagonal),
     ]
     held = held + [(code ^ 1, start, swap(array, 1)) for code, start, array in held]
     parts = [(code, start, array.shape[1]) for code, start, array in held]
-    return parts, [array for _, _, array in held]
+    return parts, [array for _, _, array in held], beside
 
 
 def local(source_field, neighbours, slope_weights, pair_block, pair_dest, remap_weights):
@@ -285,14 +268,20 @@
     slots = max(1, pair_total // partitions // 2)
     ids = jnp.arange(NB, dtype=jnp.int32)
 
-    packed = pack_field(source_field)
-    parts, shards = share_field(packed, partitions)
-
     own_names = own_index * NB + ids
+    group = lax.axis_index("groups")
+    shares = lax.axis_size("groups") if lax.axis_size("groups") == 2 else 1
     asked = jnp.any(pair_block[:, :, None] == own_names[None, None, :], axis=1)
     outgoing_blocks = blocks_of_slots(asked, ranks(asked), slots)
-    geometry = choose_geometry(outgoing_blocks, pack_geometry(neighbours, slope_weights))
-    geometry = lax.all_to_all(geometry, "src", split_axis=0, concat_axis=0, tiled=True)
+    share = slots // shares
+    if shares == 2:
+        outgoing_blocks = lax.dynamic_slice_in_dim(outgoing_blocks, group * share, share, 1)
+    packed, geometry = prepare(outgoing_blocks, source_field, neighbours, slope_weights)
+    geometry = [lax.all_to_all(geometry, "src", split_axis=0, concat_axis=0, tiled=True)]
+    first = jnp.zeros((), jnp.int32)
+    if shares == 2:
+        geometry.append(lax.ppermute(geometry[0], "groups", [(0, 1), (1, 0)]))
+        first = group
 
     row = lax.dynamic_index_in_dim(pair_block, own_index, 0, keepdims=False)
     names = jnp.arange(partitions * NB, dtype=jnp.int32)
@@ -303,13 +292,14 @@
     slot_of_name = (jnp.arange(partitions, dtype=jnp.int32)[:, None] * slots + rank).reshape(-1)
     slot = jnp.sum(jnp.where(same, slot_of_name[None, :], 0), axis=1)
 
-    remapped, edges = remap(
-        own_index.reshape(1), blocks, slot, pair_dest[0], geometry, remap_weights, parts, shards, levels
+    parts, shards, (slot, blocks) = share_field(packed, partitions, (slot, blocks))
+    remapped, top, bottom = remap(
+        jnp.stack([own_index, first]), blocks, slot, pair_dest[0], geometry, remap_weights, parts, shards, levels
     )
     up = [(i, i + 1) for i in range(partitions - 1)]
     down = [(i + 1, i) for i in range(partitions - 1)]
-    below = lax.ppermute(edges[1], "src", up)
-    above = lax.ppermute(edges[0], "src", down)
+    below = lax.ppermute(bottom, "src", up)
+    above = lax.ppermute(top, "src", down)
     padded = jnp.concatenate([below[:, None], remapped, above[:, None]], axis=1)
     meridional = 0.5 * (padded[:, 2:] - padded[:, :-2])
     return remapped, meridional

time: 91.4 us -> 77.7 us (0.85)
  Pallas kernels: 32.9 us -> 20.1 us
  starting transfers between devices: 19.7 us -> 23.7 us
  waiting for transfers between devices: 25.7 us -> 22.8 us
  local copies, waits for them, and re-layouts: 4.69 us -> 2.31 us
    pallas_call x4 -> x2, Pallas kernels: 32.9 us -> 20.1 us  [the longest x1 17.1 us: remap(): pl.pallas_call(functools.partial(remap_kernel, parts, chunk, slots, len(g...]
    ppermute x17 -> x15, starting transfers between devices: 8.35 us -> 12.8 us  [swap(): return lax.ppermute(array, 'src', [(i, i ^ code) for i in range(count)])]
    ppermute x17 -> x15, waiting for transfers between devices: 21.2 us -> 18.6 us  [swap(): return lax.ppermute(array, 'src', [(i, i ^ code) for i in range(count)])]
    slice x2 -> x0, local copies, waits for them, and re-layouts: 1.41 us -> none  [the longest x1 0.75 us: share_field(): far_high = swap(far_y[:, half:], 4)]
    ppermute x2 -> x3, waiting for transfers between devices: 4.47 us -> 4.2 us  [the longest x1 4.19 us: local(): below = lax.ppermute(bottom, 'src', up)]
    ppermute x2 -> x3, starting transfers between devices: 4.94 us -> 4.93 us  [the longest x1 2.41 us: local(): below = lax.ppermute(bottom, 'src', up)]
  transfers between devices with their start and end apart: 20 -> 19, of which waited for: 8 -> 7; matrix products, arithmetic and copies ran while one was open for 8% -> 3% of each run, Pallas kernels for 6% -> 0%
where the time goes in v2:
time: 77.7 us; the launch traced here: 76.7 us
  starting transfers between devices  23.7 us (31%)
  waiting for transfers between devices  22.8 us (29%)
  Pallas kernels  20.1 us (26%)
  other arithmetic  6.76 us (9%)
  local copies, waits for them, and re-layouts  2.31 us (3%)
  between operations  0.94 us (1%)
    ppermute x15, waiting for transfers between devices, swap(): return lax.ppermute(array, 'src', [(i, i ^ code) for i in range(count)])  18.6 us
    pallas_call x1, Pallas kernels, remap(): pl.pallas_call(functools.partial(remap_kernel, parts, chunk, slots, len(g...  17.1 us
    ppermute x15, starting transfers between devices, swap(): return lax.ppermute(array, 'src', [(i, i ^ code) for i in range(count)])  12.8 us
    all_to_all x1, starting transfers between devices, local(): lax.all_to_all(geometry, 'src', split_axis=0, concat_axis=0, tiled=True)  5.97 us
    ppermute x1, waiting for transfers between devices, local(): below = lax.ppermute(bottom, 'src', up)  4.19 us
    pallas_call x1, Pallas kernels, prepare(): pl.pallas_call(prepare_kernel, in_specs=[SMEM, VMEM, VMEM, VMEM], out_spe...  3.01 us
    ppermute x1, starting transfers between devices, local(): below = lax.ppermute(bottom, 'src', up)  2.41 us
    mul x1, other arithmetic, local(): meridional = 0.5 * (padded[:, 2:] - padded[:, :-2])  2.22 us
  transfers between devices with their start and end apart: 19, of which 7 were waited for; matrix products, arithmetic and copies ran while one was open for 3% of the time, Pallas kernels for 0%

profile of v2, /device:TPU:18, one launch (start us, length us, event | category | flops | bytes accessed | tf_op | source)
XLA Modules:
  0.0 76.7 jit_solution(4104297046171849735)
XLA Ops:
  0.7 0.7 constant_dynamic-slice_fusion
  1.7 1.1 %compare_reduce_fusion = pred[16,64]{1,0:T(8,128)(4,1)S(1)} fusion(s32[16,256]{1,0:T(8,128)} %param.9, s32[64]{0:T(128)S(1)} %iota_add_fusion), kind=kLoop, calls=%fused_computation.3 | loop fusion | flops 523264 | bytes 17664 | tf_op jit(solution)/shard_map/reduce_or | solution.py:274
  3.5 0.7 constant_dynamic-slice_fusion.1.block_ref
  4.2 3.0 %shard_map.77 = (s32[8,8192]{1,0:T(8,128)}, s32[16,36,128]{2,1,0:T(8,128)}) custom-call(s32[16,4]{1,0:T(8,128)} %constant_dynamic-slice_fusion.1.block_ref, f32[16,8192]{1,0:T(8,128)} %field_ref.1, s32[6,8192]{1,0:T(8,128)} %neighbours_ref.1, f32[6,2,8192]{2,1,0:T(2,128)} %bitcast.7), custom_call_target="tpu_custom_call" | custom-call | tf_op jit(solution)/shard_map/pallas_call | solution.py:82
  7.2 1.5 %collective-permute-start.2 = (s32[8,8192]{1,0:T(8,128)}, s32[8,8192]{1,0:T(8,128)S(1)}, u32[]{:S(2)}, u32[]{:S(2)}) collective-permute-start(s32[8,8192]{1,0:T(8,128)} %get-tuple-element.14.refs_7_), channel_id=1, source_target_pairs={{0,2},{1,3},{2,0},{3,1},{4,6},{5,7},{6,4},{7,5},{8,10},{9,11},{10,... | collective-permute-start | bytes 786440 | tf_op jit(solution)/shard_map/ppermute | solution.py:237
  8.8 1.6 %collective-permute-start.1 = (s32[8,8192]{1,0:T(8,128)}, s32[8,8192]{1,0:T(8,128)S(1)}, u32[]{:S(2)}, u32[]{:S(2)}) collective-permute-start(s32[8,8192]{1,0:T(8,128)} %get-tuple-element.14.refs_7_), channel_id=1, source_target_pairs={{0,4},{1,5},{2,6},{3,7},{4,0},{5,1},{6,2},{7,3},{8,12},{9,13},{10,... | collective-permute-start | bytes 786440 | tf_op jit(solution)/shard_map/ppermute | solution.py:237
  10.7 6.0 %all-to-all-start = ((s32[16,36,128]{2,1,0:T(8,128)}), s32[16,36,128]{2,1,0:T(8,128)S(1)}, u32[]{:S(2)}, u32[]{:S(2)}) async-start(s32[16,36,128]{2,1,0:T(8,128)} %get-tuple-element.18), calls=%async_computation | async-start | bytes 655360 | tf_op jit(solution)/shard_map/all_to_all | solution.py:280
  16.7 4.7 %collective-permute-done.1.refs_9_ = s32[8,8192]{1,0:T(8,128)S(1)} collective-permute-done((s32[8,8192]{1,0:T(8,128)}, s32[8,8192]{1,0:T(8,128)S(1)}, u32[]{:S(2)}, u32[]{:S(2)}) %collective-permute-start.1) | collective-permute-done | bytes 262176 | tf_op jit(solution)/shard_map/ppermute | solution.py:237
  21.4 2.3 %collective-permute-done.refs_11_ = s32[8,8192]{1,0:T(8,128)S(1)} collective-permute-done((s32[8,8192]{1,0:T(8,128)}, s32[8,8192]{1,0:T(8,128)S(1)}, u32[]{:S(2)}, u32[]{:S(2)}) %collective-permute-start) | collective-permute-done | bytes 262176 | tf_op jit(solution)/shard_map/ppermute | solution.py:237
  24.3 5.8 %collective-permute-start.3 = (s32[8,8192]{1,0:T(8,128)S(1)}, s32[8,8192]{1,0:T(8,128)S(1)}, u32[]{:S(2)}, u32[]{:S(2)}) collective-permute-start(s32[8,8192]{1,0:T(8,128)S(1)} %collective-permute-done.refs_11_), channel_id=1, source_target_pairs={{0,4},{1,5},{2,6},{3,7},{4,0},{5,1},{6,2},{7,3},{8,12},{9,13},{10,... | collective-permute-start | bytes 786440 | tf_op jit(solution)/shard_map/ppermute | solution.py:237
  30.2 0.9 %select_reduce_fusion.refs_2_ = s32[256]{0:T(256)} fusion(s32[1024]{0:T(1024)S(1)} %add.38, s32[256]{0:T(256)S(1)} %bitcast.11), kind=kLoop, calls=%fused_computation | loop fusion | flops 786176 | bytes 6144 | tf_op jit(solution)/shard_map/reduce_sum | solution.py:293
  31.0 0.9 %select_reduce_fusion.1.refs_1_ = s32[16,8]{1,0:T(8,128)} fusion(s32[16,64]{1,0:T(8,128)S(1)} %get-tuple-element.26, pred[16,64]{1,0:T(8,128)(4,1)S(1)} %and.51), kind=kLoop, calls=%fused_computation.10 | loop fusion | flops 32640 | bytes 5632 | tf_op jit(solution)/shard_map/reduce_sum | solution.py:104
  32.5 1.0 %collective-permute-start.6 = (s32[8,8192]{1,0:T(8,128)S(1)}, s32[8,8192]{1,0:T(8,128)S(1)}, u32[]{:S(2)}, u32[]{:S(2)}) collective-permute-start(s32[8,8192]{1,0:T(8,128)S(1)} %collective-permute-done.1.refs_9_), channel_id=1, source_target_pairs={{0,2},{1,3},{2,0},{3,1},{4,6},{5,7},{6,4},{7,5},{8,10},{9,11},{10,... | collective-permute-start | bytes 786440 | tf_op jit(solution)/shard_map/ppermute | solution.py:237
  33.5 0.9 %collective-permute-done.3.refs_12_ = s32[8,8192]{1,0:T(8,128)S(1)} collective-permute-done((s32[8,8192]{1,0:T(8,128)S(1)}, s32[8,8192]{1,0:T(8,128)S(1)}, u32[]{:S(2)}, u32[]{:S(2)}) %collective-permute-start.3) | collective-permute-done | bytes 262176 | tf_op jit(solution)/shard_map/ppermute | solution.py:237
  34.4 1.1 %collective-permute-start.7 = (s32[8,8192]{1,0:T(8,128)S(1)}, s32[8,8192]{1,0:T(8,128)S(1)}, u32[]{:S(2)}, u32[]{:S(2)}) collective-permute-start(s32[8,8192]{1,0:T(8,128)S(1)} %collective-permute-done.3.refs_12_), channel_id=1, source_target_pairs={{0,2},{1,3},{2,0},{3,1},{4,6},{5,7},{6,4},{7,5},{8,10},{9,11},{10,... | collective-permute-start | bytes 786440 | tf_op jit(solution)/shard_map/ppermute | solution.py:237
  35.5 0.6 collective-permute-start.5
  36.1 5.5 %collective-permute-done.6.refs_10_ = s32[8,8192]{1,0:T(8,128)S(1)} collective-permute-done((s32[8,8192]{1,0:T(8,128)S(1)}, s32[8,8192]{1,0:T(8,128)S(1)}, u32[]{:S(2)}, u32[]{:S(2)}) %collective-permute-start.6) | collective-permute-done | bytes 262176 | tf_op jit(solution)/shard_map/ppermute | solution.py:237
  42.2 4.2 %collective-permute-done.7.refs_14_ = s32[8,8192]{1,0:T(8,128)S(1)} collective-permute-done((s32[8,8192]{1,0:T(8,128)S(1)}, s32[8,8192]{1,0:T(8,128)S(1)}, u32[]{:S(2)}, u32[]{:S(2)}) %collective-permute-start.7) | collective-permute-done | bytes 262176 | tf_op jit(solution)/shard_map/ppermute | solution.py:237
  47.0 0.9 %collective-permute-done.15.refs_22_ = s32[8,8192]{1,0:T(8,128)S(1)} collective-permute-done((s32[8,8192]{1,0:T(8,128)S(1)}, s32[8,8192]{1,0:T(8,128)S(1)}, u32[]{:S(2)}, u32[]{:S(2)}) %collective-permute-start.15) | collective-permute-done | bytes 262176 | tf_op jit(solution)/shard_map/ppermute | solution.py:237
  48.6 17.1 %shard_map.78 = (f32[16,8,1024]{2,1,0:T(8,128)}, f32[16,1024]{1,0:T(8,128)}, f32[16,1024]{1,0:T(8,128)}) custom-call(s32[2]{0:T(128)} %pad_add_fusion.refs_0_, s32[16,8]{1,0:T(8,128)} %select_reduce_fusion.1.refs_1_, s32[256]{0:T(256)} %select_reduce_fusion.refs_2_, s32[256]{0:T(256)} %bitcast.12, s32[16,36,128]{2,1,0:T(8,128)} %copy-done, ...), custom_call_target="tpu_custom_call" | custom-call | tf_op jit(solution)/shard_map/pallas_call | solution.py:210
  65.8 1.9 %collective-permute-start.16 = (f32[16,1024]{1,0:T(8,128)}, f32[16,1024]{1,0:T(8,128)S(1)}, u32[]{:S(2)}, u32[]{:S(2)}) collective-permute-start(f32[16,1024]{1,0:T(8,128)} %get-tuple-element.24), channel_id=1, source_target_pairs={{1,0},{2,1},{3,2},{4,3},{5,4},{6,5},{7,6},{8,7},{9,8},{10,9},{11,1... | collective-permute-start | bytes 196616 | tf_op jit(solution)/shard_map/ppermute | solution.py:302
  67.7 2.4 %collective-permute-start.17 = (f32[16,1024]{1,0:T(8,128)}, f32[16,1024]{1,0:T(8,128)S(1)}, u32[]{:S(2)}, u32[]{:S(2)}) collective-permute-start(f32[16,1024]{1,0:T(8,128)} %get-tuple-element.25), channel_id=1, source_target_pairs={{0,1},{1,2},{2,3},{3,4},{4,5},{5,6},{6,7},{7,8},{8,9},{9,10},{10,1... | collective-permute-start | bytes 196616 | tf_op jit(solution)/shard_map/ppermute | solution.py:301
  70.2 4.2 %collective-permute-done.17 = f32[16,1024]{1,0:T(8,128)S(1)} collective-permute-done((f32[16,1024]{1,0:T(8,128)}, f32[16,1024]{1,0:T(8,128)S(1)}, u32[]{:S(2)}, u32[]{:S(2)}) %collective-permute-start.17) | collective-permute-done | bytes 65568 | tf_op jit(solution)/shard_map/ppermute | solution.py:301
  74.5 2.2 %fusion.2 = f32[16,8,1024]{2,1,0:T(8,128)} fusion(f32[16,8,1024]{2,1,0:T(8,128)} %get-tuple-element.12, f32[16,1,1024]{2,1,0:T(1,128)S(1)} %copy.11, f32[16,1,1024]{2,1,0:T(1,128)S(1)} %copy.10), kind=kLoop, calls=%fused_computation.6 | loop fusion | flops 524288 | bytes 1179648 | tf_op jit(solution)/shard_map/mul | solution.py:304
  (68 shorter events, 4.4 us)
Async XLA Ops:
  7.2 9.4 %collective-permute-start.2 = (s32[8,8192]{1,0:T(8,128)}, s32[8,8192]{1,0:T(8,128)S(1)}, u32[]{:S(2)}, u32[]{:S(2)}) collective-permute-start(s32[8,8192]{1,0:T(8,128)} %get-tuple-element.14.refs_7_), channel_id=1, source_target_pairs={{0,2},{1,3},{2,0},{3,1},{4,6},{5,7},{6,4},{7,5},{8,10},{9,11},{10,... | collective-permute-start | bytes 786440 | tf_op jit(solution)/shard_map/ppermute | solution.py:237
  8.8 12.7 %collective-permute-start.1 = (s32[8,8192]{1,0:T(8,128)}, s32[8,8192]{1,0:T(8,128)S(1)}, u32[]{:S(2)}, u32[]{:S(2)}) collective-permute-start(s32[8,8192]{1,0:T(8,128)} %get-tuple-element.14.refs_7_), channel_id=1, source_target_pairs={{0,4},{1,5},{2,6},{3,7},{4,0},{5,1},{6,2},{7,3},{8,12},{9,13},{10,... | collective-permute-start | bytes 786440 | tf_op jit(solution)/shard_map/ppermute | solution.py:237
  10.3 13.4 %collective-permute-start = (s32[8,8192]{1,0:T(8,128)}, s32[8,8192]{1,0:T(8,128)S(1)}, u32[]{:S(2)}, u32[]{:S(2)}) collective-permute-start(s32[8,8192]{1,0:T(8,128)} %get-tuple-element.14.refs_7_), channel_id=1, source_target_pairs={{0,8},{1,9},{2,10},{3,11},{4,12},{5,13},{6,14},{7,15},{8,0},{9,1},... | collective-permute-start | bytes 786440 | tf_op jit(solution)/shard_map/ppermute | solution.py:237
  10.7 23.7 %collective-permute-start.8 = (s32[8,8192]{1,0:T(8,128)}, s32[8,8192]{1,0:T(8,128)S(1)}, u32[]{:S(2)}, u32[]{:S(2)}) collective-permute-start(s32[8,8192]{1,0:T(8,128)} %get-tuple-element.14.refs_7_), channel_id=1, source_target_pairs={{0,1},{1,0},{2,3},{3,2},{4,5},{5,4},{6,7},{7,6},{8,9},{9,8},{10,11... | collective-permute-start | bytes 786440 | tf_op jit(solution)/shard_map/ppermute | solution.py:237
  10.7 24.8 %all-to-all-start = ((s32[16,36,128]{2,1,0:T(8,128)}), s32[16,36,128]{2,1,0:T(8,128)S(1)}, u32[]{:S(2)}, u32[]{:S(2)}) async-start(s32[16,36,128]{2,1,0:T(8,128)} %get-tuple-element.18), calls=%async_computation | async-start | bytes 655360 | tf_op jit(solution)/shard_map/all_to_all | solution.py:280
  16.7 31.3 %copy-start.2 = (s32[8,8192]{1,0:T(8,128)}, s32[8,8192]{1,0:T(8,128)S(1)}, u32[]{:S(2)}) copy-start(s32[8,8192]{1,0:T(8,128)S(1)} %collective-permute-done.2.refs_8_) | copy-start | bytes 786436
  21.4 26.5 %copy-start.3 = (s32[8,8192]{1,0:T(8,128)}, s32[8,8192]{1,0:T(8,128)S(1)}, u32[]{:S(2)}) copy-start(s32[8,8192]{1,0:T(8,128)S(1)} %collective-permute-done.1.refs_9_) | copy-start | bytes 786436
  23.7 24.2 %copy-start.4 = (s32[8,8192]{1,0:T(8,128)}, s32[8,8192]{1,0:T(8,128)S(1)}, u32[]{:S(2)}) copy-start(s32[8,8192]{1,0:T(8,128)S(1)} %collective-permute-done.refs_11_) | copy-start | bytes 786436
  23.7 8.7 %collective-permute-start.4 = (s32[8,8192]{1,0:T(8,128)S(1)}, s32[8,8192]{1,0:T(8,128)S(1)}, u32[]{:S(2)}, u32[]{:S(2)}) collective-permute-start(s32[8,8192]{1,0:T(8,128)S(1)} %collective-permute-done.refs_11_), channel_id=1, source_target_pairs={{0,2},{1,3},{2,0},{3,1},{4,6},{5,7},{6,4},{7,5},{8,10},{9,11},{10,... | collective-permute-start | bytes 786440 | tf_op jit(solution)/shard_map/ppermute | solution.py:237
  24.3 10.1 %collective-permute-start.3 = (s32[8,8192]{1,0:T(8,128)S(1)}, s32[8,8192]{1,0:T(8,128)S(1)}, u32[]{:S(2)}, u32[]{:S(2)}) collective-permute-start(s32[8,8192]{1,0:T(8,128)S(1)} %collective-permute-done.refs_11_), channel_id=1, source_target_pairs={{0,4},{1,5},{2,6},{3,7},{4,0},{5,1},{6,2},{7,3},{8,12},{9,13},{10,... | collective-permute-start | bytes 786440 | tf_op jit(solution)/shard_map/ppermute | solution.py:237
  31.0 4.4 %collective-permute-start.9 = (s32[8,8192]{1,0:T(8,128)S(1)}, s32[8,8192]{1,0:T(8,128)S(1)}, u32[]{:S(2)}, u32[]{:S(2)}) collective-permute-start(s32[8,8192]{1,0:T(8,128)S(1)} %collective-permute-done.2.refs_8_), channel_id=1, source_target_pairs={{0,1},{1,0},{2,3},{3,2},{4,5},{5,4},{6,7},{7,6},{8,9},{9,8},{10,11... | collective-permute-start | bytes 786440 | tf_op jit(solution)/shard_map/ppermute | solution.py:237
  32.0 4.1 %collective-permute-start.10 = (s32[8,8192]{1,0:T(8,128)S(1)}, s32[8,8192]{1,0:T(8,128)S(1)}, u32[]{:S(2)}, u32[]{:S(2)}) collective-permute-start(s32[8,8192]{1,0:T(8,128)S(1)} %collective-permute-done.1.refs_9_), channel_id=1, source_target_pairs={{0,1},{1,0},{2,3},{3,2},{4,5},{5,4},{6,7},{7,6},{8,9},{9,8},{10,11... | collective-permute-start | bytes 786440 | tf_op jit(solution)/shard_map/ppermute | solution.py:237
  32.5 15.4 %copy-start.6 = (s32[8,8192]{1,0:T(8,128)}, s32[8,8192]{1,0:T(8,128)S(1)}, u32[]{:S(2)}) copy-start(s32[8,8192]{1,0:T(8,128)S(1)} %collective-permute-done.4.refs_13_) | copy-start | bytes 786436
  32.5 9.2 %collective-permute-start.6 = (s32[8,8192]{1,0:T(8,128)S(1)}, s32[8,8192]{1,0:T(8,128)S(1)}, u32[]{:S(2)}, u32[]{:S(2)}) collective-permute-start(s32[8,8192]{1,0:T(8,128)S(1)} %collective-permute-done.1.refs_9_), channel_id=1, source_target_pairs={{0,2},{1,3},{2,0},{3,1},{4,6},{5,7},{6,4},{7,5},{8,10},{9,11},{10,... | collective-permute-start | bytes 786440 | tf_op jit(solution)/shard_map/ppermute | solution.py:237
  34.4 13.6 %copy-start.7 = (s32[8,8192]{1,0:T(8,128)}, s32[8,8192]{1,0:T(8,128)S(1)}, u32[]{:S(2)}) copy-start(s32[8,8192]{1,0:T(8,128)S(1)} %collective-permute-done.3.refs_12_) | copy-start | bytes 786436
  34.4 7.3 %collective-permute-start.12 = (s32[8,8192]{1,0:T(8,128)S(1)}, s32[8,8192]{1,0:T(8,128)S(1)}, u32[]{:S(2)}, u32[]{:S(2)}) collective-permute-start(s32[8,8192]{1,0:T(8,128)S(1)} %collective-permute-done.refs_11_), channel_id=1, source_target_pairs={{0,1},{1,0},{2,3},{3,2},{4,5},{5,4},{6,7},{7,6},{8,9},{9,8},{10,11... | collective-permute-start | bytes 786440 | tf_op jit(solution)/shard_map/ppermute | solution.py:237
  34.4 12.0 %collective-permute-start.7 = (s32[8,8192]{1,0:T(8,128)S(1)}, s32[8,8192]{1,0:T(8,128)S(1)}, u32[]{:S(2)}, u32[]{:S(2)}) collective-permute-start(s32[8,8192]{1,0:T(8,128)S(1)} %collective-permute-done.3.refs_12_), channel_id=1, source_target_pairs={{0,2},{1,3},{2,0},{3,1},{4,6},{5,7},{6,4},{7,5},{8,10},{9,11},{10,... | collective-permute-start | bytes 786440 | tf_op jit(solution)/shard_map/ppermute | solution.py:237
  35.5 11.5 %collective-permute-start.5 = (s32[16,36,128]{2,1,0:T(8,128)S(1)}, s32[16,36,128]{2,1,0:T(8,128)S(1)}, u32[]{:S(2)}, u32[]{:S(2)}) collective-permute-start(s32[16,36,128]{2,1,0:T(8,128)S(1)} %all-to-all-done.refs_4_), channel_id=1, source_target_pairs={{0,16},{16,0},{1,17},{17,1},{2,18},{18,2},{3,19},{19,3},{4,20},{20... | collective-permute-start | bytes 884744 | tf_op jit(solution)/shard_map/ppermute | solution.py:283
  36.1 10.9 %collective-permute-start.14 = (s32[8,8192]{1,0:T(8,128)S(1)}, s32[8,8192]{1,0:T(8,128)S(1)}, u32[]{:S(2)}, u32[]{:S(2)}) collective-permute-start(s32[8,8192]{1,0:T(8,128)S(1)} %collective-permute-done.4.refs_13_), channel_id=1, source_target_pairs={{0,1},{1,0},{2,3},{3,2},{4,5},{5,4},{6,7},{7,6},{8,9},{9,8},{10,11... | collective-permute-start | bytes 786440 | tf_op jit(solution)/shard_map/ppermute | solution.py:237
  41.7 5.3 %collective-permute-start.11 = (s32[8,8192]{1,0:T(8,128)S(1)}, s32[8,8192]{1,0:T(8,128)S(1)}, u32[]{:S(2)}, u32[]{:S(2)}) collective-permute-start(s32[8,8192]{1,0:T(8,128)S(1)} %collective-permute-done.6.refs_10_), channel_id=1, source_target_pairs={{0,1},{1,0},{2,3},{3,2},{4,5},{5,4},{6,7},{7,6},{8,9},{9,8},{10,11... | collective-permute-start | bytes 786440 | tf_op jit(solution)/shard_map/ppermute | solution.py:237
  41.7 5.3 %collective-permute-start.13 = (s32[8,8192]{1,0:T(8,128)S(1)}, s32[8,8192]{1,0:T(8,128)S(1)}, u32[]{:S(2)}, u32[]{:S(2)}) collective-permute-start(s32[8,8192]{1,0:T(8,128)S(1)} %collective-permute-done.3.refs_12_), channel_id=1, source_target_pairs={{0,1},{1,0},{2,3},{3,2},{4,5},{5,4},{6,7},{7,6},{8,9},{9,8},{10,11... | collective-permute-start | bytes 786440 | tf_op jit(solution)/shard_map/ppermute | solution.py:237
  46.4 1.5 %collective-permute-start.15 = (s32[8,8192]{1,0:T(8,128)S(1)}, s32[8,8192]{1,0:T(8,128)S(1)}, u32[]{:S(2)}, u32[]{:S(2)}) collective-permute-start(s32[8,8192]{1,0:T(8,128)S(1)} %collective-permute-done.7.refs_14_), channel_id=1, source_target_pairs={{0,1},{1,0},{2,3},{3,2},{4,5},{5,4},{6,7},{7,6},{8,9},{9,8},{10,11... | collective-permute-start | bytes 786440 | tf_op jit(solution)/shard_map/ppermute | solution.py:237
  65.8 4.3 %collective-permute-start.16 = (f32[16,1024]{1,0:T(8,128)}, f32[16,1024]{1,0:T(8,128)S(1)}, u32[]{:S(2)}, u32[]{:S(2)}) collective-permute-start(f32[16,1024]{1,0:T(8,128)} %get-tuple-element.24), channel_id=1, source_target_pairs={{1,0},{2,1},{3,2},{4,3},{5,4},{6,5},{7,6},{8,7},{9,8},{10,9},{11,1... | collective-permute-start | bytes 196616 | tf_op jit(solution)/shard_map/ppermute | solution.py:302
  67.7 6.7 %collective-permute-start.17 = (f32[16,1024]{1,0:T(8,128)}, f32[16,1024]{1,0:T(8,128)S(1)}, u32[]{:S(2)}, u32[]{:S(2)}) collective-permute-start(f32[16,1024]{1,0:T(8,128)} %get-tuple-element.25), channel_id=1, source_target_pairs={{0,1},{1,2},{2,3},{3,4},{4,5},{5,6},{6,7},{7,8},{8,9},{9,10},{10,1... | collective-permute-start | bytes 196616 | tf_op jit(solution)/shard_map/ppermute | solution.py:301
  (12 other events, 69.6 us)

commit v3 on v2

v3 whole, which is shorter than its diff:
```python
import functools

import jax
import jax.numpy as jnp
from jax import lax
from jax.experimental import pallas as pl
from jax.experimental.pallas import tpu as pltpu
from jax.sharding import PartitionSpec as P

K = 6
BLK = 128
HALO = 128
NB = 64
LAT_DEV = 8
LONB = 8
CELLS = NB * BLK
ROWS = 9
CODE = 32767.0
FIELD_BOUND = 6.0
WEIGHT_BOUND = 2.0
VMEM = pl.BlockSpec(memory_space=pltpu.VMEM)
SMEM = pl.BlockSpec(memory_space=pltpu.SMEM)
ANY = pl.BlockSpec(memory_space=pl.ANY)


def encode(values, bound):
    scaled = jnp.abs(values) * (1.0 / bound)
    root = jnp.exp2(jnp.log2(jnp.maximum(scaled, 1e-30)) * 0.2)
    code = jnp.minimum(jnp.floor(root * CODE + 0.5), CODE)
    code = jnp.where(scaled > 1e-24, code, 0.0)
    return jnp.where(values < 0, -code, code).astype(jnp.int32)


def pack(high, low):
    return high * 65536 + (low + 32768)


def unpack(word):
    return word >> 16, (word & 65535) - 32768


def decode(code, bound):
    real = code.astype(jnp.float32)
    square = real * real
    return square * square * (real * (bound / CODE**5))


def pack_field_kernel(field_ref, out_ref):
    half = field_ref.shape[0] // 2
    step = 1024

    def piece(i, carry):
        lanes = pl.ds(pl.multiple_of(i * step, step), step)
        high = encode(field_ref[:half, lanes], FIELD_BOUND)
        low = encode(field_ref[half:, lanes], FIELD_BOUND)
        out_ref[:, lanes] = pack(high, low)
        return carry

    lax.fori_loop(0, field_ref.shape[1] // step, piece, 0)


def pack_field(field):
    levels, cells = field.shape
    return pl.pallas_call(
        pack_field_kernel,
        in_specs=[VMEM],
        out_specs=VMEM,
        out_shape=jax.ShapeDtypeStruct((levels // 2, cells), jnp.int32),
    )(field)


def geometry_kernel(block_ref, neighbours_ref, weights_ref, out_ref, packed):
    tiles, slots = block_ref.shape
    cells = neighbours_ref.shape[1]
    step = 1024

    def piece(i, carry):
        lanes = pl.ds(pl.multiple_of(i * step, step), step)
        column = lax.broadcasted_iota(jnp.int32, (1, step), 1) + i * step
        start = (column >> 7) << 7
        relative = neighbours_ref[:, lanes] - start
        east = encode(weights_ref[:, 0, lanes], WEIGHT_BOUND)
        north = encode(weights_ref[:, 1, lanes], WEIGHT_BOUND)
        packed[:K, lanes] = pack(east, north)
        packed[K:ROWS, lanes] = pack(relative[: K // 2], relative[K // 2 :])
        return carry

    lax.fori_loop(0, cells // step, piece, 0)

    def tile(t, carry):
        for s in range(slots):
            lanes = pl.ds(pl.multiple_of(block_ref[t, s] * BLK, BLK), BLK)
            out_ref[t, s * ROWS : (s + 1) * ROWS, :] = packed[:ROWS, lanes]
        return carry

    lax.fori_loop(0, tiles, tile, 0)


def choose_geometry(blocks, neighbours, slope_weights):
    tiles, slots = blocks.shape
    return pl.pallas_call(
        geometry_kernel,
        in_specs=[SMEM, VMEM, VMEM],
        out_specs=VMEM,
        out_shape=jax.ShapeDtypeStruct((tiles, slots * ROWS, BLK), jnp.int32),
        scratch_shapes=[pltpu.VMEM((16, neighbours.shape[1]), jnp.int32)],
        cost_estimate=pl.CostEstimate(flops=0, bytes_accessed=10_000_000, transcendentals=0),
    )(blocks, neighbours, jnp.transpose(slope_weights, (1, 0, 2)))


def ranks(present):
    ids = jnp.arange(NB, dtype=jnp.int32)
    before = (ids[:, None] < ids[None, :])[None]
    return jnp.sum((present[:, :, None] & before).astype(jnp.int32), axis=1)


def blocks_of_slots(present, rank, slots):
    ids = jnp.arange(NB, dtype=jnp.int32)
    wanted = jnp.arange(slots, dtype=jnp.int32)
    match = present[:, :, None] & (rank[:, :, None] == wanted[None, None, :])
    return jnp.sum(jnp.where(match, ids[None, :, None], 0), axis=1)


def slopes_and_moments(window, words):
    low_block, mid_block, high_block = window
    east_code, north_code = unpack(words[0:K])
    east_weight = decode(east_code, WEIGHT_BOUND)
    north_weight = decode(north_code, WEIGHT_BOUND)
    first, second = unpack(words[K : K + 3])
    own = [decode(code, FIELD_BOUND) for code in unpack(mid_block)]
    east = [jnp.zeros_like(own[0]) for _ in own]
    north = [jnp.zeros_like(own[0]) for _ in own]
    shape = mid_block.shape
    for k in range(K):
        row = first[k : k + 1] if k < 3 else second[k - 3 : k - 2]
        place = jnp.broadcast_to(row, shape)
        lane = place & (BLK - 1)
        picked = [
            jnp.take_along_axis(part, lane, axis=1, mode="promise_in_bounds")
            for part in (low_block, mid_block, high_block)
        ]
        word = jnp.where(place < BLK, picked[0], jnp.where(place < 2 * BLK, picked[1], picked[2]))
        for side, code in enumerate(unpack(word)):
            difference = decode(code, FIELD_BOUND) - own[side]
            east[side] = east[side] + east_weight[k : k + 1] * difference
            north[side] = north[side] + north_weight[k : k + 1] * difference
    return [jnp.concatenate(part, axis=0).astype(jnp.bfloat16) for part in (own, east, north)]


def remap_kernel(parts, shares, *refs):
    me_ref, block_ref, slot_ref, dest_ref, order_ref, *refs = refs
    geometry_refs, refs = refs[:shares], refs[shares:]
    weights_ref, *refs = refs
    shards, refs = refs[: len(parts)], refs[len(parts) :]
    out_ref, top_ref, bottom_ref, field, even, odd, weights, total, field_sem, weight_sem = refs
    partitions, slots = block_ref.shape
    blocks = partitions * NB
    chunk = slot_ref.shape[0] // partitions
    share = slots // shares
    ahead = partitions // 4
    me, first_share = me_ref[0], me_ref[1]

    copies = []
    for (code, start, size), shard in zip(parts, shards):
        if code is None:
            target = field
        else:
            lanes = pl.ds(pl.multiple_of((me ^ code) * CELLS + start, BLK), size)
            target = field.at[:, lanes]
        copies.append(pltpu.make_async_copy(shard, target, field_sem))
    for copy in copies:
        copy.start()

    def fetch(q):
        for i in range(chunk):
            e = q * chunk + i
            pltpu.make_async_copy(weights_ref.at[order_ref[e]], weights.at[e], weight_sem.at[q]).start(priority=1)

    def arrived(q):
        piece = pl.ds(q * chunk, chunk)
        pltpu.make_async_copy(weights_ref.at[pl.ds(0, chunk)], weights.at[piece], weight_sem.at[q]).wait()

    def fetch_one(q, carry):
        fetch(q)
        return carry

    lax.fori_loop(0, ahead, fetch_one, 0)
    total[...] = jnp.zeros_like(total)
    for copy in copies:
        copy.wait()

    def slot_moments(q, j, moments):
        part = j // share
        s = (part ^ first_share) * share + j % share
        block = q * NB + block_ref[q, s]
        window = []
        for shift in (-1, 0, 1):
            near = lax.rem(block + (shift + blocks), blocks)
            window.append(field[:, pl.ds(pl.multiple_of(near * BLK, BLK), BLK)])
        row = j % share * ROWS
        words = geometry_refs[part][q, row : row + ROWS, :]
        for m, moment in enumerate(slopes_and_moments(window, words)):
            moments[s, :, m * BLK : (m + 1) * BLK] = moment

    def pair_product(q, i, moments):
        e = q * chunk + i
        p = order_ref[e]
        product = jnp.dot(moments[slot_ref[p]], weights[e], preferred_element_type=jnp.float32)
        dest = dest_ref[p]
        rows = pl.ds(dest >> 3, 16, stride=LAT_DEV)
        total[dest & 7, rows, :] = total[dest & 7, rows, :] + product

    def step(q, here, there):
        later = jnp.minimum(q + 1, partitions - 1)

        @pl.when(q + ahead < partitions)
        def _():
            fetch(q + ahead)

        arrived(q)
        each = max(1, chunk // slots)
        for j in range(slots):
            slot_moments(later, j, there)
            for i in range(j * each, (j + 1) * each):
                pair_product(q, i, here)

    for j in range(slots):
        slot_moments(0, j, even)

    def two(h, carry):
        step(2 * h, even, odd)
        step(2 * h + 1, odd, even)
        return carry

    lax.fori_loop(0, partitions // 2, two, 0)
    levels = out_ref.shape[0]
    for o in range(LONB):
        lanes = slice(o * BLK, (o + 1) * BLK)
        out_ref[:, :, lanes] = total[o].reshape(levels, LAT_DEV, BLK)
        top_ref[:, lanes] = total[o, pl.ds(0, levels, stride=LAT_DEV), :]
        bottom_ref[:, lanes] = total[o, pl.ds(LAT_DEV - 1, levels, stride=LAT_DEV), :]


def remap(me, blocks, slot, dest, order, geometry, weights, parts, shards, levels):
    partitions, slots = blocks.shape
    total = (LONB, levels * LAT_DEV, BLK)
    edge = jax.ShapeDtypeStruct((levels, LONB * BLK), jnp.float32)
    return pl.pallas_call(
        functools.partial(remap_kernel, parts, len(geometry)),
        in_specs=[SMEM] * 5 + [VMEM] * len(geometry) + [ANY] + [ANY] * len(shards),
        out_specs=(VMEM, VMEM, VMEM),
        out_shape=(jax.ShapeDtypeStruct((levels, LAT_DEV, LONB * BLK), jnp.float32), edge, edge),
        scratch_shapes=[
            pltpu.VMEM((levels // 2, partitions * CELLS), jnp.int32),
            pltpu.VMEM((slots, levels, 3 * BLK), jnp.bfloat16),
            pltpu.VMEM((slots, levels, 3 * BLK), jnp.bfloat16),
            pltpu.VMEM(weights.shape, jnp.bfloat16),
            pltpu.VMEM(total, jnp.float32),
            pltpu.SemaphoreType.DMA,
            pltpu.SemaphoreType.DMA((partitions,)),
        ],
        compiler_params=pltpu.CompilerParams(vmem_limit_bytes=56 * 1024 * 1024),
    )(me, blocks, slot, dest, order, *geometry, weights, *shards)


def swap(array, code):
    return lax.ppermute(array, "src", [(i, i ^ code) for i in range(lax.axis_size("src"))])


def tie(*arrays):
    return lax.optimization_barrier(arrays)


def local(source_field, neighbours, slope_weights, pair_block, pair_dest, remap_weights):
    levels, cell_count = source_field.shape
    own_index = lax.axis_index("src")
    partitions = lax.axis_size("src")
    pair_total = pair_block.shape[1]
    slots = max(1, pair_total // partitions // 2)
    ids = jnp.arange(NB, dtype=jnp.int32)

    packed = pack_field(source_field)

    own_names = own_index * NB + ids
    asked = jnp.any(pair_block[:, :, None] == own_names[None, None, :], axis=1)
    outgoing_blocks = blocks_of_slots(asked, ranks(asked), slots)
    group = lax.axis_index("groups")
    shares = 2 if lax.axis_size("groups") == 2 else 1
    share = slots // shares
    if shares == 2:
        outgoing_blocks = lax.dynamic_slice_in_dim(outgoing_blocks, group * share, share, 1)
    chosen = choose_geometry(outgoing_blocks, neighbours, slope_weights)
    geometry = [lax.all_to_all(chosen, "src", split_axis=0, concat_axis=0, tiled=True)]
    first = jnp.zeros((), jnp.int32)
    if shares == 2:
        geometry.append(lax.ppermute(geometry[0], "groups", [(0, 1), (1, 0)]))
        first = group

    row = lax.dynamic_index_in_dim(pair_block, own_index, 0, keepdims=False)
    names = jnp.arange(partitions * NB, dtype=jnp.int32)
    same = row[:, None] == names[None, :]
    needed = jnp.any(same, axis=0).reshape(partitions, NB)
    rank = ranks(needed)
    blocks = blocks_of_slots(needed, rank, slots)
    slot = jnp.sum(jnp.where(same, rank.reshape(1, -1), 0), axis=1)
    pair_ids = jnp.arange(pair_total, dtype=jnp.int32)
    key = row // NB * pair_total + pair_ids
    place = jnp.sum((key[:, None] < key[None, :]).astype(jnp.int32), axis=0)
    order = jnp.sum(jnp.where(place[:, None] == pair_ids[None, :], pair_ids[:, None], 0), axis=0)

    if partitions == 16:
        far, z, y = swap(packed, 8), swap(packed, 4), swap(packed, 2)
        far, order, _ = tie(far, order, chosen)
        far_z, far_y = swap(far, 4), swap(far, 2)
        far_z, far_y, y, order, slot, blocks = tie(far_z, far_y, y, order, slot, blocks)
        far_diagonal, diagonal = swap(far_z, 2), swap(y, 4)
        held = [
            (0, packed),
            (2, y),
            (4, z),
            (6, diagonal),
            (8, far),
            (12, far_z),
            (10, far_y),
            (14, far_diagonal),
        ]
        held = held + [(code ^ 1, swap(array, 1)) for code, array in held]
        parts = [(code, 0, array.shape[1]) for code, array in held]
        shards = [array for _, array in held]
    else:
        whole = lax.all_gather(packed, "src", axis=1, tiled=True)
        parts, shards = [(None, 0, whole.shape[1])], [whole]

    me = jnp.stack([own_index, first])
    remapped, top, bottom = remap(
        me, blocks, slot, pair_dest[0], order, geometry, remap_weights, parts, shards, levels
    )
    up = [(i, i + 1) for i in range(partitions - 1)]
    down = [(i + 1, i) for i in range(partitions - 1)]
    below = lax.ppermute(bottom, "src", up)
    above = lax.ppermute(top, "src", down)
    padded = jnp.concatenate([below[:, None], remapped, above[:, None]], axis=1)
    meridional = 0.5 * (padded[:, 2:] - padded[:, :-2])
    return remapped, meridional


def solution(mesh):
    return jax.shard_map(
        local,
        mesh=mesh,
        in_specs=(
            P("groups", "src"),
            P(None, "src"),
            P(None, None, "src"),
            P(),
            P("src", None),
            P("src", None, None),
        ),
        out_specs=(P("groups", "src", None), P("groups", "src", None)),
        check_vma=False,
    )
```

time: 77.7 us -> 68.2 us (0.88)
  waiting for transfers between devices: 22.8 us -> 19.2 us
  Pallas kernels: 20.1 us -> 16.9 us
  starting transfers between devices: 23.7 us -> 20.6 us
  other arithmetic: 6.76 us -> 8.31 us
    ppermute x15, waiting for transfers between devices: 18.6 us -> 13.3 us  [swap(): lax.ppermute(array, 'src', [(i, i ^ code) for i in range(lax.axis_size('s...]
    pallas_call x2 -> x3, Pallas kernels: 20.1 us -> 16.9 us  [the longest x1 12.4 us: remap(): pl.pallas_call(functools.partial(remap_kernel, parts, len(geometry)), in_...]
    ppermute x15, starting transfers between devices: 12.8 us -> 9.68 us  [swap(): lax.ppermute(array, 'src', [(i, i ^ code) for i in range(lax.axis_size('s...]
    ppermute x1, waiting for transfers between devices: 0.01 us -> 1.7 us  [local(): geometry.append(lax.ppermute(geometry[0], 'groups', [(0, 1), (1, 0)]))]
    reduce_sum x1 -> x3, other arithmetic: 0.85 us -> 1.67 us  [the longest x1 0.85 us: local(): slot = jnp.sum(jnp.where(same, rank.reshape(1, -1), 0), axis=1)]
  transfers between devices with their start and end apart: 19 -> 19, of which waited for: 7 -> 6; matrix products, arithmetic and copies ran while one was open for 3% -> 10% of each run, Pallas kernels for 0% -> 4%
where the time goes in v3:
time: 68.2 us; the launch traced here: 67.6 us
  starting transfers between devices  20.6 us (30%)
  waiting for transfers between devices  19.2 us (28%)
  Pallas kernels  16.9 us (25%)
  other arithmetic  8.31 us (12%)
  local copies, waits for them, and re-layouts  1.76 us (3%)
  between operations  0.9 us (1%)
    ppermute x15, waiting for transfers between devices, swap(): lax.ppermute(array, 'src', [(i, i ^ code) for i in range(lax.axis_size('s...  13.3 us
    pallas_call x1, Pallas kernels, remap(): pl.pallas_call(functools.partial(remap_kernel, parts, len(geometry)), in_...  12.4 us
    ppermute x15, starting transfers between devices, swap(): lax.ppermute(array, 'src', [(i, i ^ code) for i in range(lax.axis_size('s...  9.68 us
    all_to_all x1, starting transfers between devices, local(): lax.all_to_all(chosen, 'src', split_axis=0, concat_axis=0, tiled=True)  5.97 us
    ppermute x1, waiting for transfers between devices, local(): below = lax.ppermute(bottom, 'src', up)  4.19 us
    pallas_call x1, Pallas kernels, choose_geometry(): pl.pallas_call(geometry_kernel, in_specs=[SMEM, VMEM, VMEM], out_specs=VM...  2.42 us
    ppermute x1, starting transfers between devices, local(): below = lax.ppermute(bottom, 'src', up)  2.41 us
    mul x1, other arithmetic, local(): meridional = 0.5 * (padded[:, 2:] - padded[:, :-2])  2.22 us
  transfers between devices with their start and end apart: 19, of which 6 were waited for; matrix products, arithmetic and copies ran while one was open for 10% of the time, Pallas kernels for 4%

profile of v3, /device:TPU:18, one launch (start us, length us, event | category | flops | bytes accessed | tf_op | source)
XLA Modules:
  0.0 67.6 jit_solution(14116495509116009992)
XLA Ops:
  0.6 2.2 %shard_map.77.refs_8_ = s32[8,8192]{1,0:T(8,128)} custom-call(f32[16,8192]{1,0:T(8,128)} %field_ref.1), custom_call_target="tpu_custom_call" | custom-call | tf_op jit(solution)/shard_map/pallas_call | solution.py:64
  2.8 1.6 %collective-permute-start.5 = (s32[8,8192]{1,0:T(8,128)}, s32[8,8192]{1,0:T(8,128)S(1)}, u32[]{:S(2)}, u32[]{:S(2)}) collective-permute-start(s32[8,8192]{1,0:T(8,128)} %shard_map.77.refs_8_), channel_id=1, source_target_pairs={{0,4},{1,5},{2,6},{3,7},{4,0},{5,1},{6,2},{7,3},{8,12},{9,13},{10,... | collective-permute-start | bytes 786440 | tf_op jit(solution)/shard_map/ppermute | solution.py:267
  4.4 1.5 %collective-permute-start.3 = (s32[8,8192]{1,0:T(8,128)}, s32[8,8192]{1,0:T(8,128)S(1)}, u32[]{:S(2)}, u32[]{:S(2)}) collective-permute-start(s32[8,8192]{1,0:T(8,128)} %shard_map.77.refs_8_), channel_id=1, source_target_pairs={{0,2},{1,3},{2,0},{3,1},{4,6},{5,7},{6,4},{7,5},{8,10},{9,11},{10,... | collective-permute-start | bytes 786440 | tf_op jit(solution)/shard_map/ppermute | solution.py:267
  6.2 1.1 %compare_reduce_fusion = pred[16,64]{1,0:T(8,128)(4,1)S(1)} fusion(s32[16,256]{1,0:T(8,128)} %param.9, s32[64]{0:T(128)S(1)} %iota_add_fusion.2), kind=kLoop, calls=%fused_computation.3 | loop fusion | flops 523264 | bytes 17664 | tf_op jit(solution)/shard_map/reduce_or | solution.py:285
  7.4 0.7 %iota_add_fusion = (s32[1,256]{1,0:T(1,128)S(1)}, s32[1,256]{1,0:T(1,128)S(1)}) fusion(s32[16,256]{1,0:T(8,128)} %param.9, s32[]{:T(128)S(6)} %select_n.34), kind=kLoop, calls=%fused_computation.28 | loop fusion | flops 4352 | bytes 3076 | tf_op jit(solution)/shard_map/add | solution.py:307
  9.1 0.7 %constant_dynamic-slice_fusion.block_ref = s32[16,4]{1,0:T(8,128)} fusion(s32[16,8]{1,0:T(8,128)S(1)} %select_reduce_fusion.3, s32[]{:T(128)S(6)} %select_n.39), kind=kLoop, calls=%fused_computation.32 | loop fusion | bytes 516 | tf_op jit(solution)/shard_map/dynamic_slice | solution.py:291
  9.8 2.4 %shard_map.78 = s32[16,36,128]{2,1,0:T(8,128)} custom-call(s32[16,4]{1,0:T(8,128)} %constant_dynamic-slice_fusion.block_ref, s32[6,8192]{1,0:T(8,128)} %neighbours_ref.1, f32[6,2,8192]{2,1,0:T(2,128)} %bitcast.8), custom_call_target="tpu_custom_call" | custom-call | bytes 10000000 | tf_op jit(solution)/shard_map/pallas_call | solution.py:101
  12.2 6.0 %all-to-all-start = ((s32[16,36,128]{2,1,0:T(8,128)}), s32[16,36,128]{2,1,0:T(8,128)S(1)}, u32[]{:S(2)}, u32[]{:S(2)}) async-start(s32[16,36,128]{2,1,0:T(8,128)} %shard_map.78), calls=%async_computation | async-start | bytes 655360 | tf_op jit(solution)/shard_map/all_to_all | solution.py:293
  18.3 0.7 %select_reduce_fusion.1.refs_4_ = s32[256]{0:T(256)} fusion(s32[256]{0:T(256)S(1)} %convert_reduce_fusion.2), kind=kLoop, calls=%fused_computation.10 | loop fusion | flops 196352 | bytes 2048 | tf_op jit(solution)/shard_map/reduce_sum | solution.py:309
  19.0 1.5 %collective-permute-start.2 = (s32[8,8192]{1,0:T(8,128)S(1)}, s32[8,8192]{1,0:T(8,128)S(1)}, u32[]{:S(2)}, u32[]{:S(2)}) collective-permute-start(s32[8,8192]{1,0:T(8,128)S(1)} %collective-permute-done.refs_12_), channel_id=1, source_target_pairs={{0,2},{1,3},{2,0},{3,1},{4,6},{5,7},{6,4},{7,5},{8,10},{9,11},{10,... | collective-permute-start | bytes 786440 | tf_op jit(solution)/shard_map/ppermute | solution.py:267
  20.5 1.5 %collective-permute-start.1 = (s32[8,8192]{1,0:T(8,128)S(1)}, s32[8,8192]{1,0:T(8,128)S(1)}, u32[]{:S(2)}, u32[]{:S(2)}) collective-permute-start(s32[8,8192]{1,0:T(8,128)S(1)} %collective-permute-done.refs_12_), channel_id=1, source_target_pairs={{0,4},{1,5},{2,6},{3,7},{4,0},{5,1},{6,2},{7,3},{8,12},{9,13},{10,... | collective-permute-start | bytes 786440 | tf_op jit(solution)/shard_map/ppermute | solution.py:267
  22.1 0.9 %select_reduce_fusion.refs_2_ = s32[256]{0:T(256)} fusion(s32[1024]{0:T(1024)S(1)} %broadcast_in_dim.77, s32[256]{0:T(256)S(1)} %bitcast.13), kind=kLoop, calls=%fused_computation | loop fusion | flops 786176 | bytes 6144 | tf_op jit(solution)/shard_map/reduce_sum | solution.py:305
  23.4 0.9 %select_reduce_fusion.2.refs_1_ = s32[16,8]{1,0:T(8,128)} fusion(s32[16,64]{1,0:T(8,128)S(1)} %get-tuple-element.24, pred[16,64]{1,0:T(8,128)(4,1)S(1)} %and.70), kind=kLoop, calls=%fused_computation.13 | loop fusion | flops 32640 | bytes 5632 | tf_op jit(solution)/shard_map/reduce_sum | solution.py:121
  24.4 5.6 %collective-permute-done.2.refs_14_ = s32[8,8192]{1,0:T(8,128)S(1)} collective-permute-done((s32[8,8192]{1,0:T(8,128)S(1)}, s32[8,8192]{1,0:T(8,128)S(1)}, u32[]{:S(2)}, u32[]{:S(2)}) %collective-permute-start.2) | collective-permute-done | bytes 262176 | tf_op jit(solution)/shard_map/ppermute | solution.py:267
  30.0 1.8 %collective-permute-done.1.refs_13_ = s32[8,8192]{1,0:T(8,128)S(1)} collective-permute-done((s32[8,8192]{1,0:T(8,128)S(1)}, s32[8,8192]{1,0:T(8,128)S(1)}, u32[]{:S(2)}, u32[]{:S(2)}) %collective-permute-start.1) | collective-permute-done | bytes 262176 | tf_op jit(solution)/shard_map/ppermute | solution.py:267
  32.3 1.5 %collective-permute-start.7 = (s32[8,8192]{1,0:T(8,128)S(1)}, s32[8,8192]{1,0:T(8,128)S(1)}, u32[]{:S(2)}, u32[]{:S(2)}) collective-permute-start(s32[8,8192]{1,0:T(8,128)S(1)} %collective-permute-done.1.refs_13_), channel_id=1, source_target_pairs={{0,2},{1,3},{2,0},{3,1},{4,6},{5,7},{6,4},{7,5},{8,10},{9,11},{10,... | collective-permute-start | bytes 786440 | tf_op jit(solution)/shard_map/ppermute | solution.py:267
  34.9 5.6 %collective-permute-done.6.refs_11_ = s32[8,8192]{1,0:T(8,128)S(1)} collective-permute-done((s32[8,8192]{1,0:T(8,128)S(1)}, s32[8,8192]{1,0:T(8,128)S(1)}, u32[]{:S(2)}, u32[]{:S(2)}) %collective-permute-start.6) | collective-permute-done | bytes 262176 | tf_op jit(solution)/shard_map/ppermute | solution.py:267
  41.1 0.7 pad_add_fusion.refs_0_
  41.7 1.7 %collective-permute-done.4.refs_6_ = s32[16,36,128]{2,1,0:T(8,128)S(1)} collective-permute-done((s32[16,36,128]{2,1,0:T(8,128)S(1)}, s32[16,36,128]{2,1,0:T(8,128)S(1)}, u32[]{:S(2)}, u32[]{:S(2)}) %collective-permute-start.4) | collective-permute-done | bytes 294944 | tf_op jit(solution)/shard_map/ppermute | solution.py:296
  44.3 12.4 %shard_map.79 = (f32[16,8,1024]{2,1,0:T(8,128)}, f32[16,1024]{1,0:T(8,128)}, f32[16,1024]{1,0:T(8,128)}) custom-call(s32[2]{0:T(128)} %pad_add_fusion.refs_0_, s32[16,8]{1,0:T(8,128)} %select_reduce_fusion.2.refs_1_, s32[256]{0:T(256)} %select_reduce_fusion.refs_2_, s32[256]{0:T(256)} %bitcast.15, s32[256]{0:T(256)} %select_reduce_fusion.1.refs_4_, ...), custom_call_target="tpu_custom_call" | custom-call | tf_op jit(solution)/shard_map/pallas_call | solution.py:248
  56.7 1.9 %collective-permute-start.16 = (f32[16,1024]{1,0:T(8,128)}, f32[16,1024]{1,0:T(8,128)S(1)}, u32[]{:S(2)}, u32[]{:S(2)}) collective-permute-start(f32[16,1024]{1,0:T(8,128)} %get-tuple-element.22), channel_id=1, source_target_pairs={{1,0},{2,1},{3,2},{4,3},{5,4},{6,5},{7,6},{8,7},{9,8},{10,9},{11,1... | collective-permute-start | bytes 196616 | tf_op jit(solution)/shard_map/ppermute | solution.py:341
  58.6 2.4 %collective-permute-start.17 = (f32[16,1024]{1,0:T(8,128)}, f32[16,1024]{1,0:T(8,128)S(1)}, u32[]{:S(2)}, u32[]{:S(2)}) collective-permute-start(f32[16,1024]{1,0:T(8,128)} %get-tuple-element.23), channel_id=1, source_target_pairs={{0,1},{1,2},{2,3},{3,4},{4,5},{5,6},{6,7},{7,8},{8,9},{9,10},{10,1... | collective-permute-start | bytes 196616 | tf_op jit(solution)/shard_map/ppermute | solution.py:340
  61.1 4.2 %collective-permute-done.17 = f32[16,1024]{1,0:T(8,128)S(1)} collective-permute-done((f32[16,1024]{1,0:T(8,128)}, f32[16,1024]{1,0:T(8,128)S(1)}, u32[]{:S(2)}, u32[]{:S(2)}) %collective-permute-start.17) | collective-permute-done | bytes 65568 | tf_op jit(solution)/shard_map/ppermute | solution.py:340
  65.4 2.2 %fusion.2 = f32[16,8,1024]{2,1,0:T(8,128)} fusion(f32[16,8,1024]{2,1,0:T(8,128)} %get-tuple-element.11, f32[16,1,1024]{2,1,0:T(1,128)S(1)} %copy.11, f32[16,1,1024]{2,1,0:T(1,128)S(1)} %copy.10), kind=kLoop, calls=%fused_computation.6 | loop fusion | flops 524288 | bytes 1179648 | tf_op jit(solution)/shard_map/mul | solution.py:343
  (70 shorter events, 5.1 us)
Async XLA Ops:
  2.8 20.1 %collective-permute-start.5 = (s32[8,8192]{1,0:T(8,128)}, s32[8,8192]{1,0:T(8,128)S(1)}, u32[]{:S(2)}, u32[]{:S(2)}) collective-permute-start(s32[8,8192]{1,0:T(8,128)} %shard_map.77.refs_8_), channel_id=1, source_target_pairs={{0,4},{1,5},{2,6},{3,7},{4,0},{5,1},{6,2},{7,3},{8,12},{9,13},{10,... | collective-permute-start | bytes 786440 | tf_op jit(solution)/shard_map/ppermute | solution.py:267
  4.4 20.0 %collective-permute-start.3 = (s32[8,8192]{1,0:T(8,128)}, s32[8,8192]{1,0:T(8,128)S(1)}, u32[]{:S(2)}, u32[]{:S(2)}) collective-permute-start(s32[8,8192]{1,0:T(8,128)} %shard_map.77.refs_8_), channel_id=1, source_target_pairs={{0,2},{1,3},{2,0},{3,1},{4,6},{5,7},{6,4},{7,5},{8,10},{9,11},{10,... | collective-permute-start | bytes 786440 | tf_op jit(solution)/shard_map/ppermute | solution.py:267
  5.9 13.1 %collective-permute-start = (s32[8,8192]{1,0:T(8,128)}, s32[8,8192]{1,0:T(8,128)S(1)}, u32[]{:S(2)}, u32[]{:S(2)}) collective-permute-start(s32[8,8192]{1,0:T(8,128)} %shard_map.77.refs_8_), channel_id=1, source_target_pairs={{0,8},{1,9},{2,10},{3,11},{4,12},{5,13},{6,14},{7,15},{8,0},{9,1},... | collective-permute-start | bytes 786440 | tf_op jit(solution)/shard_map/ppermute | solution.py:267
  12.2 21.6 %all-to-all-start = ((s32[16,36,128]{2,1,0:T(8,128)}), s32[16,36,128]{2,1,0:T(8,128)S(1)}, u32[]{:S(2)}, u32[]{:S(2)}) async-start(s32[16,36,128]{2,1,0:T(8,128)} %shard_map.78), calls=%async_computation | async-start | bytes 655360 | tf_op jit(solution)/shard_map/all_to_all | solution.py:293
  19.0 24.4 %copy-start.4 = (s32[8,8192]{1,0:T(8,128)}, s32[8,8192]{1,0:T(8,128)S(1)}, u32[]{:S(2)}) copy-start(s32[8,8192]{1,0:T(8,128)S(1)} %collective-permute-done.refs_12_) | copy-start | bytes 786436
  19.0 11.0 %collective-permute-start.2 = (s32[8,8192]{1,0:T(8,128)S(1)}, s32[8,8192]{1,0:T(8,128)S(1)}, u32[]{:S(2)}, u32[]{:S(2)}) collective-permute-start(s32[8,8192]{1,0:T(8,128)S(1)} %collective-permute-done.refs_12_), channel_id=1, source_target_pairs={{0,2},{1,3},{2,0},{3,1},{4,6},{5,7},{6,4},{7,5},{8,10},{9,11},{10,... | collective-permute-start | bytes 786440 | tf_op jit(solution)/shard_map/ppermute | solution.py:267
  20.5 11.3 %collective-permute-start.1 = (s32[8,8192]{1,0:T(8,128)S(1)}, s32[8,8192]{1,0:T(8,128)S(1)}, u32[]{:S(2)}, u32[]{:S(2)}) collective-permute-start(s32[8,8192]{1,0:T(8,128)S(1)} %collective-permute-done.refs_12_), channel_id=1, source_target_pairs={{0,4},{1,5},{2,6},{3,7},{4,0},{5,1},{6,2},{7,3},{8,12},{9,13},{10,... | collective-permute-start | bytes 786440 | tf_op jit(solution)/shard_map/ppermute | solution.py:267
  22.0 10.3 %collective-permute-start.8 = (s32[8,8192]{1,0:T(8,128)}, s32[8,8192]{1,0:T(8,128)S(1)}, u32[]{:S(2)}, u32[]{:S(2)}) collective-permute-start(s32[8,8192]{1,0:T(8,128)} %shard_map.77.refs_8_), channel_id=1, source_target_pairs={{0,1},{1,0},{2,3},{3,2},{4,5},{5,4},{6,7},{7,6},{8,9},{9,8},{10,11... | collective-permute-start | bytes 786440 | tf_op jit(solution)/shard_map/ppermute | solution.py:267
  22.9 20.6 %copy-start.2 = (s32[8,8192]{1,0:T(8,128)}, s32[8,8192]{1,0:T(8,128)S(1)}, u32[]{:S(2)}) copy-start(s32[8,8192]{1,0:T(8,128)S(1)} %collective-permute-done.5.refs_10_) | copy-start | bytes 786436
  22.9 10.9 %collective-permute-start.10 = (s32[8,8192]{1,0:T(8,128)S(1)}, s32[8,8192]{1,0:T(8,128)S(1)}, u32[]{:S(2)}, u32[]{:S(2)}) collective-permute-start(s32[8,8192]{1,0:T(8,128)S(1)} %collective-permute-done.5.refs_10_), channel_id=1, source_target_pairs={{0,1},{1,0},{2,3},{3,2},{4,5},{5,4},{6,7},{7,6},{8,9},{9,8},{10,11... | collective-permute-start | bytes 786440 | tf_op jit(solution)/shard_map/ppermute | solution.py:267
  24.4 19.1 %copy-start.3 = (s32[8,8192]{1,0:T(8,128)}, s32[8,8192]{1,0:T(8,128)S(1)}, u32[]{:S(2)}) copy-start(s32[8,8192]{1,0:T(8,128)S(1)} %collective-permute-done.3.refs_9_) | copy-start | bytes 786436
  24.4 10.0 %collective-permute-start.12 = (s32[8,8192]{1,0:T(8,128)S(1)}, s32[8,8192]{1,0:T(8,128)S(1)}, u32[]{:S(2)}, u32[]{:S(2)}) collective-permute-start(s32[8,8192]{1,0:T(8,128)S(1)} %collective-permute-done.refs_12_), channel_id=1, source_target_pairs={{0,1},{1,0},{2,3},{3,2},{4,5},{5,4},{6,7},{7,6},{8,9},{9,8},{10,11... | collective-permute-start | bytes 786440 | tf_op jit(solution)/shard_map/ppermute | solution.py:267
  30.0 13.5 %copy-start.5 = (s32[8,8192]{1,0:T(8,128)}, s32[8,8192]{1,0:T(8,128)S(1)}, u32[]{:S(2)}) copy-start(s32[8,8192]{1,0:T(8,128)S(1)} %collective-permute-done.2.refs_14_) | copy-start | bytes 786436
  31.8 11.7 %copy-start.6 = (s32[8,8192]{1,0:T(8,128)}, s32[8,8192]{1,0:T(8,128)S(1)}, u32[]{:S(2)}) copy-start(s32[8,8192]{1,0:T(8,128)S(1)} %collective-permute-done.1.refs_13_) | copy-start | bytes 786436
  31.8 2.6 %collective-permute-start.14 = (s32[8,8192]{1,0:T(8,128)S(1)}, s32[8,8192]{1,0:T(8,128)S(1)}, u32[]{:S(2)}, u32[]{:S(2)}) collective-permute-start(s32[8,8192]{1,0:T(8,128)S(1)} %collective-permute-done.2.refs_14_), channel_id=1, source_target_pairs={{0,1},{1,0},{2,3},{3,2},{4,5},{5,4},{6,7},{7,6},{8,9},{9,8},{10,11... | collective-permute-start | bytes 786440 | tf_op jit(solution)/shard_map/ppermute | solution.py:267
  31.8 8.7 %collective-permute-start.6 = (s32[8,8192]{1,0:T(8,128)S(1)}, s32[8,8192]{1,0:T(8,128)S(1)}, u32[]{:S(2)}, u32[]{:S(2)}) collective-permute-start(s32[8,8192]{1,0:T(8,128)S(1)} %collective-permute-done.3.refs_9_), channel_id=1, source_target_pairs={{0,4},{1,5},{2,6},{3,7},{4,0},{5,1},{6,2},{7,3},{8,12},{9,13},{10,... | collective-permute-start | bytes 786440 | tf_op jit(solution)/shard_map/ppermute | solution.py:267
  32.3 8.4 %collective-permute-start.7 = (s32[8,8192]{1,0:T(8,128)S(1)}, s32[8,8192]{1,0:T(8,128)S(1)}, u32[]{:S(2)}, u32[]{:S(2)}) collective-permute-start(s32[8,8192]{1,0:T(8,128)S(1)} %collective-permute-done.1.refs_13_), channel_id=1, source_target_pairs={{0,2},{1,3},{2,0},{3,1},{4,6},{5,7},{6,4},{7,5},{8,10},{9,11},{10,... | collective-permute-start | bytes 786440 | tf_op jit(solution)/shard_map/ppermute | solution.py:267
  33.8 9.6 %collective-permute-start.4 = (s32[16,36,128]{2,1,0:T(8,128)S(1)}, s32[16,36,128]{2,1,0:T(8,128)S(1)}, u32[]{:S(2)}, u32[]{:S(2)}) collective-permute-start(s32[16,36,128]{2,1,0:T(8,128)S(1)} %all-to-all-done.refs_5_), channel_id=1, source_target_pairs={{0,16},{16,0},{1,17},{17,1},{2,18},{18,2},{3,19},{19,3},{4,20},{20... | collective-permute-start | bytes 884744 | tf_op jit(solution)/shard_map/ppermute | solution.py:296
  34.4 7.3 %collective-permute-start.9 = (s32[8,8192]{1,0:T(8,128)S(1)}, s32[8,8192]{1,0:T(8,128)S(1)}, u32[]{:S(2)}, u32[]{:S(2)}) collective-permute-start(s32[8,8192]{1,0:T(8,128)S(1)} %collective-permute-done.3.refs_9_), channel_id=1, source_target_pairs={{0,1},{1,0},{2,3},{3,2},{4,5},{5,4},{6,7},{7,6},{8,9},{9,8},{10,11... | collective-permute-start | bytes 786440 | tf_op jit(solution)/shard_map/ppermute | solution.py:267
  34.4 7.3 %collective-permute-start.13 = (s32[8,8192]{1,0:T(8,128)S(1)}, s32[8,8192]{1,0:T(8,128)S(1)}, u32[]{:S(2)}, u32[]{:S(2)}) collective-permute-start(s32[8,8192]{1,0:T(8,128)S(1)} %collective-permute-done.1.refs_13_), channel_id=1, source_target_pairs={{0,1},{1,0},{2,3},{3,2},{4,5},{5,4},{6,7},{7,6},{8,9},{9,8},{10,11... | collective-permute-start | bytes 786440 | tf_op jit(solution)/shard_map/ppermute | solution.py:267
  40.5 2.9 %collective-permute-start.11 = (s32[8,8192]{1,0:T(8,128)S(1)}, s32[8,8192]{1,0:T(8,128)S(1)}, u32[]{:S(2)}, u32[]{:S(2)}) collective-permute-start(s32[8,8192]{1,0:T(8,128)S(1)} %collective-permute-done.6.refs_11_), channel_id=1, source_target_pairs={{0,1},{1,0},{2,3},{3,2},{4,5},{5,4},{6,7},{7,6},{8,9},{9,8},{10,11... | collective-permute-start | bytes 786440 | tf_op jit(solution)/shard_map/ppermute | solution.py:267
  40.8 2.7 %collective-permute-start.15 = (s32[8,8192]{1,0:T(8,128)S(1)}, s32[8,8192]{1,0:T(8,128)S(1)}, u32[]{:S(2)}, u32[]{:S(2)}) collective-permute-start(s32[8,8192]{1,0:T(8,128)S(1)} %collective-permute-done.7.refs_15_), channel_id=1, source_target_pairs={{0,1},{1,0},{2,3},{3,2},{4,5},{5,4},{6,7},{7,6},{8,9},{9,8},{10,11... | collective-permute-start | bytes 786440 | tf_op jit(solution)/shard_map/ppermute | solution.py:267
  56.7 4.3 %collective-permute-start.16 = (f32[16,1024]{1,0:T(8,128)}, f32[16,1024]{1,0:T(8,128)S(1)}, u32[]{:S(2)}, u32[]{:S(2)}) collective-permute-start(f32[16,1024]{1,0:T(8,128)} %get-tuple-element.22), channel_id=1, source_target_pairs={{1,0},{2,1},{3,2},{4,3},{5,4},{6,5},{7,6},{8,7},{9,8},{10,9},{11,1... | collective-permute-start | bytes 196616 | tf_op jit(solution)/shard_map/ppermute | solution.py:341
  58.6 6.7 %collective-permute-start.17 = (f32[16,1024]{1,0:T(8,128)}, f32[16,1024]{1,0:T(8,128)S(1)}, u32[]{:S(2)}, u32[]{:S(2)}) collective-permute-start(f32[16,1024]{1,0:T(8,128)} %get-tuple-element.23), channel_id=1, source_target_pairs={{0,1},{1,2},{2,3},{3,4},{4,5},{5,6},{6,7},{7,8},{8,9},{9,10},{10,1... | collective-permute-start | bytes 196616 | tf_op jit(solution)/shard_map/ppermute | solution.py:340
  (12 other events, 60.9 us)

commit v4 on v3

--- a/solution.py
+++ b/solution.py
@@ -14,6 +14,11 @@
 LAT_DEV = 8
 LONB = 8
 CELLS = NB * BLK
+PAIR_BITS = 16
+PAIRS = 1 << PAIR_BITS
+SLOT_BITS = 6
+EARLY = (2, 3, 4, 5, 8, 9, 10, 12)
+SLOTS = 1 << SLOT_BITS
 ROWS = 9
 CODE = 32767.0
 FIELD_BOUND = 6.0
@@ -69,8 +74,9 @@
     )(field)
 
 
-def geometry_kernel(block_ref, neighbours_ref, weights_ref, out_ref, packed):
-    tiles, slots = block_ref.shape
+def geometry_kernel(first_ref, block_ref, neighbours_ref, weights_ref, out_ref, packed):
+    tiles, slots = out_ref.shape[0], out_ref.shape[1] // ROWS
+    first = first_ref[0]
     cells = neighbours_ref.shape[1]
     step = 1024
 
@@ -89,23 +95,23 @@
 
     def tile(t, carry):
         for s in range(slots):
-            lanes = pl.ds(pl.multiple_of(block_ref[t, s] * BLK, BLK), BLK)
+            lanes = pl.ds(pl.multiple_of(block_ref[t, first + s] * BLK, BLK), BLK)
             out_ref[t, s * ROWS : (s + 1) * ROWS, :] = packed[:ROWS, lanes]
         return carry
 
     lax.fori_loop(0, tiles, tile, 0)
 
 
-def choose_geometry(blocks, neighbours, slope_weights):
-    tiles, slots = blocks.shape
+def choose_geometry(first, slots, blocks, neighbours, slope_weights):
+    tiles = blocks.shape[0]
     return pl.pallas_call(
         geometry_kernel,
-        in_specs=[SMEM, VMEM, VMEM],
+        in_specs=[SMEM, SMEM, VMEM, VMEM],
         out_specs=VMEM,
         out_shape=jax.ShapeDtypeStruct((tiles, slots * ROWS, BLK), jnp.int32),
         scratch_shapes=[pltpu.VMEM((16, neighbours.shape[1]), jnp.int32)],
         cost_estimate=pl.CostEstimate(flops=0, bytes_accessed=10_000_000, transcendentals=0),
-    )(blocks, neighbours, jnp.transpose(slope_weights, (1, 0, 2)))
+    )(first, blocks, neighbours, jnp.transpose(slope_weights, (1, 0, 2)))
 
 
 def ranks(present):
@@ -148,14 +154,14 @@
 
 
 def remap_kernel(parts, shares, *refs):
-    me_ref, block_ref, slot_ref, dest_ref, order_ref, *refs = refs
+    me_ref, block_ref, table_ref, *refs = refs
     geometry_refs, refs = refs[:shares], refs[shares:]
     weights_ref, *refs = refs
     shards, refs = refs[: len(parts)], refs[len(parts) :]
-    out_ref, top_ref, bottom_ref, field, even, odd, weights, total, field_sem, weight_sem = refs
+    out_ref, near_ref, next_ref, field, even, odd, weights, total, field_sem, weight_sem = refs
     partitions, slots = block_ref.shape
     blocks = partitions * NB
-    chunk = slot_ref.shape[0] // partitions
+    chunk = table_ref.shape[0] // partitions
     share = slots // shares
     ahead = partitions // 4
     me, first_share = me_ref[0], me_ref[1]
@@ -174,7 +180,8 @@
     def fetch(q):
         for i in range(chunk):
             e = q * chunk + i
-            pltpu.make_async_copy(weights_ref.at[order_ref[e]], weights.at[e], weight_sem.at[q]).start(priority=1)
+            pair = table_ref[e] & (PAIRS - 1)
+            pltpu.make_async_copy(weights_ref.at[pair], weights.at[e], weight_sem.at[q]).start(priority=1)
 
     def arrived(q):
         piece = pl.ds(q * chunk, chunk)
@@ -204,9 +211,9 @@
 
     def pair_product(q, i, moments):
         e = q * chunk + i
-        p = order_ref[e]
-        product = jnp.dot(moments[slot_ref[p]], weights[e], preferred_element_type=jnp.float32)
-        dest = dest_ref[p]
+        word = table_ref[e] >> PAIR_BITS
+        dest = word >> SLOT_BITS
+        product = jnp.dot(moments[word & (SLOTS - 1)], weights[e], preferred_element_type=jnp.float32)
         rows = pl.ds(dest >> 3, 16, stride=LAT_DEV)
         total[dest & 7, rows, :] = total[dest & 7, rows, :] + product
 
@@ -237,17 +244,19 @@
     for o in range(LONB):
         lanes = slice(o * BLK, (o + 1) * BLK)
         out_ref[:, :, lanes] = total[o].reshape(levels, LAT_DEV, BLK)
-        top_ref[:, lanes] = total[o, pl.ds(0, levels, stride=LAT_DEV), :]
-        bottom_ref[:, lanes] = total[o, pl.ds(LAT_DEV - 1, levels, stride=LAT_DEV), :]
-
-
-def remap(me, blocks, slot, dest, order, geometry, weights, parts, shards, levels):
+        top = total[o, pl.ds(0, levels, stride=LAT_DEV), :]
+        bottom = total[o, pl.ds(LAT_DEV - 1, levels, stride=LAT_DEV), :]
+        near_ref[:, lanes] = jnp.where(me & 1 == 0, bottom, top)
+        next_ref[:, lanes] = jnp.where(me & 1 == 0, top, bottom)
+
+
+def remap(me, blocks, table, geometry, weights, parts, shards, levels):
     partitions, slots = blocks.shape
     total = (LONB, levels * LAT_DEV, BLK)
     edge = jax.ShapeDtypeStruct((levels, LONB * BLK), jnp.float32)
     return pl.pallas_call(
         functools.partial(remap_kernel, parts, len(geometry)),
-        in_specs=[SMEM] * 5 + [VMEM] * len(geometry) + [ANY] + [ANY] * len(shards),
+        in_specs=[SMEM] * 3 + [VMEM] * len(geometry) + [ANY] + [ANY] * len(shards),
         out_specs=(VMEM, VMEM, VMEM),
         out_shape=(jax.ShapeDtypeStruct((levels, LAT_DEV, LONB * BLK), jnp.float32), edge, edge),
         scratch_shapes=[
@@ -259,8 +268,8 @@
             pltpu.SemaphoreType.DMA,
             pltpu.SemaphoreType.DMA((partitions,)),
         ],
-        compiler_params=pltpu.CompilerParams(vmem_limit_bytes=56 * 1024 * 1024),
-    )(me, blocks, slot, dest, order, *geometry, weights, *shards)
+        compiler_params=pltpu.CompilerParams(vmem_limit_bytes=44 * 1024 * 1024),
+    )(me, blocks, table, *geometry, weights, *shards)
 
 
 def swap(array, code):
@@ -287,15 +296,15 @@
     group = lax.axis_index("groups")
     shares = 2 if lax.axis_size("groups") == 2 else 1
     share = slots // shares
-    if shares == 2:
-        outgoing_blocks = lax.dynamic_slice_in_dim(outgoing_blocks, group * share, share, 1)
-    chosen = choose_geometry(outgoing_blocks, neighbours, slope_weights)
+    start = (group * share if shares == 2 else jnp.zeros((), jnp.int32)).reshape(1)
+    chosen = choose_geometry(start, share, outgoing_blocks, neighbours, slope_weights)
     geometry = [lax.all_to_all(chosen, "src", split_axis=0, concat_axis=0, tiled=True)]
     first = jnp.zeros((), jnp.int32)
     if shares == 2:
         geometry.append(lax.ppermute(geometry[0], "groups", [(0, 1), (1, 0)]))
         first = group
 
+    pair_block, _ = tie(pair_block, chosen)
     row = lax.dynamic_index_in_dim(pair_block, own_index, 0, keepdims=False)
     names = jnp.arange(partitions * NB, dtype=jnp.int32)
     same = row[:, None] == names[None, :]
@@ -303,17 +312,20 @@
     rank = ranks(needed)
     blocks = blocks_of_slots(needed, rank, slots)
     slot = jnp.sum(jnp.where(same, rank.reshape(1, -1), 0), axis=1)
+    word = (pair_dest[0] * SLOTS + slot) * PAIRS + jnp.arange(pair_total, dtype=jnp.int32)
     pair_ids = jnp.arange(pair_total, dtype=jnp.int32)
     key = row // NB * pair_total + pair_ids
     place = jnp.sum((key[:, None] < key[None, :]).astype(jnp.int32), axis=0)
-    order = jnp.sum(jnp.where(place[:, None] == pair_ids[None, :], pair_ids[:, None], 0), axis=0)
-
+    table = jnp.sum(jnp.where(place[:, None] == pair_ids[None, :], word[:, None], 0), axis=0)
+
+    me = jnp.stack([own_index, first])
     if partitions == 16:
         far, z, y = swap(packed, 8), swap(packed, 4), swap(packed, 2)
-        far, order, _ = tie(far, order, chosen)
+        far, _ = tie(far, chosen)
+        diagonal = swap(y, 4)
         far_z, far_y = swap(far, 4), swap(far, 2)
-        far_z, far_y, y, order, slot, blocks = tie(far_z, far_y, y, order, slot, blocks)
-        far_diagonal, diagonal = swap(far_z, 2), swap(y, 4)
+        far_z, far_y, table, blocks, me = tie(far_z, far_y, table, blocks, me)
+        far_diagonal = swap(far_z, 2)
         held = [
             (0, packed),
             (2, y),
@@ -326,19 +338,20 @@
         ]
         held = held + [(code ^ 1, swap(array, 1)) for code, array in held]
         parts = [(code, 0, array.shape[1]) for code, array in held]
-        shards = [array for _, array in held]
+        shards = [pltpu.with_memory_space_constraint(array, pltpu.VMEM) if code in EARLY else array for code, array in held]
     else:
         whole = lax.all_gather(packed, "src", axis=1, tiled=True)
         parts, shards = [(None, 0, whole.shape[1])], [whole]
 
-    me = jnp.stack([own_index, first])
-    remapped, top, bottom = remap(
-        me, blocks, slot, pair_dest[0], order, geometry, remap_weights, parts, shards, levels
+    remapped, near, beyond = remap(
+        me, blocks, table, geometry, remap_weights, parts, shards, levels
     )
-    up = [(i, i + 1) for i in range(partitions - 1)]
-    down = [(i + 1, i) for i in range(partitions - 1)]
-    below = lax.ppermute(bottom, "src", up)
-    above = lax.ppermute(top, "src", down)
+    steps = [(i, i + 1) for i in range(1, partitions - 1, 2)]
+    beyond = lax.ppermute(beyond, "src", steps + [(j, i) for i, j in steps])
+    near = swap(near, 1)
+    even = own_index % 2 == 0
+    below = jnp.where(even, beyond, near)
+    above = jnp.where(even, near, beyond)
     padded = jnp.concatenate([below[:, None], remapped, above[:, None]], axis=1)
     meridional = 0.5 * (padded[:, 2:] - padded[:, :-2])
     return remapped, meridional

time: 68.2 us -> 64.3 us (0.943)
  waiting for transfers between devices: 19.2 us -> 14.8 us
  starting transfers between devices: 20.6 us -> 23.4 us
  Pallas kernels: 16.9 us -> 15.7 us
  other arithmetic: 8.31 us -> 7.37 us
    ppermute x15 -> x16, starting transfers between devices: 9.68 us -> 14.5 us  [swap(): lax.ppermute(array, 'src', [(i, i ^ code) for i in range(lax.axis_size('s...]
    ppermute x15 -> x16, waiting for transfers between devices: 13.3 us -> 9.59 us  [swap(): lax.ppermute(array, 'src', [(i, i ^ code) for i in range(lax.axis_size('s...]
    ppermute x2 -> x1, starting transfers between devices: 4.33 us -> 2.34 us  [local(): beyond = lax.ppermute(beyond, 'src', steps + [(j, i) for i, j in steps])]
    pallas_call x1, Pallas kernels: 12.4 us -> 11 us  [remap(): pl.pallas_call(functools.partial(remap_kernel, parts, len(geometry)), in_...]
    ppermute x2 -> x1, waiting for transfers between devices: 4.2 us -> 4.2 us  [local(): beyond = lax.ppermute(beyond, 'src', steps + [(j, i) for i, j in steps])]
  transfers between devices with their start and end apart: 19 -> 19, of which waited for: 6 -> 8; matrix products, arithmetic and copies ran while one was open for 10% -> 8% of each run, Pallas kernels for 4% -> 4%
where the time goes in v4:
time: 64.3 us; the launch traced here: 63.3 us
  starting transfers between devices  23.4 us (36%)
  Pallas kernels  15.7 us (24%)
  waiting for transfers between devices  14.8 us (23%)
  other arithmetic  7.37 us (11%)
  local copies, waits for them, and re-layouts  1.24 us (2%)
  between operations  0.78 us (1%)
    ppermute x16, starting transfers between devices, swap(): lax.ppermute(array, 'src', [(i, i ^ code) for i in range(lax.axis_size('s...  14.5 us
    pallas_call x1, Pallas kernels, remap(): pl.pallas_call(functools.partial(remap_kernel, parts, len(geometry)), in_...  11 us
    ppermute x16, waiting for transfers between devices, swap(): lax.ppermute(array, 'src', [(i, i ^ code) for i in range(lax.axis_size('s...  9.59 us
    all_to_all x1, starting transfers between devices, local(): lax.all_to_all(chosen, 'src', split_axis=0, concat_axis=0, tiled=True)  5.97 us
    ppermute x1, waiting for transfers between devices, local(): beyond = lax.ppermute(beyond, 'src', steps + [(j, i) for i, j in steps])  4.2 us
    pallas_call x1, Pallas kernels, choose_geometry(): pl.pallas_call(geometry_kernel, in_specs=[SMEM, SMEM, VMEM, VMEM], out_sp...  2.5 us
    ppermute x1, starting transfers between devices, local(): beyond = lax.ppermute(beyond, 'src', steps + [(j, i) for i, j in steps])  2.34 us
    mul x1, other arithmetic, local(): meridional = 0.5 * (padded[:, 2:] - padded[:, :-2])  2.22 us
  transfers between devices with their start and end apart: 19, of which 8 were waited for; matrix products, arithmetic and copies ran while one was open for 8% of the time, Pallas kernels for 4%

profile of v4, /device:TPU:18, one launch (start us, length us, event | category | flops | bytes accessed | tf_op | source)
XLA Modules:
  0.0 63.3 jit_solution(12291392491186654711)
XLA Ops:
  0.6 2.2 %shard_map.77.refs_6_ = s32[8,8192]{1,0:T(8,128)} custom-call(f32[16,8192]{1,0:T(8,128)} %field_ref.1), custom_call_target="tpu_custom_call" | custom-call | tf_op jit(solution)/shard_map/pallas_call | solution.py:69
  2.8 1.6 %collective-permute-start.5 = (s32[8,8192]{1,0:T(8,128)}, s32[8,8192]{1,0:T(8,128)S(1)}, u32[]{:S(2)}, u32[]{:S(2)}) collective-permute-start(s32[8,8192]{1,0:T(8,128)} %shard_map.77.refs_6_), channel_id=1, source_target_pairs={{0,4},{1,5},{2,6},{3,7},{4,0},{5,1},{6,2},{7,3},{8,12},{9,13},{10,... | collective-permute-start | bytes 786440 | tf_op jit(solution)/shard_map/ppermute | solution.py:276
  4.4 1.5 %collective-permute-start.4 = (s32[8,8192]{1,0:T(8,128)}, s32[8,8192]{1,0:T(8,128)S(1)}, u32[]{:S(2)}, u32[]{:S(2)}) collective-permute-start(s32[8,8192]{1,0:T(8,128)} %shard_map.77.refs_6_), channel_id=1, source_target_pairs={{0,2},{1,3},{2,0},{3,1},{4,6},{5,7},{6,4},{7,5},{8,10},{9,11},{10,... | collective-permute-start | bytes 786440 | tf_op jit(solution)/shard_map/ppermute | solution.py:276
  6.3 1.1 %compare_reduce_fusion = pred[16,64]{1,0:T(8,128)(4,1)S(1)} fusion(s32[16,256]{1,0:T(8,128)} %param.9, s32[64]{0:T(128)S(1)} %iota_add_fusion.3), kind=kLoop, calls=%fused_computation.3 | loop fusion | flops 523264 | bytes 17664 | tf_op jit(solution)/shard_map/reduce_or | solution.py:294
  7.6 0.9 %select_reduce_fusion.3.block_ref = s32[16,8]{1,0:T(8,128)} fusion(s32[16,64]{1,0:T(8,128)S(1)} %convert_reduce_fusion.1, pred[16,64]{1,0:T(8,128)(4,1)S(1)} %compare_reduce_fusion), kind=kLoop, calls=%fused_computation.17 | loop fusion | flops 32640 | bytes 5632 | tf_op jit(solution)/shard_map/reduce_sum | solution.py:127
  8.6 2.5 %shard_map.78 = s32[16,36,128]{2,1,0:T(8,128)} custom-call(s32[1]{0:T(128)} %bitcast.first_ref, s32[16,8]{1,0:T(8,128)} %select_reduce_fusion.3.block_ref, s32[6,8192]{1,0:T(8,128)} %neighbours_ref.1, f32[6,2,8192]{2,1,0:T(2,128)} %bitcast.11), custom_call_target="tpu_custom_call" | custom-call | bytes 10000000 | tf_op jit(solution)/shard_map/pallas_call | solution.py:107
  11.1 6.0 %all-to-all-start = ((s32[16,36,128]{2,1,0:T(8,128)}), s32[16,36,128]{2,1,0:T(8,128)S(1)}, u32[]{:S(2)}, u32[]{:S(2)}) async-start(s32[16,36,128]{2,1,0:T(8,128)} %shard_map.78), calls=%async_computation | async-start | bytes 655360 | tf_op jit(solution)/shard_map/all_to_all | solution.py:301
  17.0 0.7 %broadcast_multiply_fusion = s32[1,256]{1,0:T(1,128)S(1)} fusion(s32[1,256]{1,0:T(1,128)} %param.10), kind=kLoop, calls=%fused_computation.34 | loop fusion | flops 256 | bytes 2048 | tf_op jit(solution)/shard_map/mul | solution.py:315
  17.7 0.7 %iota_add_fusion.1 = (s32[1,256]{1,0:T(1,128)S(1)}, s32[1,256]{1,0:T(1,128)S(1)}) fusion(s32[16,256]{1,0:T(8,128)} %param.9, s32[]{:T(128)S(6)} %select_n.51), kind=kLoop, calls=%fused_computation.31 | loop fusion | flops 4352 | bytes 3076 | tf_op jit(solution)/shard_map/add | solution.py:317
  19.5 1.5 %collective-permute-start.2 = (s32[8,8192]{1,0:T(8,128)S(1)}, s32[8,8192]{1,0:T(8,128)S(1)}, u32[]{:S(2)}, u32[]{:S(2)}) collective-permute-start(s32[8,8192]{1,0:T(8,128)S(1)} %collective-permute-done.refs_10_), channel_id=1, source_target_pairs={{0,2},{1,3},{2,0},{3,1},{4,6},{5,7},{6,4},{7,5},{8,10},{9,11},{10,... | collective-permute-start | bytes 786440 | tf_op jit(solution)/shard_map/ppermute | solution.py:276
  21.0 4.8 %collective-permute-start.1 = (s32[8,8192]{1,0:T(8,128)S(1)}, s32[8,8192]{1,0:T(8,128)S(1)}, u32[]{:S(2)}, u32[]{:S(2)}) collective-permute-start(s32[8,8192]{1,0:T(8,128)S(1)} %collective-permute-done.refs_10_), channel_id=1, source_target_pairs={{0,4},{1,5},{2,6},{3,7},{4,0},{5,1},{6,2},{7,3},{8,12},{9,13},{10,... | collective-permute-start | bytes 786440 | tf_op jit(solution)/shard_map/ppermute | solution.py:276
  26.9 2.9 %collective-permute-done.2.refs_12_ = s32[8,8192]{1,0:T(8,128)S(1)} collective-permute-done((s32[8,8192]{1,0:T(8,128)S(1)}, s32[8,8192]{1,0:T(8,128)S(1)}, u32[]{:S(2)}, u32[]{:S(2)}) %collective-permute-start.2) | collective-permute-done | bytes 262176 | tf_op jit(solution)/shard_map/ppermute | solution.py:276
  29.9 0.8 %collective-permute-done.1.refs_11_ = s32[8,8192]{1,0:T(8,128)S(1)} collective-permute-done((s32[8,8192]{1,0:T(8,128)S(1)}, s32[8,8192]{1,0:T(8,128)S(1)}, u32[]{:S(2)}, u32[]{:S(2)}) %collective-permute-start.1) | collective-permute-done | bytes 262176 | tf_op jit(solution)/shard_map/ppermute | solution.py:276
  30.7 1.9 %collective-permute-start.6 = (s32[8,8192]{1,0:T(8,128)S(1)}, s32[8,8192]{1,0:T(8,128)S(1)}, u32[]{:S(2)}, u32[]{:S(2)}) collective-permute-start(s32[8,8192]{1,0:T(8,128)S(1)} %collective-permute-done.4.refs_7_), channel_id=1, source_target_pairs={{0,4},{1,5},{2,6},{3,7},{4,0},{5,1},{6,2},{7,3},{8,12},{9,13},{10,... | collective-permute-start | bytes 786440 | tf_op jit(solution)/shard_map/ppermute | solution.py:276
  32.6 1.6 %collective-permute-start.7 = (s32[8,8192]{1,0:T(8,128)S(1)}, s32[8,8192]{1,0:T(8,128)S(1)}, u32[]{:S(2)}, u32[]{:S(2)}) collective-permute-start(s32[8,8192]{1,0:T(8,128)S(1)} %collective-permute-done.1.refs_11_), channel_id=1, source_target_pairs={{0,2},{1,3},{2,0},{3,1},{4,6},{5,7},{6,4},{7,5},{8,10},{9,11},{10,... | collective-permute-start | bytes 786440 | tf_op jit(solution)/shard_map/ppermute | solution.py:276
  34.2 0.5 collective-permute-start.3
  34.7 4.4 %collective-permute-done.6.refs_9_ = s32[8,8192]{1,0:T(8,128)S(1)} collective-permute-done((s32[8,8192]{1,0:T(8,128)S(1)}, s32[8,8192]{1,0:T(8,128)S(1)}, u32[]{:S(2)}, u32[]{:S(2)}) %collective-permute-start.6) | collective-permute-done | bytes 262176 | tf_op jit(solution)/shard_map/ppermute | solution.py:276
  39.6 1.0 %collective-permute-done.7.refs_13_ = s32[8,8192]{1,0:T(8,128)S(1)} collective-permute-done((s32[8,8192]{1,0:T(8,128)S(1)}, s32[8,8192]{1,0:T(8,128)S(1)}, u32[]{:S(2)}, u32[]{:S(2)}) %collective-permute-start.7) | collective-permute-done | bytes 262176 | tf_op jit(solution)/shard_map/ppermute | solution.py:276
  41.0 1.0 %collective-permute-done.3.refs_4_ = s32[16,36,128]{2,1,0:T(8,128)S(1)} collective-permute-done((s32[16,36,128]{2,1,0:T(8,128)S(1)}, s32[16,36,128]{2,1,0:T(8,128)S(1)}, u32[]{:S(2)}, u32[]{:S(2)}) %collective-permute-start.3) | collective-permute-done | bytes 294944 | tf_op jit(solution)/shard_map/ppermute | solution.py:304
  42.1 0.9 %copy-done = s32[8,8192]{1,0:T(8,128)S(1)} copy-done((s32[8,8192]{1,0:T(8,128)S(1)}, s32[8,8192]{1,0:T(8,128)}, u32[]{:S(2)}) %copy-start) | copy-done | bytes 262168
  43.1 11.0 %shard_map.79 = (f32[16,8,1024]{2,1,0:T(8,128)}, f32[16,1024]{1,0:T(8,128)S(1)}, f32[16,1024]{1,0:T(8,128)S(1)}) custom-call(s32[2]{0:T(128)S(1)} %pad_add_fusion.refs_0_, s32[16,8]{1,0:T(8,128)S(1)} %select_reduce_fusion.2.refs_1_, s32[256]{0:T(256)S(1)} %select_reduce_fusion.1.refs_2_, s32[16,36,128]{2,1,0:T(8,128)S(1)} %all-to-all-done.refs_3_, ...), custom_call_target="tpu_custom_call" | custom-call | tf_op jit(solution)/shard_map/pallas_call | solution.py:257
  54.3 2.3 %collective-permute-start.17 = (f32[16,1024]{1,0:T(8,128)S(1)}, f32[16,1024]{1,0:T(8,128)S(1)}, u32[]{:S(2)}, u32[]{:S(2)}) collective-permute-start(f32[16,1024]{1,0:T(8,128)S(1)} %get-tuple-element.21), channel_id=1, source_target_pairs={{1,2},{3,4},{5,6},{7,8},{9,10},{11,12},{13,14},{2,1},{4,3},{6,5},{... | collective-permute-start | bytes 196616 | tf_op jit(solution)/shard_map/ppermute | solution.py:350
  56.7 4.2 %collective-permute-done.17 = f32[16,1024]{1,0:T(8,128)S(1)} collective-permute-done((f32[16,1024]{1,0:T(8,128)S(1)}, f32[16,1024]{1,0:T(8,128)S(1)}, u32[]{:S(2)}, u32[]{:S(2)}) %collective-permute-start.17) | collective-permute-done | bytes 65568 | tf_op jit(solution)/shard_map/ppermute | solution.py:350
  61.0 2.2 %fusion.2 = f32[16,8,1024]{2,1,0:T(8,128)} fusion(f32[16,8,1024]{2,1,0:T(8,128)} %get-tuple-element.10, f32[16,1,1024]{2,1,0:T(1,128)S(1)} %copy.11, f32[16,1,1024]{2,1,0:T(1,128)S(1)} %copy.10), kind=kLoop, calls=%fused_computation.6 | loop fusion | flops 524288 | bytes 1179648 | tf_op jit(solution)/shard_map/mul | solution.py:356
  (41 shorter events, 4.1 us)
Async XLA Ops:
  2.8 29.8 %collective-permute-start.8 = (s32[8,8192]{1,0:T(8,128)}, s32[8,8192]{1,0:T(8,128)S(1)}, u32[]{:S(2)}, u32[]{:S(2)}) collective-permute-start(s32[8,8192]{1,0:T(8,128)} %shard_map.77.refs_6_), channel_id=1, source_target_pairs={{0,1},{1,0},{2,3},{3,2},{4,5},{5,4},{6,7},{7,6},{8,9},{9,8},{10,11... | collective-permute-start | bytes 786440 | tf_op jit(solution)/shard_map/ppermute | solution.py:276
  2.8 23.5 %collective-permute-start.5 = (s32[8,8192]{1,0:T(8,128)}, s32[8,8192]{1,0:T(8,128)S(1)}, u32[]{:S(2)}, u32[]{:S(2)}) collective-permute-start(s32[8,8192]{1,0:T(8,128)} %shard_map.77.refs_6_), channel_id=1, source_target_pairs={{0,4},{1,5},{2,6},{3,7},{4,0},{5,1},{6,2},{7,3},{8,12},{9,13},{10,... | collective-permute-start | bytes 786440 | tf_op jit(solution)/shard_map/ppermute | solution.py:276
  4.4 22.1 %collective-permute-start.4 = (s32[8,8192]{1,0:T(8,128)}, s32[8,8192]{1,0:T(8,128)S(1)}, u32[]{:S(2)}, u32[]{:S(2)}) collective-permute-start(s32[8,8192]{1,0:T(8,128)} %shard_map.77.refs_6_), channel_id=1, source_target_pairs={{0,2},{1,3},{2,0},{3,1},{4,6},{5,7},{6,4},{7,5},{8,10},{9,11},{10,... | collective-permute-start | bytes 786440 | tf_op jit(solution)/shard_map/ppermute | solution.py:276
  5.9 13.6 %collective-permute-start = (s32[8,8192]{1,0:T(8,128)}, s32[8,8192]{1,0:T(8,128)S(1)}, u32[]{:S(2)}, u32[]{:S(2)}) collective-permute-start(s32[8,8192]{1,0:T(8,128)} %shard_map.77.refs_6_), channel_id=1, source_target_pairs={{0,8},{1,9},{2,10},{3,11},{4,12},{5,13},{6,14},{7,15},{8,0},{9,1},... | collective-permute-start | bytes 786440 | tf_op jit(solution)/shard_map/ppermute | solution.py:276
  11.1 23.1 %all-to-all-start = ((s32[16,36,128]{2,1,0:T(8,128)}), s32[16,36,128]{2,1,0:T(8,128)S(1)}, u32[]{:S(2)}, u32[]{:S(2)}) async-start(s32[16,36,128]{2,1,0:T(8,128)} %shard_map.78), calls=%async_computation | async-start | bytes 655360 | tf_op jit(solution)/shard_map/all_to_all | solution.py:301
  19.5 10.4 %collective-permute-start.2 = (s32[8,8192]{1,0:T(8,128)S(1)}, s32[8,8192]{1,0:T(8,128)S(1)}, u32[]{:S(2)}, u32[]{:S(2)}) collective-permute-start(s32[8,8192]{1,0:T(8,128)S(1)} %collective-permute-done.refs_10_), channel_id=1, source_target_pairs={{0,2},{1,3},{2,0},{3,1},{4,6},{5,7},{6,4},{7,5},{8,10},{9,11},{10,... | collective-permute-start | bytes 786440 | tf_op jit(solution)/shard_map/ppermute | solution.py:276
  21.0 9.6 %collective-permute-start.1 = (s32[8,8192]{1,0:T(8,128)S(1)}, s32[8,8192]{1,0:T(8,128)S(1)}, u32[]{:S(2)}, u32[]{:S(2)}) collective-permute-start(s32[8,8192]{1,0:T(8,128)S(1)} %collective-permute-done.refs_10_), channel_id=1, source_target_pairs={{0,4},{1,5},{2,6},{3,7},{4,0},{5,1},{6,2},{7,3},{8,12},{9,13},{10,... | collective-permute-start | bytes 786440 | tf_op jit(solution)/shard_map/ppermute | solution.py:276
  26.3 7.9 %collective-permute-start.10 = (s32[8,8192]{1,0:T(8,128)S(1)}, s32[8,8192]{1,0:T(8,128)S(1)}, u32[]{:S(2)}, u32[]{:S(2)}) collective-permute-start(s32[8,8192]{1,0:T(8,128)S(1)} %collective-permute-done.5.refs_8_), channel_id=1, source_target_pairs={{0,1},{1,0},{2,3},{3,2},{4,5},{5,4},{6,7},{7,6},{8,9},{9,8},{10,11... | collective-permute-start | bytes 786440 | tf_op jit(solution)/shard_map/ppermute | solution.py:276
  26.4 12.7 %collective-permute-start.12 = (s32[8,8192]{1,0:T(8,128)S(1)}, s32[8,8192]{1,0:T(8,128)S(1)}, u32[]{:S(2)}, u32[]{:S(2)}) collective-permute-start(s32[8,8192]{1,0:T(8,128)S(1)} %collective-permute-done.refs_10_), channel_id=1, source_target_pairs={{0,1},{1,0},{2,3},{3,2},{4,5},{5,4},{6,7},{7,6},{8,9},{9,8},{10,11... | collective-permute-start | bytes 786440 | tf_op jit(solution)/shard_map/ppermute | solution.py:276
  29.9 4.8 %collective-permute-start.9 = (s32[8,8192]{1,0:T(8,128)S(1)}, s32[8,8192]{1,0:T(8,128)S(1)}, u32[]{:S(2)}, u32[]{:S(2)}) collective-permute-start(s32[8,8192]{1,0:T(8,128)S(1)} %collective-permute-done.4.refs_7_), channel_id=1, source_target_pairs={{0,1},{1,0},{2,3},{3,2},{4,5},{5,4},{6,7},{7,6},{8,9},{9,8},{10,11... | collective-permute-start | bytes 786440 | tf_op jit(solution)/shard_map/ppermute | solution.py:276
  30.7 8.5 %collective-permute-start.6 = (s32[8,8192]{1,0:T(8,128)S(1)}, s32[8,8192]{1,0:T(8,128)S(1)}, u32[]{:S(2)}, u32[]{:S(2)}) collective-permute-start(s32[8,8192]{1,0:T(8,128)S(1)} %collective-permute-done.4.refs_7_), channel_id=1, source_target_pairs={{0,4},{1,5},{2,6},{3,7},{4,0},{5,1},{6,2},{7,3},{8,12},{9,13},{10,... | collective-permute-start | bytes 786440 | tf_op jit(solution)/shard_map/ppermute | solution.py:276
  32.6 8.0 %collective-permute-start.7 = (s32[8,8192]{1,0:T(8,128)S(1)}, s32[8,8192]{1,0:T(8,128)S(1)}, u32[]{:S(2)}, u32[]{:S(2)}) collective-permute-start(s32[8,8192]{1,0:T(8,128)S(1)} %collective-permute-done.1.refs_11_), channel_id=1, source_target_pairs={{0,2},{1,3},{2,0},{3,1},{4,6},{5,7},{6,4},{7,5},{8,10},{9,11},{10,... | collective-permute-start | bytes 786440 | tf_op jit(solution)/shard_map/ppermute | solution.py:276
  34.2 7.9 %collective-permute-start.3 = (s32[16,36,128]{2,1,0:T(8,128)S(1)}, s32[16,36,128]{2,1,0:T(8,128)S(1)}, u32[]{:S(2)}, u32[]{:S(2)}) collective-permute-start(s32[16,36,128]{2,1,0:T(8,128)S(1)} %all-to-all-done.refs_3_), channel_id=1, source_target_pairs={{0,16},{16,0},{1,17},{17,1},{2,18},{18,2},{3,19},{19,3},{4,20},{20... | collective-permute-start | bytes 884744 | tf_op jit(solution)/shard_map/ppermute | solution.py:304
  34.7 5.9 %collective-permute-start.14 = (s32[8,8192]{1,0:T(8,128)S(1)}, s32[8,8192]{1,0:T(8,128)S(1)}, u32[]{:S(2)}, u32[]{:S(2)}) collective-permute-start(s32[8,8192]{1,0:T(8,128)S(1)} %collective-permute-done.2.refs_12_), channel_id=1, source_target_pairs={{0,1},{1,0},{2,3},{3,2},{4,5},{5,4},{6,7},{7,6},{8,9},{9,8},{10,11... | collective-permute-start | bytes 786440 | tf_op jit(solution)/shard_map/ppermute | solution.py:276
  39.1 1.5 %collective-permute-start.11 = (s32[8,8192]{1,0:T(8,128)S(1)}, s32[8,8192]{1,0:T(8,128)S(1)}, u32[]{:S(2)}, u32[]{:S(2)}) collective-permute-start(s32[8,8192]{1,0:T(8,128)S(1)} %collective-permute-done.6.refs_9_), channel_id=1, source_target_pairs={{0,1},{1,0},{2,3},{3,2},{4,5},{5,4},{6,7},{7,6},{8,9},{9,8},{10,11... | collective-permute-start | bytes 786440 | tf_op jit(solution)/shard_map/ppermute | solution.py:276
  39.1 1.9 %collective-permute-start.13 = (s32[8,8192]{1,0:T(8,128)S(1)}, s32[8,8192]{1,0:T(8,128)S(1)}, u32[]{:S(2)}, u32[]{:S(2)}) collective-permute-start(s32[8,8192]{1,0:T(8,128)S(1)} %collective-permute-done.1.refs_11_), channel_id=1, source_target_pairs={{0,1},{1,0},{2,3},{3,2},{4,5},{5,4},{6,7},{7,6},{8,9},{9,8},{10,11... | collective-permute-start | bytes 786440 | tf_op jit(solution)/shard_map/ppermute | solution.py:276
  40.6 1.5 %collective-permute-start.15 = (s32[8,8192]{1,0:T(8,128)S(1)}, s32[8,8192]{1,0:T(8,128)S(1)}, u32[]{:S(2)}, u32[]{:S(2)}) collective-permute-start(s32[8,8192]{1,0:T(8,128)S(1)} %collective-permute-done.7.refs_13_), channel_id=1, source_target_pairs={{0,1},{1,0},{2,3},{3,2},{4,5},{5,4},{6,7},{7,6},{8,9},{9,8},{10,11... | collective-permute-start | bytes 786440 | tf_op jit(solution)/shard_map/ppermute | solution.py:276
  42.1 1.0 %copy-start = (s32[8,8192]{1,0:T(8,128)S(1)}, s32[8,8192]{1,0:T(8,128)}, u32[]{:S(2)}) copy-start(s32[8,8192]{1,0:T(8,128)} %shard_map.77.refs_6_) | copy-start | bytes 786436
  54.1 2.6 %collective-permute-start.16 = (f32[16,1024]{1,0:T(8,128)S(1)}, f32[16,1024]{1,0:T(8,128)S(1)}, u32[]{:S(2)}, u32[]{:S(2)}) collective-permute-start(f32[16,1024]{1,0:T(8,128)S(1)} %get-tuple-element.20), channel_id=1, source_target_pairs={{0,1},{1,0},{2,3},{3,2},{4,5},{5,4},{6,7},{7,6},{8,9},{9,8},{10,11... | collective-permute-start | bytes 196616 | tf_op jit(solution)/shard_map/ppermute | solution.py:276
  54.3 6.6 %collective-permute-start.17 = (f32[16,1024]{1,0:T(8,128)S(1)}, f32[16,1024]{1,0:T(8,128)S(1)}, u32[]{:S(2)}, u32[]{:S(2)}) collective-permute-start(f32[16,1024]{1,0:T(8,128)S(1)} %get-tuple-element.21), channel_id=1, source_target_pairs={{1,2},{3,4},{5,6},{7,8},{9,10},{11,12},{13,14},{2,1},{4,3},{6,5},{... | collective-permute-start | bytes 196616 | tf_op jit(solution)/shard_map/ppermute | solution.py:350

commit v5 on v4

--- a/solution.py
+++ b/solution.py
@@ -156,7 +156,7 @@
 def remap_kernel(parts, shares, *refs):
     me_ref, block_ref, table_ref, *refs = refs
     geometry_refs, refs = refs[:shares], refs[shares:]
-    weights_ref, *refs = refs
+    early_weights, weights_ref, *refs = refs
     shards, refs = refs[: len(parts)], refs[len(parts) :]
     out_ref, near_ref, next_ref, field, even, odd, weights, total, field_sem, weight_sem = refs
     partitions, slots = block_ref.shape
@@ -164,6 +164,7 @@
     chunk = table_ref.shape[0] // partitions
     share = slots // shares
     ahead = partitions // 4
+    kept = early_weights.shape[0] // chunk
     me, first_share = me_ref[0], me_ref[1]
 
     copies = []
@@ -181,17 +182,18 @@
         for i in range(chunk):
             e = q * chunk + i
             pair = table_ref[e] & (PAIRS - 1)
-            pltpu.make_async_copy(weights_ref.at[pair], weights.at[e], weight_sem.at[q]).start(priority=1)
+            target = weights.at[e - kept * chunk]
+            pltpu.make_async_copy(weights_ref.at[pair], target, weight_sem.at[q]).start(priority=1)
 
     def arrived(q):
-        piece = pl.ds(q * chunk, chunk)
+        piece = pl.ds((q - kept) * chunk, chunk)
         pltpu.make_async_copy(weights_ref.at[pl.ds(0, chunk)], weights.at[piece], weight_sem.at[q]).wait()
 
     def fetch_one(q, carry):
         fetch(q)
         return carry
 
-    lax.fori_loop(0, ahead, fetch_one, 0)
+    lax.fori_loop(kept, kept + ahead, fetch_one, 0)
     total[...] = jnp.zeros_like(total)
     for copy in copies:
         copy.wait()
@@ -209,37 +211,40 @@
         for m, moment in enumerate(slopes_and_moments(window, words)):
             moments[s, :, m * BLK : (m + 1) * BLK] = moment
 
-    def pair_product(q, i, moments):
+    def pair_product(q, i, moments, source, first):
         e = q * chunk + i
         word = table_ref[e] >> PAIR_BITS
         dest = word >> SLOT_BITS
-        product = jnp.dot(moments[word & (SLOTS - 1)], weights[e], preferred_element_type=jnp.float32)
+        product = jnp.dot(moments[word & (SLOTS - 1)], source[e - first], preferred_element_type=jnp.float32)
         rows = pl.ds(dest >> 3, 16, stride=LAT_DEV)
         total[dest & 7, rows, :] = total[dest & 7, rows, :] + product
 
-    def step(q, here, there):
+    def step(q, here, there, streamed):
         later = jnp.minimum(q + 1, partitions - 1)
 
-        @pl.when(q + ahead < partitions)
-        def _():
-            fetch(q + ahead)
-
-        arrived(q)
+        if streamed:
+
+            @pl.when(q + ahead < partitions)
+            def _():
+                fetch(q + ahead)
+
+            arrived(q)
         each = max(1, chunk // slots)
         for j in range(slots):
             slot_moments(later, j, there)
             for i in range(j * each, (j + 1) * each):
-                pair_product(q, i, here)
+                pair_product(q, i, here, *((weights, kept * chunk) if streamed else (early_weights, 0)))
 
     for j in range(slots):
         slot_moments(0, j, even)
 
-    def two(h, carry):
-        step(2 * h, even, odd)
-        step(2 * h + 1, odd, even)
-        return carry
-
-    lax.fori_loop(0, partitions // 2, two, 0)
+    def two(streamed, h, carry):
+        step(2 * h, even, odd, streamed)
+        step(2 * h + 1, odd, even, streamed)
+        return carry
+
+    lax.fori_loop(0, kept // 2, functools.partial(two, False), 0)
+    lax.fori_loop(kept // 2, partitions // 2, functools.partial(two, True), 0)
     levels = out_ref.shape[0]
     for o in range(LONB):
         lanes = slice(o * BLK, (o + 1) * BLK)
@@ -250,26 +255,58 @@
         next_ref[:, lanes] = jnp.where(me & 1 == 0, top, bottom)
 
 
-def remap(me, blocks, table, geometry, weights, parts, shards, levels):
+def remap(me, blocks, table, geometry, early, weights, parts, shards, levels):
     partitions, slots = blocks.shape
     total = (LONB, levels * LAT_DEV, BLK)
     edge = jax.ShapeDtypeStruct((levels, LONB * BLK), jnp.float32)
     return pl.pallas_call(
         functools.partial(remap_kernel, parts, len(geometry)),
-        in_specs=[SMEM] * 3 + [VMEM] * len(geometry) + [ANY] + [ANY] * len(shards),
+        in_specs=[SMEM] * 3 + [VMEM] * len(geometry) + [VMEM, ANY] + [ANY] * len(shards),
         out_specs=(VMEM, VMEM, VMEM),
         out_shape=(jax.ShapeDtypeStruct((levels, LAT_DEV, LONB * BLK), jnp.float32), edge, edge),
         scratch_shapes=[
             pltpu.VMEM((levels // 2, partitions * CELLS), jnp.int32),
             pltpu.VMEM((slots, levels, 3 * BLK), jnp.bfloat16),
             pltpu.VMEM((slots, levels, 3 * BLK), jnp.bfloat16),
-            pltpu.VMEM(weights.shape, jnp.bfloat16),
+            pltpu.VMEM((weights.shape[0] - early.shape[0],) + weights.shape[1:], jnp.bfloat16),
             pltpu.VMEM(total, jnp.float32),
             pltpu.SemaphoreType.DMA,
             pltpu.SemaphoreType.DMA((partitions,)),
         ],
-        compiler_params=pltpu.CompilerParams(vmem_limit_bytes=44 * 1024 * 1024),
-    )(me, blocks, table, *geometry, weights, *shards)
+        compiler_params=pltpu.CompilerParams(vmem_limit_bytes=38 * 1024 * 1024),
+    )(me, blocks, table, *geometry, early, weights, *shards)
+
+
+def preload_kernel(chunk, table_ref, weights_ref, after_ref, array_ref, out_ref, array_out, sem, array_sem):
+    count = out_ref.shape[0]
+    copy = pltpu.make_async_copy(array_ref, array_out, array_sem)
+    copy.start()
+
+    def fetch(c, carry):
+        for i in range(chunk):
+            e = c * chunk + i
+            pair = table_ref[e] & (PAIRS - 1)
+            pltpu.make_async_copy(weights_ref.at[pair], out_ref.at[e], sem).start()
+        return carry
+
+    lax.fori_loop(0, count // chunk, fetch, 0)
+    copy.wait()
+    pltpu.make_async_copy(weights_ref.at[pl.ds(0, count)], out_ref, sem).wait()
+
+
+def preload(count, table, weights, after, array):
+    kept, array = pl.pallas_call(
+        functools.partial(preload_kernel, 16),
+        in_specs=[SMEM, ANY, ANY, ANY],
+        out_specs=(VMEM, ANY),
+        out_shape=(
+            pltpu.VMEM((count,) + weights.shape[1:], weights.dtype),
+            jax.ShapeDtypeStruct(array.shape, array.dtype),
+        ),
+        scratch_shapes=[pltpu.SemaphoreType.DMA, pltpu.SemaphoreType.DMA],
+        compiler_params=pltpu.CompilerParams(vmem_limit_bytes=40 * 1024 * 1024),
+    )(table, weights, after, array)
+    return pltpu.with_memory_space_constraint(kept, pltpu.VMEM), array
 
 
 def swap(array, code):
@@ -319,6 +356,7 @@
     table = jnp.sum(jnp.where(place[:, None] == pair_ids[None, :], word[:, None], 0), axis=0)
 
     me = jnp.stack([own_index, first])
+    remap_weights = pltpu.with_memory_space_constraint(remap_weights, pltpu.HBM)
     if partitions == 16:
         far, z, y = swap(packed, 8), swap(packed, 4), swap(packed, 2)
         far, _ = tie(far, chosen)
@@ -326,6 +364,7 @@
         far_z, far_y = swap(far, 4), swap(far, 2)
         far_z, far_y, table, blocks, me = tie(far_z, far_y, table, blocks, me)
         far_diagonal = swap(far_z, 2)
+        early_weights, again = preload(pair_total // 4, table, remap_weights, far_z, far_z)
         held = [
             (0, packed),
             (2, y),
@@ -336,15 +375,16 @@
             (10, far_y),
             (14, far_diagonal),
         ]
-        held = held + [(code ^ 1, swap(array, 1)) for code, array in held]
+        held = held + [(code ^ 1, swap(again if code == 12 else array, 1)) for code, array in held]
         parts = [(code, 0, array.shape[1]) for code, array in held]
         shards = [pltpu.with_memory_space_constraint(array, pltpu.VMEM) if code in EARLY else array for code, array in held]
     else:
+        early_weights, packed = preload(pair_total // 4, table, remap_weights, packed, packed)
         whole = lax.all_gather(packed, "src", axis=1, tiled=True)
         parts, shards = [(None, 0, whole.shape[1])], [whole]
 
     remapped, near, beyond = remap(
-        me, blocks, table, geometry, remap_weights, parts, shards, levels
+        me, blocks, table, geometry, early_weights, remap_weights, parts, shards, levels
     )
     steps = [(i, i + 1) for i in range(1, partitions - 1, 2)]
     beyond = lax.ppermute(beyond, "src", steps + [(j, i) for i, j in steps])

time: 64.3 us -> 62 us (0.964)
  waiting for transfers between devices: 14.8 us -> 11.3 us
  Pallas kernels: 15.7 us -> 17.8 us
  local copies, waits for them, and re-layouts: 1.24 us -> 0.29 us
    ppermute x16, waiting for transfers between devices: 9.59 us -> 6.02 us  [swap(): lax.ppermute(array, 'src', [(i, i ^ code) for i in range(lax.axis_size('s...]
    pallas_call x0 -> x1, Pallas kernels: none -> 3.48 us  [preload(): pl.pallas_call(functools.partial(preload_kernel, 16), in_specs=[SMEM, ANY...]
    pallas_call x1, Pallas kernels: 11 us -> 9.68 us  [remap(): pl.pallas_call(functools.partial(remap_kernel, parts, len(geometry)), in_...]
    unnamed x2, local copies, waits for them, and re-layouts: 0.95 us -> 0.01 us
  transfers between devices with their start and end apart: 19 -> 19, of which waited for: 8 -> 8; matrix products, arithmetic and copies ran while one was open for 8% -> 9% of each run, Pallas kernels for 4% -> 10%
where the time goes in v5:
time: 62 us; the launch traced here: 61 us
  starting transfers between devices  23.4 us (38%)
  Pallas kernels  17.8 us (29%)
  waiting for transfers between devices  11.3 us (18%)
  other arithmetic  7.37 us (12%)
  between operations  0.81 us (1%)
    ppermute x16, starting transfers between devices, swap(): lax.ppermute(array, 'src', [(i, i ^ code) for i in range(lax.axis_size('s...  14.6 us
    pallas_call x1, Pallas kernels, remap(): pl.pallas_call(functools.partial(remap_kernel, parts, len(geometry)), in_...  9.68 us
    ppermute x16, waiting for transfers between devices, swap(): lax.ppermute(array, 'src', [(i, i ^ code) for i in range(lax.axis_size('s...  6.02 us
    all_to_all x1, starting transfers between devices, local(): lax.all_to_all(chosen, 'src', split_axis=0, concat_axis=0, tiled=True)  5.97 us
    ppermute x1, waiting for transfers between devices, local(): beyond = lax.ppermute(beyond, 'src', steps + [(j, i) for i, j in steps])  4.2 us
    pallas_call x1, Pallas kernels, preload(): pl.pallas_call(functools.partial(preload_kernel, 16), in_specs=[SMEM, ANY...  3.48 us
    pallas_call x1, Pallas kernels, choose_geometry(): pl.pallas_call(geometry_kernel, in_specs=[SMEM, SMEM, VMEM, VMEM], out_sp...  2.5 us
    ppermute x1, starting transfers between devices, local(): beyond = lax.ppermute(beyond, 'src', steps + [(j, i) for i, j in steps])  2.35 us
  transfers between devices with their start and end apart: 19, of which 8 were waited for; matrix products, arithmetic and copies ran while one was open for 9% of the time, Pallas kernels for 10%

profile of v5, /device:TPU:18, one launch (start us, length us, event | category | flops | bytes accessed | tf_op | source)
XLA Modules:
  0.0 61.0 jit_solution(12559856559136996392)
XLA Ops:
  0.6 2.2 %shard_map.77.refs_7_ = s32[8,8192]{1,0:T(8,128)} custom-call(f32[16,8192]{1,0:T(8,128)} %field_ref.1), custom_call_target="tpu_custom_call" | custom-call | tf_op jit(solution)/shard_map/pallas_call | solution.py:69
  2.8 1.6 %collective-permute-start.5 = (s32[8,8192]{1,0:T(8,128)}, s32[8,8192]{1,0:T(8,128)S(1)}, u32[]{:S(2)}, u32[]{:S(2)}) collective-permute-start(s32[8,8192]{1,0:T(8,128)} %shard_map.77.refs_7_), channel_id=1, source_target_pairs={{0,4},{1,5},{2,6},{3,7},{4,0},{5,1},{6,2},{7,3},{8,12},{9,13},{10,... | collective-permute-start | bytes 786440 | tf_op jit(solution)/shard_map/ppermute | solution.py:313
  4.4 1.5 %collective-permute-start.4 = (s32[8,8192]{1,0:T(8,128)}, s32[8,8192]{1,0:T(8,128)S(1)}, u32[]{:S(2)}, u32[]{:S(2)}) collective-permute-start(s32[8,8192]{1,0:T(8,128)} %shard_map.77.refs_7_), channel_id=1, source_target_pairs={{0,2},{1,3},{2,0},{3,1},{4,6},{5,7},{6,4},{7,5},{8,10},{9,11},{10,... | collective-permute-start | bytes 786440 | tf_op jit(solution)/shard_map/ppermute | solution.py:313
  6.3 1.1 %compare_reduce_fusion = pred[16,64]{1,0:T(8,128)(4,1)S(1)} fusion(s32[16,256]{1,0:T(8,128)} %param.9, s32[64]{0:T(128)S(1)} %iota_add_fusion.3), kind=kLoop, calls=%fused_computation.3 | loop fusion | flops 523264 | bytes 17664 | tf_op jit(solution)/shard_map/reduce_or | solution.py:331
  7.6 0.9 %select_reduce_fusion.3.block_ref = s32[16,8]{1,0:T(8,128)} fusion(s32[16,64]{1,0:T(8,128)S(1)} %convert_reduce_fusion.1, pred[16,64]{1,0:T(8,128)(4,1)S(1)} %compare_reduce_fusion), kind=kLoop, calls=%fused_computation.17 | loop fusion | flops 32640 | bytes 5632 | tf_op jit(solution)/shard_map/reduce_sum | solution.py:127
  8.6 2.5 %shard_map.78 = s32[16,36,128]{2,1,0:T(8,128)} custom-call(s32[1]{0:T(128)} %bitcast.first_ref, s32[16,8]{1,0:T(8,128)} %select_reduce_fusion.3.block_ref, s32[6,8192]{1,0:T(8,128)} %neighbours_ref.1, f32[6,2,8192]{2,1,0:T(2,128)} %bitcast.11), custom_call_target="tpu_custom_call" | custom-call | bytes 10000000 | tf_op jit(solution)/shard_map/pallas_call | solution.py:107
  11.1 6.0 %all-to-all-start = ((s32[16,36,128]{2,1,0:T(8,128)}), s32[16,36,128]{2,1,0:T(8,128)S(1)}, u32[]{:S(2)}, u32[]{:S(2)}) async-start(s32[16,36,128]{2,1,0:T(8,128)} %shard_map.78), calls=%async_computation | async-start | bytes 655360 | tf_op jit(solution)/shard_map/all_to_all | solution.py:338
  17.0 0.7 %broadcast_multiply_fusion = s32[1,256]{1,0:T(1,128)S(1)} fusion(s32[1,256]{1,0:T(1,128)} %param.10), kind=kLoop, calls=%fused_computation.34 | loop fusion | flops 256 | bytes 2048 | tf_op jit(solution)/shard_map/mul | solution.py:352
  17.7 0.7 %iota_add_fusion.1 = (s32[1,256]{1,0:T(1,128)S(1)}, s32[1,256]{1,0:T(1,128)S(1)}) fusion(s32[16,256]{1,0:T(8,128)} %param.9, s32[]{:T(128)S(6)} %select_n.51), kind=kLoop, calls=%fused_computation.31 | loop fusion | flops 4352 | bytes 3076 | tf_op jit(solution)/shard_map/add | solution.py:354
  19.5 1.5 %collective-permute-start.2 = (s32[8,8192]{1,0:T(8,128)S(1)}, s32[8,8192]{1,0:T(8,128)S(1)}, u32[]{:S(2)}, u32[]{:S(2)}) collective-permute-start(s32[8,8192]{1,0:T(8,128)S(1)} %collective-permute-done.refs_11_), channel_id=1, source_target_pairs={{0,2},{1,3},{2,0},{3,1},{4,6},{5,7},{6,4},{7,5},{8,10},{9,11},{10,... | collective-permute-start | bytes 786440 | tf_op jit(solution)/shard_map/ppermute | solution.py:313
  21.0 4.8 %collective-permute-start.1 = (s32[8,8192]{1,0:T(8,128)S(1)}, s32[8,8192]{1,0:T(8,128)S(1)}, u32[]{:S(2)}, u32[]{:S(2)}) collective-permute-start(s32[8,8192]{1,0:T(8,128)S(1)} %collective-permute-done.refs_11_), channel_id=1, source_target_pairs={{0,4},{1,5},{2,6},{3,7},{4,0},{5,1},{6,2},{7,3},{8,12},{9,13},{10,... | collective-permute-start | bytes 786440 | tf_op jit(solution)/shard_map/ppermute | solution.py:313
  26.9 2.9 %collective-permute-done.2.refs_13_ = s32[8,8192]{1,0:T(8,128)S(1)} collective-permute-done((s32[8,8192]{1,0:T(8,128)S(1)}, s32[8,8192]{1,0:T(8,128)S(1)}, u32[]{:S(2)}, u32[]{:S(2)}) %collective-permute-start.2) | collective-permute-done | bytes 262176 | tf_op jit(solution)/shard_map/ppermute | solution.py:313
  29.9 0.8 %collective-permute-done.1.after_ref.array_ref.refs_12_ = s32[8,8192]{1,0:T(8,128)S(1)} collective-permute-done((s32[8,8192]{1,0:T(8,128)S(1)}, s32[8,8192]{1,0:T(8,128)S(1)}, u32[]{:S(2)}, u32[]{:S(2)}) %collective-permute-start.1) | collective-permute-done | bytes 262176 | tf_op jit(solution)/shard_map/ppermute | solution.py:313
  30.7 1.9 %collective-permute-start.6 = (s32[8,8192]{1,0:T(8,128)S(1)}, s32[8,8192]{1,0:T(8,128)S(1)}, u32[]{:S(2)}, u32[]{:S(2)}) collective-permute-start(s32[8,8192]{1,0:T(8,128)S(1)} %collective-permute-done.4.refs_8_), channel_id=1, source_target_pairs={{0,4},{1,5},{2,6},{3,7},{4,0},{5,1},{6,2},{7,3},{8,12},{9,13},{10,... | collective-permute-start | bytes 786440 | tf_op jit(solution)/shard_map/ppermute | solution.py:313
  32.6 1.6 %collective-permute-start.7 = (s32[8,8192]{1,0:T(8,128)S(1)}, s32[8,8192]{1,0:T(8,128)S(1)}, u32[]{:S(2)}, u32[]{:S(2)}) collective-permute-start(s32[8,8192]{1,0:T(8,128)S(1)} %collective-permute-done.1.after_ref.array_ref.refs_12_), channel_id=1, source_target_pairs={{0,2},{1,3},{2,0},{3,1},{4,6},{5,7},{6,4},{7,5},{8,10},{9,11},{10,... | collective-permute-start | bytes 786440 | tf_op jit(solution)/shard_map/ppermute | solution.py:313
  34.2 0.5 collective-permute-start.3
  34.7 3.5 %shard_map.79 = (bf16[64,384,128]{2,1,0:T(8,128)(2,1)S(1)}, s32[8,8192]{1,0:T(8,128)S(1)}) custom-call(s32[256]{0:T(256)S(1)} %select_reduce_fusion.1.table_ref.refs_2_, bf16[256,384,128]{2,1,0:T(8,128)(2,1)} %refs_6_.1, s32[8,8192]{1,0:T(8,128)S(1)} %collective-permute-done.1.after_ref.array_ref.refs_12_, ...), custom_call_target="tpu_custom_call" | custom-call | tf_op jit(solution)/shard_map/pallas_call | solution.py:298
  38.3 0.8 %collective-permute-done.6.refs_10_ = s32[8,8192]{1,0:T(8,128)S(1)} collective-permute-done((s32[8,8192]{1,0:T(8,128)S(1)}, s32[8,8192]{1,0:T(8,128)S(1)}, u32[]{:S(2)}, u32[]{:S(2)}) %collective-permute-start.6) | collective-permute-done | bytes 262176 | tf_op jit(solution)/shard_map/ppermute | solution.py:313
  39.6 1.0 %collective-permute-done.7.refs_14_ = s32[8,8192]{1,0:T(8,128)S(1)} collective-permute-done((s32[8,8192]{1,0:T(8,128)S(1)}, s32[8,8192]{1,0:T(8,128)S(1)}, u32[]{:S(2)}, u32[]{:S(2)}) %collective-permute-start.7) | collective-permute-done | bytes 262176 | tf_op jit(solution)/shard_map/ppermute | solution.py:313
  41.0 1.0 %collective-permute-done.3.refs_4_ = s32[16,36,128]{2,1,0:T(8,128)S(1)} collective-permute-done((s32[16,36,128]{2,1,0:T(8,128)S(1)}, s32[16,36,128]{2,1,0:T(8,128)S(1)}, u32[]{:S(2)}, u32[]{:S(2)}) %collective-permute-start.3) | collective-permute-done | bytes 294944 | tf_op jit(solution)/shard_map/ppermute | solution.py:341
  42.1 9.7 %shard_map.80 = (f32[16,8,1024]{2,1,0:T(8,128)}, f32[16,1024]{1,0:T(8,128)}, f32[16,1024]{1,0:T(8,128)S(1)}) custom-call(s32[2]{0:T(128)S(1)} %pad_add_fusion.refs_0_, s32[16,8]{1,0:T(8,128)S(1)} %select_reduce_fusion.2.refs_1_, s32[256]{0:T(256)S(1)} %select_reduce_fusion.1.table_ref.refs_2_, s32[16,36,128]{2,1,0:T(8,128)S(1)} %all-to-all-done.refs_3_, ...), custom_call_target="tpu_custom_call" | custom-call | tf_op jit(solution)/shard_map/pallas_call | solution.py:262
  52.0 2.3 %collective-permute-start.17 = (f32[16,1024]{1,0:T(8,128)S(1)}, f32[16,1024]{1,0:T(8,128)S(1)}, u32[]{:S(2)}, u32[]{:S(2)}) collective-permute-start(f32[16,1024]{1,0:T(8,128)S(1)} %get-tuple-element.25), channel_id=1, source_target_pairs={{1,2},{3,4},{5,6},{7,8},{9,10},{11,12},{13,14},{2,1},{4,3},{6,5},{... | collective-permute-start | bytes 196616 | tf_op jit(solution)/shard_map/ppermute | solution.py:390
  54.4 4.2 %collective-permute-done.17 = f32[16,1024]{1,0:T(8,128)S(1)} collective-permute-done((f32[16,1024]{1,0:T(8,128)S(1)}, f32[16,1024]{1,0:T(8,128)S(1)}, u32[]{:S(2)}, u32[]{:S(2)}) %collective-permute-start.17) | collective-permute-done | bytes 65568 | tf_op jit(solution)/shard_map/ppermute | solution.py:390
  58.8 2.2 %fusion.2 = f32[16,8,1024]{2,1,0:T(8,128)} fusion(f32[16,8,1024]{2,1,0:T(8,128)} %get-tuple-element.12, f32[16,1,1024]{2,1,0:T(1,128)S(1)} %copy.11, f32[16,1,1024]{2,1,0:T(1,128)S(1)} %copy.10), kind=kLoop, calls=%fused_computation.6 | loop fusion | flops 524288 | bytes 1179648 | tf_op jit(solution)/shard_map/mul | solution.py:396
  (42 shorter events, 4.2 us)
Async XLA Ops:
  2.8 39.3 %copy-start = (s32[8,8192]{1,0:T(8,128)S(1)}, s32[8,8192]{1,0:T(8,128)}, u32[]{:S(2)}) copy-start(s32[8,8192]{1,0:T(8,128)} %shard_map.77.refs_7_) | copy-start | bytes 786436
  2.8 29.8 %collective-permute-start.8 = (s32[8,8192]{1,0:T(8,128)}, s32[8,8192]{1,0:T(8,128)S(1)}, u32[]{:S(2)}, u32[]{:S(2)}) collective-permute-start(s32[8,8192]{1,0:T(8,128)} %shard_map.77.refs_7_), channel_id=1, source_target_pairs={{0,1},{1,0},{2,3},{3,2},{4,5},{5,4},{6,7},{7,6},{8,9},{9,8},{10,11... | collective-permute-start | bytes 786440 | tf_op jit(solution)/shard_map/ppermute | solution.py:313
  2.8 23.5 %collective-permute-start.5 = (s32[8,8192]{1,0:T(8,128)}, s32[8,8192]{1,0:T(8,128)S(1)}, u32[]{:S(2)}, u32[]{:S(2)}) collective-permute-start(s32[8,8192]{1,0:T(8,128)} %shard_map.77.refs_7_), channel_id=1, source_target_pairs={{0,4},{1,5},{2,6},{3,7},{4,0},{5,1},{6,2},{7,3},{8,12},{9,13},{10,... | collective-permute-start | bytes 786440 | tf_op jit(solution)/shard_map/ppermute | solution.py:313
  4.4 22.1 %collective-permute-start.4 = (s32[8,8192]{1,0:T(8,128)}, s32[8,8192]{1,0:T(8,128)S(1)}, u32[]{:S(2)}, u32[]{:S(2)}) collective-permute-start(s32[8,8192]{1,0:T(8,128)} %shard_map.77.refs_7_), channel_id=1, source_target_pairs={{0,2},{1,3},{2,0},{3,1},{4,6},{5,7},{6,4},{7,5},{8,10},{9,11},{10,... | collective-permute-start | bytes 786440 | tf_op jit(solution)/shard_map/ppermute | solution.py:313
  5.9 13.6 %collective-permute-start = (s32[8,8192]{1,0:T(8,128)}, s32[8,8192]{1,0:T(8,128)S(1)}, u32[]{:S(2)}, u32[]{:S(2)}) collective-permute-start(s32[8,8192]{1,0:T(8,128)} %shard_map.77.refs_7_), channel_id=1, source_target_pairs={{0,8},{1,9},{2,10},{3,11},{4,12},{5,13},{6,14},{7,15},{8,0},{9,1},... | collective-permute-start | bytes 786440 | tf_op jit(solution)/shard_map/ppermute | solution.py:313
  11.1 23.1 %all-to-all-start = ((s32[16,36,128]{2,1,0:T(8,128)}), s32[16,36,128]{2,1,0:T(8,128)S(1)}, u32[]{:S(2)}, u32[]{:S(2)}) async-start(s32[16,36,128]{2,1,0:T(8,128)} %shard_map.78), calls=%async_computation | async-start | bytes 655360 | tf_op jit(solution)/shard_map/all_to_all | solution.py:338
  19.5 10.4 %collective-permute-start.2 = (s32[8,8192]{1,0:T(8,128)S(1)}, s32[8,8192]{1,0:T(8,128)S(1)}, u32[]{:S(2)}, u32[]{:S(2)}) collective-permute-start(s32[8,8192]{1,0:T(8,128)S(1)} %collective-permute-done.refs_11_), channel_id=1, source_target_pairs={{0,2},{1,3},{2,0},{3,1},{4,6},{5,7},{6,4},{7,5},{8,10},{9,11},{10,... | collective-permute-start | bytes 786440 | tf_op jit(solution)/shard_map/ppermute | solution.py:313
  21.0 9.6 %collective-permute-start.1 = (s32[8,8192]{1,0:T(8,128)S(1)}, s32[8,8192]{1,0:T(8,128)S(1)}, u32[]{:S(2)}, u32[]{:S(2)}) collective-permute-start(s32[8,8192]{1,0:T(8,128)S(1)} %collective-permute-done.refs_11_), channel_id=1, source_target_pairs={{0,4},{1,5},{2,6},{3,7},{4,0},{5,1},{6,2},{7,3},{8,12},{9,13},{10,... | collective-permute-start | bytes 786440 | tf_op jit(solution)/shard_map/ppermute | solution.py:313
  26.3 7.9 %collective-permute-start.10 = (s32[8,8192]{1,0:T(8,128)S(1)}, s32[8,8192]{1,0:T(8,128)S(1)}, u32[]{:S(2)}, u32[]{:S(2)}) collective-permute-start(s32[8,8192]{1,0:T(8,128)S(1)} %collective-permute-done.5.refs_9_), channel_id=1, source_target_pairs={{0,1},{1,0},{2,3},{3,2},{4,5},{5,4},{6,7},{7,6},{8,9},{9,8},{10,11... | collective-permute-start | bytes 786440 | tf_op jit(solution)/shard_map/ppermute | solution.py:313
  26.4 11.8 %collective-permute-start.9 = (s32[8,8192]{1,0:T(8,128)S(1)}, s32[8,8192]{1,0:T(8,128)S(1)}, u32[]{:S(2)}, u32[]{:S(2)}) collective-permute-start(s32[8,8192]{1,0:T(8,128)S(1)} %collective-permute-done.4.refs_8_), channel_id=1, source_target_pairs={{0,1},{1,0},{2,3},{3,2},{4,5},{5,4},{6,7},{7,6},{8,9},{9,8},{10,11... | collective-permute-start | bytes 786440 | tf_op jit(solution)/shard_map/ppermute | solution.py:313
  29.9 9.3 %collective-permute-start.12 = (s32[8,8192]{1,0:T(8,128)S(1)}, s32[8,8192]{1,0:T(8,128)S(1)}, u32[]{:S(2)}, u32[]{:S(2)}) collective-permute-start(s32[8,8192]{1,0:T(8,128)S(1)} %collective-permute-done.refs_11_), channel_id=1, source_target_pairs={{0,1},{1,0},{2,3},{3,2},{4,5},{5,4},{6,7},{7,6},{8,9},{9,8},{10,11... | collective-permute-start | bytes 786440 | tf_op jit(solution)/shard_map/ppermute | solution.py:313
  30.7 8.5 %collective-permute-start.6 = (s32[8,8192]{1,0:T(8,128)S(1)}, s32[8,8192]{1,0:T(8,128)S(1)}, u32[]{:S(2)}, u32[]{:S(2)}) collective-permute-start(s32[8,8192]{1,0:T(8,128)S(1)} %collective-permute-done.4.refs_8_), channel_id=1, source_target_pairs={{0,4},{1,5},{2,6},{3,7},{4,0},{5,1},{6,2},{7,3},{8,12},{9,13},{10,... | collective-permute-start | bytes 786440 | tf_op jit(solution)/shard_map/ppermute | solution.py:313
  32.6 8.0 %collective-permute-start.7 = (s32[8,8192]{1,0:T(8,128)S(1)}, s32[8,8192]{1,0:T(8,128)S(1)}, u32[]{:S(2)}, u32[]{:S(2)}) collective-permute-start(s32[8,8192]{1,0:T(8,128)S(1)} %collective-permute-done.1.after_ref.array_ref.refs_12_), channel_id=1, source_target_pairs={{0,2},{1,3},{2,0},{3,1},{4,6},{5,7},{6,4},{7,5},{8,10},{9,11},{10,... | collective-permute-start | bytes 786440 | tf_op jit(solution)/shard_map/ppermute | solution.py:313
  34.2 7.9 %collective-permute-start.3 = (s32[16,36,128]{2,1,0:T(8,128)S(1)}, s32[16,36,128]{2,1,0:T(8,128)S(1)}, u32[]{:S(2)}, u32[]{:S(2)}) collective-permute-start(s32[16,36,128]{2,1,0:T(8,128)S(1)} %all-to-all-done.refs_3_), channel_id=1, source_target_pairs={{0,16},{16,0},{1,17},{17,1},{2,18},{18,2},{3,19},{19,3},{4,20},{20... | collective-permute-start | bytes 884744 | tf_op jit(solution)/shard_map/ppermute | solution.py:341
  38.2 2.5 %collective-permute-start.14 = (s32[8,8192]{1,0:T(8,128)S(1)}, s32[8,8192]{1,0:T(8,128)S(1)}, u32[]{:S(2)}, u32[]{:S(2)}) collective-permute-start(s32[8,8192]{1,0:T(8,128)S(1)} %collective-permute-done.2.refs_13_), channel_id=1, source_target_pairs={{0,1},{1,0},{2,3},{3,2},{4,5},{5,4},{6,7},{7,6},{8,9},{9,8},{10,11... | collective-permute-start | bytes 786440 | tf_op jit(solution)/shard_map/ppermute | solution.py:313
  39.1 1.5 %collective-permute-start.11 = (s32[8,8192]{1,0:T(8,128)S(1)}, s32[8,8192]{1,0:T(8,128)S(1)}, u32[]{:S(2)}, u32[]{:S(2)}) collective-permute-start(s32[8,8192]{1,0:T(8,128)S(1)} %collective-permute-done.6.refs_10_), channel_id=1, source_target_pairs={{0,1},{1,0},{2,3},{3,2},{4,5},{5,4},{6,7},{7,6},{8,9},{9,8},{10,11... | collective-permute-start | bytes 786440 | tf_op jit(solution)/shard_map/ppermute | solution.py:313
  39.1 1.9 %collective-permute-start.13 = (s32[8,8192]{1,0:T(8,128)S(1)}, s32[8,8192]{1,0:T(8,128)S(1)}, u32[]{:S(2)}, u32[]{:S(2)}) collective-permute-start(s32[8,8192]{1,0:T(8,128)S(1)} %get-tuple-element.22), channel_id=1, source_target_pairs={{0,1},{1,0},{2,3},{3,2},{4,5},{5,4},{6,7},{7,6},{8,9},{9,8},{10,11... | collective-permute-start | bytes 786440 | tf_op jit(solution)/shard_map/ppermute | solution.py:313
  40.6 1.5 %collective-permute-start.15 = (s32[8,8192]{1,0:T(8,128)S(1)}, s32[8,8192]{1,0:T(8,128)S(1)}, u32[]{:S(2)}, u32[]{:S(2)}) collective-permute-start(s32[8,8192]{1,0:T(8,128)S(1)} %collective-permute-done.7.refs_14_), channel_id=1, source_target_pairs={{0,1},{1,0},{2,3},{3,2},{4,5},{5,4},{6,7},{7,6},{8,9},{9,8},{10,11... | collective-permute-start | bytes 786440 | tf_op jit(solution)/shard_map/ppermute | solution.py:313
  51.8 2.6 %collective-permute-start.16 = (f32[16,1024]{1,0:T(8,128)}, f32[16,1024]{1,0:T(8,128)S(1)}, u32[]{:S(2)}, u32[]{:S(2)}) collective-permute-start(f32[16,1024]{1,0:T(8,128)} %get-tuple-element.24), channel_id=1, source_target_pairs={{0,1},{1,0},{2,3},{3,2},{4,5},{5,4},{6,7},{7,6},{8,9},{9,8},{10,11... | collective-permute-start | bytes 196616 | tf_op jit(solution)/shard_map/ppermute | solution.py:313
  52.0 6.6 %collective-permute-start.17 = (f32[16,1024]{1,0:T(8,128)S(1)}, f32[16,1024]{1,0:T(8,128)S(1)}, u32[]{:S(2)}, u32[]{:S(2)}) collective-permute-start(f32[16,1024]{1,0:T(8,128)S(1)} %get-tuple-element.25), channel_id=1, source_target_pairs={{1,2},{3,4},{5,6},{7,8},{9,10},{11,12},{13,14},{2,1},{4,3},{6,5},{... | collective-permute-start | bytes 196616 | tf_op jit(solution)/shard_map/ppermute | solution.py:390
